TPU v7x, 32 devices: a whole 2x2x4 slice. The times are simulated.
32 devices in a mesh: seq: 4 (over y, x), fsdp: 8 (over z, core).
Axes of the slice: x: 2, y: 2, z: 4, core: 2. Of those that a mesh axis runs over, the one named last changes fastest.
Arguments:
- tokens: bfloat16 [8, 1024, 2048], P('fsdp', 'seq'), may hold values from -6 to 6
- qkv_weight: bfloat16 [2048, 6144], P('fsdp'), may hold values from -0.125 to 0.125
- out_weight: bfloat16 [2048, 2048], P('fsdp'), may hold values from -1.5 to 1.5
- up_weight: bfloat16 [2048, 8192], P('fsdp'), may hold values from -0.125 to 0.125
- down_weight: bfloat16 [8192, 2048], P('fsdp'), may hold values from -0.0625 to 0.0625
- norm_gain: bfloat16 [2048], P('fsdp'), may hold values from 0.5 to 1.5
- norm_bias: bfloat16 [2048], P('fsdp'), may hold values from -3 to 3
- qkv_bias: bfloat16 [6144], P('fsdp'), may hold values from -4 to 4
- out_bias: bfloat16 [2048], P('fsdp'), may hold values from -4 to 4
- up_bias: bfloat16 [8192], P('fsdp'), may hold values from -6 to 6
- down_bias: bfloat16 [2048], P('fsdp'), may hold values from -4 to 4
- cotangent: bfloat16 [8, 1024, 2048], P('fsdp', 'seq'), may hold values from -6 to 6
Outputs:
- block_out: bfloat16 [8, 1024, 2048], P('fsdp', 'seq')
- tokens_grad: bfloat16 [8, 1024, 2048], P('fsdp', 'seq')
- qkv_wgrad: float32 [2048, 6144], P('fsdp')
- out_wgrad: float32 [2048, 2048], P('fsdp')
- up_wgrad: float32 [2048, 8192], P('fsdp')
- down_wgrad: float32 [8192, 2048], P('fsdp')
- gain_grad: float32 [2048], P('fsdp')
- norm_bgrad: float32 [2048], P('fsdp')
- qkv_bgrad: float32 [4096], P('fsdp')
- value_bgrad: float32 [2048], P('fsdp')
- out_bgrad: float32 [2048], P('fsdp')
- up_bgrad: float32 [8192], P('fsdp')
- down_bgrad: float32 [2048], P('fsdp')
All inputs are finite; a program needn't handle non-finite values.
Results may differ from a plain program's by a relative error of at most 0.011.
Values may be sent and summed in bfloat16 or wider, within the bound.
No kernel may reach another device: no remote copies, remote signals or barrier semaphores. Data moves between devices by JAX's collectives and lax.ppermute only.
A program may use at most 576 MiB of HBM per device.

v0:
```python
import math

import jax
import jax.numpy as jnp
from jax import lax
from jax.sharding import PartitionSpec as P

D = 2048
HD = 64
ROT = 32


epsilon = 1e-05
rope_base = 10000.0
masked_score = -1000000000.0


def rotary_tables(positions):
    halves = ROT // 2
    frequency = rope_base ** (-(2.0 * jnp.arange(halves).astype(jnp.float32)) / ROT)
    angles = positions.astype(jnp.float32)[:, None] * frequency[None, :]
    return (jnp.cos(angles), jnp.sin(angles))


def rotate(values, cos_table, sin_table):
    halves = ROT // 2
    leading = values[..., :halves]
    trailing = values[..., halves:ROT]
    cos_wide = cos_table[:, None, :]
    sin_wide = sin_table[:, None, :]
    return jnp.concatenate(
        [
            leading * cos_wide - trailing * sin_wide,
            trailing * cos_wide + leading * sin_wide,
            values[..., ROT:],
        ],
        axis=-1,
    )


def rotate_back(values, cos_table, sin_table):
    halves = ROT // 2
    leading = values[..., :halves]
    trailing = values[..., halves:ROT]
    cos_wide = cos_table[:, None, :]
    sin_wide = sin_table[:, None, :]
    return jnp.concatenate(
        [
            leading * cos_wide + trailing * sin_wide,
            trailing * cos_wide - leading * sin_wide,
            values[..., ROT:],
        ],
        axis=-1,
    )


def normalize(token_rows, gain_vector, bias_vector):
    average = jnp.mean(token_rows, axis=-1, keepdims=True)
    centred = token_rows - average
    variance = jnp.mean(centred * centred, axis=-1, keepdims=True)
    return centred * lax.rsqrt(variance + epsilon) * gain_vector + bias_vector


def gelu_tanh(hidden):
    return jax.nn.gelu(hidden, approximate=True)


def attention_forward(queries, key_rows, values):
    length, columns = queries.shape
    head_count = columns // HD
    block_rows = math.gcd(length, 512)
    block_count = length // block_rows
    score_scale = HD ** (-0.5)
    key_view = key_rows.reshape(length, head_count, HD)
    value_view = values.reshape(length, head_count, HD)
    key_place = jnp.arange(length)

    def one_block(operands):
        query_block, first_row = operands
        scores = (
            jnp.einsum("bhd,lhd->hbl", query_block, key_view, preferred_element_type=jnp.float32)
            * score_scale
        )
        query_place = first_row + jnp.arange(block_rows)
        visible = key_place[None, None, :] <= query_place[None, :, None]
        scores = jnp.where(visible, scores, masked_score)
        highest = jnp.max(scores, axis=-1, keepdims=True)
        exponent = jnp.exp(scores - highest)
        totals = jnp.sum(exponent, axis=-1, keepdims=True)
        weights = (exponent / totals).astype(jnp.bfloat16)
        output = jnp.einsum("hbl,lhd->bhd", weights, value_view, preferred_element_type=jnp.float32)
        return (output.astype(jnp.bfloat16), (highest + jnp.log(totals))[..., 0])

    stacked = queries.reshape(block_count, block_rows, head_count, HD)
    firsts = jnp.arange(block_count) * block_rows
    outputs, logsums = lax.map(one_block, (stacked, firsts))
    return (outputs.reshape(length, columns), logsums)


def attention_backward(queries, key_rows, values, out_grad, logsums):
    length, columns = queries.shape
    head_count = columns // HD
    block_rows = math.gcd(length, 512)
    block_count = length // block_rows
    score_scale = HD ** (-0.5)
    key_view = key_rows.reshape(length, head_count, HD)
    value_view = values.reshape(length, head_count, HD)
    key_place = jnp.arange(length)

    def one_block(carried, operands):
        key_grad, value_grad = carried
        query_block, grad_block, logsum, first_row = operands
        scores = (
            jnp.einsum("bhd,lhd->hbl", query_block, key_view, preferred_element_type=jnp.float32)
            * score_scale
        )
        query_place = first_row + jnp.arange(block_rows)
        visible = key_place[None, None, :] <= query_place[None, :, None]
        scores = jnp.where(visible, scores, masked_score)
        attn_probs = jnp.exp(scores - logsum[..., None])
        value_grad = value_grad + jnp.einsum(
            "hbl,bhd->lhd",
            attn_probs.astype(jnp.bfloat16),
            grad_block,
            preferred_element_type=jnp.float32,
        )
        prob_grad = jnp.einsum(
            "bhd,lhd->hbl", grad_block, value_view, preferred_element_type=jnp.float32
        )
        row_inner = jnp.sum(attn_probs * prob_grad, axis=-1, keepdims=True)
        score_grad = (attn_probs * (prob_grad - row_inner)).astype(jnp.bfloat16)
        query_grad = (
            jnp.einsum("hbl,lhd->bhd", score_grad, key_view, preferred_element_type=jnp.float32)
            * score_scale
        )
        key_grad = (
            key_grad
            + jnp.einsum(
                "hbl,bhd->lhd", score_grad, query_block, preferred_element_type=jnp.float32
            )
            * score_scale
        )
        return ((key_grad, value_grad), query_grad)

    stacked = queries.reshape(block_count, block_rows, head_count, HD)
    grad_stacked = out_grad.reshape(block_count, block_rows, head_count, HD)
    firsts = jnp.arange(block_count) * block_rows
    zeros_init = jnp.zeros((length, head_count, HD), jnp.float32)
    (key_grad, value_grad), query_grad = lax.scan(
        one_block, (zeros_init, zeros_init), (stacked, grad_stacked, logsums, firsts)
    )
    return (query_grad.reshape(length, head_count, HD), key_grad, value_grad)


def on_device(
    tokens,
    qkv_weight,
    out_weight,
    up_weight,
    down_weight,
    norm_gain,
    norm_bias,
    qkv_bias,
    out_bias,
    up_bias,
    down_bias,
    cotangent,
):
    gathered = (
        lax.all_gather(qkv_weight, "fsdp", axis=0, tiled=True),
        lax.all_gather(out_weight, "fsdp", axis=0, tiled=True),
        lax.all_gather(up_weight, "fsdp", axis=0, tiled=True),
        lax.all_gather(down_weight, "fsdp", axis=0, tiled=True),
        lax.all_gather(norm_gain, "fsdp", axis=0, tiled=True),
        lax.all_gather(norm_bias, "fsdp", axis=0, tiled=True),
        lax.all_gather(qkv_bias, "fsdp", axis=0, tiled=True),
        lax.all_gather(out_bias, "fsdp", axis=0, tiled=True),
        lax.all_gather(up_bias, "fsdp", axis=0, tiled=True),
        lax.all_gather(down_bias, "fsdp", axis=0, tiled=True),
    )
    (
        qkv_full,
        out_full,
        up_full,
        down_full,
        gain_full,
        nbias_full,
        qkvb_full,
        outb_full,
        upb_full,
        downb_full,
    ) = gathered
    token_rows = tokens[0].astype(jnp.float32)
    tok_count = token_rows.shape[0]
    head_all = D // HD
    normed_wide, norm_pull = jax.vjp(
        normalize, token_rows, gain_full.astype(jnp.float32), nbias_full.astype(jnp.float32)
    )
    normed = normed_wide.astype(jnp.bfloat16)
    mixed_cols = jnp.dot(normed, qkv_full, preferred_element_type=jnp.float32) + qkvb_full.astype(
        jnp.float32
    )
    positions = lax.axis_index("seq") * tok_count + jnp.arange(tok_count)
    cos_table, sin_table = rotary_tables(positions)
    queries = (
        rotate(mixed_cols[:, :D].reshape(tok_count, head_all, HD), cos_table, sin_table)
        .reshape(tok_count, D)
        .astype(jnp.bfloat16)
    )
    key_rows = (
        rotate(mixed_cols[:, D : 2 * D].reshape(tok_count, head_all, HD), cos_table, sin_table)
        .reshape(tok_count, D)
        .astype(jnp.bfloat16)
    )
    values = mixed_cols[:, 2 * D :].astype(jnp.bfloat16)
    query_heads, key_heads, value_heads = (
        lax.all_to_all(queries, "seq", split_axis=1, concat_axis=0, tiled=True),
        lax.all_to_all(key_rows, "seq", split_axis=1, concat_axis=0, tiled=True),
        lax.all_to_all(values, "seq", split_axis=1, concat_axis=0, tiled=True),
    )
    attended_heads, logsums = attention_forward(query_heads, key_heads, value_heads)
    attended = lax.all_to_all(attended_heads, "seq", split_axis=0, concat_axis=1, tiled=True)
    hidden = jnp.dot(normed, up_full, preferred_element_type=jnp.float32) + upb_full.astype(
        jnp.float32
    )
    activated_wide, gelu_pull = jax.vjp(gelu_tanh, hidden)
    activated = activated_wide.astype(jnp.bfloat16)
    attn_branch = jnp.dot(
        attended, out_full, preferred_element_type=jnp.float32
    ) + outb_full.astype(jnp.float32)
    mlp_branch = jnp.dot(
        activated, down_full, preferred_element_type=jnp.float32
    ) + downb_full.astype(jnp.float32)
    block_out = (token_rows + attn_branch + mlp_branch).astype(jnp.bfloat16)[None]
    qkv_back, out_back, up_back, down_back = (
        lax.all_gather(qkv_weight, "fsdp", axis=0, tiled=True),
        lax.all_gather(out_weight, "fsdp", axis=0, tiled=True),
        lax.all_gather(up_weight, "fsdp", axis=0, tiled=True),
        lax.all_gather(down_weight, "fsdp", axis=0, tiled=True),
    )
    upstream = cotangent[0]
    out_local = jnp.einsum("td,te->de", attended, upstream, preferred_element_type=jnp.float32)
    down_local = jnp.einsum("tf,te->fe", activated, upstream, preferred_element_type=jnp.float32)
    bias_local = jnp.sum(upstream.astype(jnp.float32), axis=0)
    attended_grad = jnp.einsum(
        "te,de->td", upstream, out_back, preferred_element_type=jnp.float32
    ).astype(jnp.bfloat16)
    activated_grad = jnp.einsum(
        "te,fe->tf", upstream, down_back, preferred_element_type=jnp.float32
    )
    hidden_grad = gelu_pull(activated_grad)[0].astype(jnp.bfloat16)
    up_local = jnp.einsum("td,tf->df", normed, hidden_grad, preferred_element_type=jnp.float32)
    upb_local = jnp.sum(hidden_grad.astype(jnp.float32), axis=0)
    grad_heads = lax.all_to_all(attended_grad, "seq", split_axis=1, concat_axis=0, tiled=True)
    query_grad, key_grad, value_grad = attention_backward(
        query_heads, key_heads, value_heads, grad_heads, logsums
    )
    seq_length = query_heads.shape[0]
    head_cols = query_heads.shape[1]
    cos_long, sin_long = rotary_tables(jnp.arange(seq_length))
    query_back = (
        rotate_back(query_grad, cos_long, sin_long)
        .reshape(seq_length, head_cols)
        .astype(jnp.bfloat16)
    )
    key_back = (
        rotate_back(key_grad, cos_long, sin_long)
        .reshape(seq_length, head_cols)
        .astype(jnp.bfloat16)
    )
    value_back = value_grad.reshape(seq_length, head_cols).astype(jnp.bfloat16)
    query_tok, key_tok, value_tok = (
        lax.all_to_all(query_back, "seq", split_axis=0, concat_axis=1, tiled=True),
        lax.all_to_all(key_back, "seq", split_axis=0, concat_axis=1, tiled=True),
        lax.all_to_all(value_back, "seq", split_axis=0, concat_axis=1, tiled=True),
    )
    mixed_grad = jnp.concatenate([query_tok, key_tok, value_tok], axis=1)
    qkv_local = jnp.einsum("td,tc->dc", normed, mixed_grad, preferred_element_type=jnp.float32)
    qkvb_local = jnp.sum(mixed_grad.astype(jnp.float32), axis=0)
    qk_bias_local = qkvb_local[: 2 * D]
    value_bias_local = qkvb_local[2 * D :]
    normed_grad = jnp.einsum(
        "tc,dc->td", mixed_grad, qkv_back, preferred_element_type=jnp.float32
    ) + jnp.einsum("tf,df->td", hidden_grad, up_back, preferred_element_type=jnp.float32)
    rows_grad, gain_local, nbias_local = norm_pull(normed_grad)
    tokens_grad = (upstream.astype(jnp.float32) + rows_grad).astype(jnp.bfloat16)[None]
    shards = (
        lax.psum_scatter(qkv_local, "fsdp", scatter_dimension=0, tiled=True),
        lax.psum_scatter(out_local, "fsdp", scatter_dimension=0, tiled=True),
        lax.psum_scatter(up_local, "fsdp", scatter_dimension=0, tiled=True),
        lax.psum_scatter(down_local, "fsdp", scatter_dimension=0, tiled=True),
        lax.psum_scatter(gain_local, "fsdp", scatter_dimension=0, tiled=True),
        lax.psum_scatter(nbias_local, "fsdp", scatter_dimension=0, tiled=True),
        lax.psum_scatter(qk_bias_local, "fsdp", scatter_dimension=0, tiled=True),
        lax.psum_scatter(value_bias_local, "fsdp", scatter_dimension=0, tiled=True),
        lax.psum_scatter(bias_local, "fsdp", scatter_dimension=0, tiled=True),
        lax.psum_scatter(upb_local, "fsdp", scatter_dimension=0, tiled=True),
    )
    summed = lax.psum(
        (
            shards[0],
            shards[1],
            shards[2],
            shards[3],
            shards[4],
            shards[5],
            shards[6],
            shards[7],
            shards[8],
            shards[9],
        ),
        "seq",
    )
    (
        qkv_wgrad,
        out_wgrad,
        up_wgrad,
        down_wgrad,
        gain_grad,
        norm_bgrad,
        qkv_bgrad,
        value_bgrad,
        out_bgrad,
        up_bgrad,
    ) = summed
    return (
        block_out,
        tokens_grad,
        qkv_wgrad,
        out_wgrad,
        up_wgrad,
        down_wgrad,
        gain_grad,
        norm_bgrad,
        qkv_bgrad,
        value_bgrad,
        out_bgrad,
        up_bgrad,
        out_bgrad,
    )


def solution(mesh):
    placed = (
        P("fsdp", "seq", None),
        P("fsdp", None),
        P("fsdp", None),
        P("fsdp", None),
        P("fsdp", None),
        P("fsdp"),
        P("fsdp"),
        P("fsdp"),
        P("fsdp"),
        P("fsdp"),
        P("fsdp"),
        P("fsdp", "seq", None),
    )
    return jax.shard_map(
        on_device,
        mesh=mesh,
        in_specs=placed,
        out_specs=(
            P("fsdp", "seq", None),
            P("fsdp", "seq", None),
            P("fsdp", None),
            P("fsdp", None),
            P("fsdp", None),
            P("fsdp", None),
            P("fsdp"),
            P("fsdp"),
            P("fsdp"),
            P("fsdp"),
            P("fsdp"),
            P("fsdp"),
            P("fsdp"),
        ),
        check_vma=False,
    )
```

profile of v0, /device:TPU:0, one launch (start us, length us, event | category | flops | bytes accessed | tf_op | source)
XLA Modules:
  0.0 3358.3 jit_solution(14858124402555615251)
XLA Ops:
  32.4 16.7 all-gather.2
  50.5 182.0 %all-gather.10.cloned.1.call-done = bf16[2048,6144]{1,0:T(8,128)(2,1)} async-done(((bf16[256,6144]{1,0:T(8,128)(2,1)}), bf16[2048,6144]{1,0:T(8,128)(2,1)}) %all-gather.10.cloned.1.call-update) | async-done | bytes 25165840 | tf_op jit(solution)/shard_map/all_gather | solution.py:170
  258.6 17.9 all_to_all.125
  313.7 35.2 %while.28 = (s32[]{:T(128)}, bf16[2,512,8,64]{1,3,2,0:T(8,128)(2,1)}, f32[2,8,512]{2,1,0:T(8,128)}, s32[2]{0:T(128)S(1)}, bf16[2,512,8,64]{1,3,2,0:T(8,128)(2,1)...) while((s32[]{:T(128)}, bf16[2,512,8,64]{1,3,2,0:T(8,128)(2,1)}, ...), condition=%wide.region_5.6_spmd.clone, body=%wide.region_2.5_spmd.clone.sunk | while | flops 1124856320 | bytes 64099488 | solution.py:96
  353.9 28.6 all_to_all.126
  416.8 141.9 %while.29 = (s32[]{:T(128)}, f32[1024,8,64]{0,2,1:T(8,128)}, f32[1024,8,64]{0,2,1:T(8,128)}, f32[2,512,8,64]{1,0,3,2:T(2,128)}, bf16[2,512,8,64]{1,3,2,0:T(8,128...) while((s32[]{:T(128)}, f32[1024,8,64]{0,2,1:T(8,128)}, ...), condition=%wide.region_8.9_spmd.clone, body=%wide.region_6.8_spmd.clone.sunk | while | flops 2725507584 | bytes 166942480 | solution.py:149
  452.8 19.7 dynamic_update_slice.22
  523.4 19.7 dynamic_update_slice.22
  604.2 17.1 all_to_all.127
  622.2 19.9 fusion.69
  642.8 22.2 all_gather.41
  665.0 18.1 convolution_add_fusion
  683.1 208.5 %all-gather.16.cloned.1.call-done = bf16[8192,2048]{1,0:T(8,128)(2,1)} async-done(((bf16[1024,2048]{1,0:T(8,128)(2,1)}), bf16[8192,2048]{1,0:T(8,128)(2,1)}) %all-gather.16.cloned.1.call-update) | async-done | bytes 33554448 | tf_op jit(solution)/shard_map/all_gather | solution.py:173
  891.6 21.6 convert_reduce_fusion
  913.2 26.2 fusion.72
  939.4 28.3 fusion.59
  985.2 18.9 fusion.77
  1010.4 49.8 %reduce-scatter.7.cloned.1.call-done = f32[256,2048]{1,0:T(8,128)} async-done(((f32[2048,2048]{1,0:T(8,128)}), f32[256,2048]{1,0:T(8,128)}) %reduce-scatter.7.cloned.1.call-update) | async-done | bytes 2097168 | tf_op jit(solution)/shard_map/reduce_scatter | solution.py:289
  1060.3 483.8 %reduce-scatter.5.cloned.1.call-done = f32[256,6144]{1,0:T(8,128)} async-done(((f32[2048,6144]{1,0:T(8,128)}), f32[256,6144]{1,0:T(8,128)}) %reduce-scatter.5.cloned.1.call-update) | async-done | bytes 6291472 | tf_op jit(solution)/shard_map/reduce_scatter | solution.py:288
  1544.0 641.0 %reduce-scatter.9.cloned.1.call-done = f32[256,8192]{1,0:T(8,128)} async-done(((f32[2048,8192]{1,0:T(8,128)}), f32[256,8192]{1,0:T(8,128)}) %reduce-scatter.9.cloned.1.call-update) | async-done | bytes 8388624 | tf_op jit(solution)/shard_map/reduce_scatter | solution.py:290
  2185.0 640.9 %reduce-scatter.11.cloned.1.call-done = f32[1024,2048]{1,0:T(8,128)} async-done(((f32[8192,2048]{1,0:T(8,128)}), f32[1024,2048]{1,0:T(8,128)}) %reduce-scatter.11.cloned.1.call-update) | async-done | bytes 8388624 | tf_op jit(solution)/shard_map/reduce_scatter | solution.py:291
  2855.1 19.9 fusion.49
  2883.2 16.8 all-reduce.7
  2900.0 432.6 %all-reduce.14.cloned.1.call-done = (f32[256,6144]{1,0:T(8,128)}, f32[256,2048]{1,0:T(8,128)}, f32[256,8192]{1,0:T(8,128)}, f32[1024,2048]{1,0:T(8,128)}) async-done(((f32[256,6144]{1,0:T(8,128)}, f32[256,2048]{1,0:T(8,128)}, f32[256,8192]{1,0:T(8,128)}, f32[1024,2048]{1,0:T(8,128)}), (f32[256,6144]{1,0:T(8,128)}, f32[256,2048]{1,0:T(8,128)}, f32[256,8192]{1,0:T(8,128)}, ...) | async-done | bytes 25165840 | tf_op jit(solution)/shard_map/psum | solution.py:299
  (258 shorter events, 390.9 us)
Async XLA Ops:
  7.2 225.3 %all-gather.10.cloned.1.call-start = ((), (), s32[]{:S(2)}) async-start(), calls=%async_computation.12 | async-start | bytes 28311552 | tf_op jit(solution)/shard_map/all_gather | solution.py:170
  7.9 383.8 %all-gather.12.cloned.1.call-start = ((), (), s32[]{:S(2)}) async-start(), calls=%async_computation.13 | async-start | bytes 9437184 | tf_op jit(solution)/shard_map/all_gather | solution.py:171
  8.7 40.4 %copy-start.3 = (bf16[1,256,2048]{2,1,0:T(8,128)(2,1)S(1)}, bf16[1,256,2048]{2,1,0:T(8,128)(2,1)}, u32[]{:S(2)}) copy-start(bf16[1,256,2048]{2,1,0:T(8,128)(2,1)} %param.16) | copy-start | bytes 3145732
  8.7 656.3 %all-gather.14.cloned.1.call-start = ((), (), s32[]{:S(2)}) async-start(), calls=%async_computation.14 | async-start | bytes 37748736 | tf_op jit(solution)/shard_map/all_gather | solution.py:172
  9.4 882.2 %all-gather.16.cloned.1.call-start = ((), (), s32[]{:S(2)}) async-start(), calls=%async_computation.15 | async-start | bytes 37748736 | tf_op jit(solution)/shard_map/all_gather | solution.py:173
  23.5 209.0 %copy-start.15 = (f32[8,1,256]{2,1,0:T(1,128)}, f32[8,1,256]{2,1,0:T(1,128)S(1)}, u32[]{:S(2)}) copy-start(f32[8,1,256]{2,1,0:T(1,128)S(1)} %convert_element_type.173) | copy-start | bytes 24580
  32.4 200.2 %copy-start.18 = (f32[8,1,256]{2,1,0:T(1,128)}, f32[8,1,256]{2,1,0:T(1,128)S(1)}, u32[]{:S(2)}) copy-start(f32[8,1,256]{2,1,0:T(1,128)S(1)} %convert_element_type.174) | copy-start | bytes 24580
  49.1 183.4 %copy-start.31 = (f32[16]{0:T(128)}, f32[16]{0:T(128)S(1)}, u32[]{:S(2)}) copy-start(f32[16]{0:T(128)S(1)} %multiply_power_fusion) | copy-start | bytes 196
  49.4 183.1 %copy-start.22 = (f32[256]{0:T(256)}, f32[256]{0:T(256)S(1)}, u32[]{:S(2)}) copy-start(f32[256]{0:T(256)S(1)} %broadcast_multiply_fusion) | copy-start | bytes 3076
  50.4 182.1 %copy-start.24 = (f32[256]{0:T(256)}, f32[256]{0:T(256)S(1)}, u32[]{:S(2)}) copy-start(f32[256]{0:T(256)S(1)} %fusion.68) | copy-start | bytes 3076
  276.5 16.4 all-to-all-start.1
  292.9 17.5 all-to-all-start.2
  297.2 763.1 %reduce-scatter.7.cloned.1.call-start = ((), (), s32[]{:S(2)}) async-start(), calls=%async_computation.17 | async-start | bytes 18874368 | tf_op jit(solution)/shard_map/reduce_scatter | solution.py:289
  398.8 15.3 all-to-all-start.4
  570.9 16.6 all-to-all-start.5
  587.5 16.7 all-to-all-start.6
  591.0 953.0 %reduce-scatter.5.cloned.1.call-start = ((), (), s32[]{:S(2)}) async-start(), calls=%async_computation.16 | async-start | bytes 56623104 | tf_op jit(solution)/shard_map/reduce_scatter | solution.py:288
  604.2 38.0 %copy-start.10 = (bf16[4,256,512]{1,2,0:T(8,128)(2,1)}, bf16[4,256,512]{1,2,0:T(8,128)(2,1)S(1)}, u32[]{:S(2)}) copy-start(bf16[4,256,512]{1,2,0:T(8,128)(2,1)S(1)} %all-to-all-done.6) | copy-start | bytes 3145732
  642.1 1542.9 %reduce-scatter.9.cloned.1.call-start = ((), (), s32[]{:S(2)}) async-start(), calls=%async_computation.18 | async-start | bytes 75497472 | tf_op jit(solution)/shard_map/reduce_scatter | solution.py:290
  665.0 226.6 %copy-start.9 = (bf16[1,256,2048]{2,1,0:T(8,128)(2,1)S(1)}, bf16[1,256,2048]{2,1,0:T(8,128)(2,1)}, u32[]{:S(2)}) copy-start(bf16[1,256,2048]{2,1,0:T(8,128)(2,1)} %param.27) | copy-start | bytes 3145732
  939.4 1886.5 %reduce-scatter.11.cloned.1.call-start = ((), (), s32[]{:S(2)}) async-start(), calls=%async_computation.19 | async-start | bytes 75497472 | tf_op jit(solution)/shard_map/reduce_scatter | solution.py:291
  967.7 1911.1 %all-reduce.12.cloned.1.call-start = ((), (), s32[]{:S(2)}) async-start(), calls=%async_computation.20 | async-start | bytes 163840
  1010.1 2322.5 %all-reduce.14.cloned.1.call-start = ((), (), s32[]{:S(2)}) async-start(), calls=%async_computation.21 | async-start | bytes 50331648 | tf_op jit(solution)/shard_map/psum | solution.py:299
  2900.0 440.0 %copy-start.35 = (f32[256]{0:T(256)}, f32[256]{0:T(256)S(1)}, u32[]{:S(2)}) copy-start(f32[256]{0:T(256)S(1)} %get-tuple-element.530) | copy-start | bytes 3076
  (40 other events, 445.5 us)
Sparse Core Ops, SparseCore 0:
  9.7 222.7 all-gather.9
  234.1 80.2 all-gather.11
  316.0 287.1 all-gather.13
  604.6 286.9 all-gather.15
  893.8 166.4 reduce-scatter.6
  1062.5 481.4 reduce-scatter.4
  1546.5 638.4 reduce-scatter.8
  2187.4 638.4 reduce-scatter.10
  2829.5 49.1 all-reduce.11
  2882.6 450.0 all-reduce.13
where the time goes:
time: 3370 us; the launch traced here: 3360 us
  waiting for transfers between devices  2690 us (80%)
  matrix products  294 us (9%)
  blocking collectives  160 us (5%)
  local copies, waits for them, and re-layouts  124 us (4%)
  other arithmetic  53.4 us (2%)
    reduce_scatter x1, waiting for transfers between devices, on_device(): lax.psum_scatter(up_local, 'fsdp', scatter_dimension=0, tiled=True)  641 us
    reduce_scatter x1, waiting for transfers between devices, on_device(): lax.psum_scatter(down_local, 'fsdp', scatter_dimension=0, tiled=True)  641 us
    reduce_scatter x1, waiting for transfers between devices, on_device(): lax.psum_scatter(qkv_local, 'fsdp', scatter_dimension=0, tiled=True)  484 us
    psum x1, waiting for transfers between devices, on_device(): lax.psum((shards[0], shards[1], shards[2], shards[3], shards[4], shards[5...  433 us
    all_gather x1, waiting for transfers between devices, on_device(): lax.all_gather(down_weight, 'fsdp', axis=0, tiled=True)  209 us
    all_gather x1, waiting for transfers between devices, on_device(): lax.all_gather(qkv_weight, 'fsdp', axis=0, tiled=True)  182 us
  transfers between devices with their start and end apart: 15, of which 13 were waited for; matrix products, arithmetic and copies ran while one was open for 13% of the time, Pallas kernels for 0%

commit v1 on v0

v1 whole, which is shorter than its diff:
```python
import functools

import jax
import jax.numpy as jnp
from jax import lax
from jax.experimental import pallas as pl
from jax.experimental.pallas import tpu as pltpu
from jax.sharding import PartitionSpec as P

HD = 64
ROT = 32
PAIR = 2 * HD
CORES = 2
BLOCK = 256

epsilon = 1e-05
rope_base = 10000.0
masked_score = -1000000000.0
f32 = jnp.float32
bf16 = jnp.bfloat16


def rotary_lanes(length):
    halves = ROT // 2
    lane = jnp.arange(PAIR) % HD
    frequency = rope_base ** (-(2.0 * (lane % halves).astype(f32)) / ROT)
    angles = jnp.arange(length).astype(f32)[:, None] * frequency[None, :]
    rotated = lane < ROT
    cos = jnp.where(rotated, jnp.cos(angles), 1.0)
    sin = jnp.sin(angles)
    from_right = jnp.where(lane < halves, -sin, 0.0)
    from_left = jnp.where((lane >= halves) & rotated, sin, 0.0)
    return cos, from_right, from_left


def turn(x, cos, from_right, from_left):
    halves = ROT // 2
    return (
        x * cos
        + pltpu.roll(x, PAIR - halves, 1) * from_right
        + pltpu.roll(x, halves, 1) * from_left
    )


def last_last(left, right):
    return lax.dot_general(left, right, (((1,), (1,)), ((), ())), preferred_element_type=f32)


def plain_dot(left, right):
    return jnp.dot(left, right, preferred_element_type=f32)


def head_lanes(head):
    lane = lax.broadcasted_iota(jnp.int32, (1, PAIR), 1)
    return (lane >= head * HD) & (lane < (head + 1) * HD)


def visible_block(block):
    key_place = lax.broadcasted_iota(jnp.int32, (block, block), 0)
    query_place = lax.broadcasted_iota(jnp.int32, (block, block), 1)
    return key_place <= query_place


def attend_kernel(mixed_ref, cos_ref, right_ref, left_ref, heads_ref, out_ref, logsum_ref, turned):
    length = mixed_ref.shape[0]
    block = min(BLOCK, length)
    tables = (cos_ref[...], right_ref[...], left_ref[...])
    heads_ref[:, :PAIR] = (turn(mixed_ref[:, :PAIR], *tables) * HD**-0.5).astype(bf16)
    heads_ref[:, PAIR : 2 * PAIR] = turn(mixed_ref[:, PAIR : 2 * PAIR], *tables).astype(bf16)
    heads_ref[:, 2 * PAIR :] = mixed_ref[:, 2 * PAIR :].astype(bf16)
    values_t = jnp.transpose(mixed_ref[:, 2 * PAIR :]).astype(bf16)
    visible = visible_block(block)
    for head in range(2):
        lanes = head_lanes(head)
        rows = slice(head * HD, (head + 1) * HD)
        for i in range(length // block):
            here = slice(i * block, (i + 1) * block)
            query = heads_ref[here, :PAIR]
            query = jnp.where(lanes, query, jnp.zeros_like(query))
            diag = last_last(heads_ref[here, PAIR : 2 * PAIR], query)
            diag = jnp.where(visible, diag, masked_score)
            highest = jnp.max(diag, axis=0, keepdims=True)
            if i > 0:
                past = last_last(heads_ref[: i * block, PAIR : 2 * PAIR], query)
                highest = jnp.maximum(highest, jnp.max(past, axis=0, keepdims=True))
            diag = jnp.exp(diag - highest)
            total = jnp.sum(diag, axis=0, keepdims=True)
            result = plain_dot(values_t[rows, here], diag.astype(bf16))
            if i > 0:
                past = jnp.exp(past - highest)
                total = total + jnp.sum(past, axis=0, keepdims=True)
                result = result + plain_dot(values_t[rows, : i * block], past.astype(bf16))
            turned[rows, here] = result / total
            logsum_ref[head : head + 1, here] = highest + jnp.log(total)
    out_ref[...] = jnp.transpose(turned[...]).astype(bf16)


def attend_back_kernel(
    heads_ref, grad_ref, logsum_ref, cos_ref, right_ref, left_ref, back_ref, turned, key_sum, value_sum
):
    length = heads_ref.shape[0]
    block = min(BLOCK, length)
    tables = (cos_ref[...], -right_ref[...], -left_ref[...])
    scaled = heads_ref[:, PAIR : 2 * PAIR].astype(f32) * HD**-0.5
    keys_t = jnp.transpose(scaled).astype(bf16)
    visible = visible_block(block)
    key_sum[...] = jnp.zeros_like(key_sum)
    value_sum[...] = jnp.zeros_like(value_sum)
    for head in range(2):
        lanes = head_lanes(head)
        rows = slice(head * HD, (head + 1) * HD)
        for i in range(length // block):
            here = slice(i * block, (i + 1) * block)
            upto = slice(0, (i + 1) * block)
            query = heads_ref[here, :PAIR]
            query = jnp.where(lanes, query, jnp.zeros_like(query))
            grad = grad_ref[here, :]
            grad = jnp.where(lanes, grad, jnp.zeros_like(grad))
            logsum = logsum_ref[head : head + 1, here]
            parts = []
            inner = None
            for begin, end in ((0, i * block), (i * block, (i + 1) * block)):
                if begin == end:
                    continue
                probs = jnp.exp(last_last(heads_ref[begin:end, PAIR : 2 * PAIR], query) - logsum)
                if end > i * block:
                    probs = jnp.where(visible, probs, 0.0)
                prob_grad = last_last(heads_ref[begin:end, 2 * PAIR :], grad)
                term = jnp.sum(probs * prob_grad, axis=0, keepdims=True)
                inner = term if inner is None else inner + term
                parts.append((begin, end, probs, prob_grad))
            query_grad = None
            for begin, end, probs, prob_grad in parts:
                score_grad = (probs * (prob_grad - inner)).astype(bf16)
                value_sum[begin:end, :] += plain_dot(probs.astype(bf16), grad)
                key_sum[begin:end, :] += plain_dot(score_grad, query)
                term = plain_dot(keys_t[rows, begin:end], score_grad)
                query_grad = term if query_grad is None else query_grad + term
            turned[rows, here] = query_grad
    back_ref[:, :PAIR] = turn(jnp.transpose(turned[...]), *tables).astype(bf16)
    back_ref[:, PAIR : 2 * PAIR] = turn(key_sum[...], *tables).astype(bf16)
    back_ref[:, 2 * PAIR :] = value_sum[...].astype(bf16)


def attend(mixed, tables, length):
    count, width = mixed.shape[0] // length, mixed.shape[1]
    pairs = width // (3 * PAIR)
    table = pl.BlockSpec((length, PAIR), lambda n, p: (0, 0))
    wide = pl.BlockSpec((length, 3 * PAIR), lambda n, p: (n, p))
    return pl.pallas_call(
        attend_kernel,
        grid=(count, pairs),
        in_specs=[wide, table, table, table],
        out_specs=[
            wide,
            pl.BlockSpec((length, PAIR), lambda n, p: (n, p)),
            pl.BlockSpec((None, None, 2, length), lambda n, p: (n, p, 0, 0)),
        ],
        out_shape=[
            jax.ShapeDtypeStruct(mixed.shape, bf16),
            jax.ShapeDtypeStruct((count * length, pairs * PAIR), bf16),
            jax.ShapeDtypeStruct((count, pairs, 2, length), f32),
        ],
        scratch_shapes=[pltpu.VMEM((PAIR, length), f32)],
        compiler_params=pltpu.CompilerParams(vmem_limit_bytes=40 * 1024 * 1024),
        cost_estimate=pl.CostEstimate(
            flops=count * pairs * 2 * length * length * 64 * 4,
            bytes_accessed=mixed.size * 8,
            transcendentals=count * pairs * length * length,
        ),
        name="attend",
    )(mixed, *tables)


def attend_back(heads, grad, logsums, tables, length):
    count, width = heads.shape[0] // length, heads.shape[1]
    pairs = width // (3 * PAIR)
    table = pl.BlockSpec((length, PAIR), lambda n, p: (0, 0))
    wide = pl.BlockSpec((length, 3 * PAIR), lambda n, p: (n, p))
    return pl.pallas_call(
        attend_back_kernel,
        grid=(count, pairs),
        in_specs=[
            wide,
            pl.BlockSpec((length, PAIR), lambda n, p: (n, p)),
            pl.BlockSpec((None, None, 2, length), lambda n, p: (n, p, 0, 0)),
            table,
            table,
            table,
        ],
        out_specs=wide,
        out_shape=jax.ShapeDtypeStruct(heads.shape, bf16),
        scratch_shapes=[
            pltpu.VMEM((PAIR, length), f32),
            pltpu.VMEM((length, PAIR), f32),
            pltpu.VMEM((length, PAIR), f32),
        ],
        compiler_params=pltpu.CompilerParams(vmem_limit_bytes=40 * 1024 * 1024),
        cost_estimate=pl.CostEstimate(
            flops=count * pairs * 2 * length * length * 64 * 10,
            bytes_accessed=heads.size * 6,
            transcendentals=count * pairs * length * length,
        ),
        name="attend_back",
    )(heads, grad, logsums, *tables)


def norm_kernel(place_ref, gain_ref, bias_ref, *refs):
    *pieces, out_ref = refs
    half = len(pieces) // 2
    for i, piece in enumerate(pieces):

        @pl.when(pl.program_id(0) == i // half * half + ((i % half) ^ place_ref[0]))
        def _(piece=piece):
            x = piece[...].astype(f32)
            centred = x - jnp.mean(x, axis=-1, keepdims=True)
            variance = jnp.mean(centred * centred, axis=-1, keepdims=True)
            out_ref[...] = (
                centred * lax.rsqrt(variance + epsilon) * gain_ref[...] + bias_ref[...]
            ).astype(bf16)


def norm_both(place, pieces, gain, bias):
    local, d = pieces[0].shape
    fixed = lambda i, place: (0, 0)
    return pl.pallas_call(
        norm_kernel,
        grid_spec=pltpu.PrefetchScalarGridSpec(
            num_scalar_prefetch=1,
            grid=(len(pieces),),
            in_specs=[pl.BlockSpec((1, d), fixed)] * 2 + [pl.BlockSpec((local, d), fixed)] * len(pieces),
            out_specs=pl.BlockSpec((local, d), lambda i, place: (i, 0)),
        ),
        out_shape=jax.ShapeDtypeStruct((len(pieces) * local, d), bf16),
        compiler_params=pltpu.CompilerParams(vmem_limit_bytes=48 * 1024 * 1024),
        name="norm_both",
    )(place, gain[None], bias[None], *pieces)


def order_kernel(place_ref, *refs):
    *pieces, out_ref = refs
    for i, piece in enumerate(pieces):

        @pl.when(pl.program_id(0) == i)
        def _(piece=piece):
            out_ref[...] = piece[...]


def order_both(place, pieces):
    local, d = pieces[0].shape
    half = len(pieces) // 2
    return pl.pallas_call(
        order_kernel,
        grid_spec=pltpu.PrefetchScalarGridSpec(
            num_scalar_prefetch=1,
            grid=(len(pieces),),
            in_specs=[pl.BlockSpec((local, d), lambda i, place: (0, 0))] * len(pieces),
            out_specs=pl.BlockSpec(
                (local, d),
                lambda i, place: (
                    jnp.where(i < half, i ^ place[0], half + ((i - half) ^ place[0])),
                    0,
                ),
            ),
        ),
        out_shape=jax.ShapeDtypeStruct((len(pieces) * local, d), pieces[0].dtype),
        compiler_params=pltpu.CompilerParams(vmem_limit_bytes=48 * 1024 * 1024),
        name="order_both",
    )(place, *pieces)


def row_blocks(rows):
    return min(64, rows)


def unit_kernel(nz, ns, w, place_ref, in_ref, out_ref):
    for c in range(CORES):
        for q in range(nz):
            at = pl.multiple_of(((q * CORES + c) * ns + place_ref[0]) * w, w)
            to = (c * nz + q) * w
            out_ref[:, to : to + w] = in_ref[:, pl.ds(at, w)]


def unit_columns(weight, place, nz, ns, w):
    rows, ff = weight.shape
    block = row_blocks(rows)
    wide = CORES * nz * w
    return pl.pallas_call(
        functools.partial(unit_kernel, nz, ns, w),
        grid_spec=pltpu.PrefetchScalarGridSpec(
            num_scalar_prefetch=1,
            grid=(rows // block,),
            in_specs=[pl.BlockSpec((block, ff), lambda i, place: (i, 0))],
            out_specs=pl.BlockSpec((block, wide), lambda i, place: (i, 0)),
        ),
        out_shape=jax.ShapeDtypeStruct((rows, wide), weight.dtype),
        name="unit_columns",
    )(place, weight)


def place_units_kernel(nz, w, place_ref, *refs):
    *pieces, out_ref = refs
    ns = len(pieces)
    for d, piece in enumerate(pieces):
        device = place_ref[0] ^ d
        for q in range(nz):
            for c in range(CORES):
                to = pl.multiple_of(((q * CORES + c) * ns + device) * w, w)
                out_ref[:, pl.ds(to, w)] = piece[c, :, q * w : (q + 1) * w].astype(f32)


def place_units(place, pieces, nz, w):
    cores, rows, width = pieces[0].shape
    block = row_blocks(rows)
    ff = width * cores * len(pieces)
    return pl.pallas_call(
        functools.partial(place_units_kernel, nz, w),
        grid_spec=pltpu.PrefetchScalarGridSpec(
            num_scalar_prefetch=1,
            grid=(rows // block,),
            in_specs=[pl.BlockSpec((cores, block, width), lambda i, place: (0, i, 0)) for _ in pieces],
            out_specs=pl.BlockSpec((block, ff), lambda i, place: (i, 0)),
        ),
        out_shape=jax.ShapeDtypeStruct((rows, ff), f32),
        name="place_units",
    )(place, *pieces)


def low_half():
    return lax.broadcasted_iota(jnp.int32, (1, PAIR), 1) < HD


def lows(first, second):
    return jnp.where(low_half(), first, pltpu.roll(second, HD, 1))


def highs(first, second):
    return jnp.where(low_half(), pltpu.roll(first, HD, 1), second)


def head_kernel(nz, ns, place_ref, in_ref, out_ref):
    tiles = ns // 2
    part = nz * CORES * tiles
    even = lax.rem(place_ref[0], 2) == 0

    def tile(j, q, c):
        at = (j * part + (q * CORES + c) * tiles + lax.div(place_ref[0], 2)) * PAIR
        return in_ref[:, pl.ds(pl.multiple_of(at, PAIR), PAIR)].astype(f32)

    for c in range(CORES):
        for p in range(nz // 2):
            for j in range(3):
                first, second = tile(j, 2 * p, c), tile(j, 2 * p + 1, c)
                to = ((c * (nz // 2) + p) * 3 + j) * PAIR
                out_ref[:, to : to + PAIR] = jnp.where(
                    even, lows(first, second), highs(first, second)
                ).astype(out_ref.dtype)


def head_columns(weight, place, nz, ns):
    rows, width = weight.shape
    block = row_blocks(rows)
    wide = CORES * nz * 3 * HD
    return pl.pallas_call(
        functools.partial(head_kernel, nz, ns),
        grid_spec=pltpu.PrefetchScalarGridSpec(
            num_scalar_prefetch=1,
            grid=(rows // block,),
            in_specs=[pl.BlockSpec((block, width), lambda i, place: (i, 0))],
            out_specs=pl.BlockSpec((block, wide), lambda i, place: (i, 0)),
        ),
        out_shape=jax.ShapeDtypeStruct((rows, wide), weight.dtype),
        name="head_columns",
    )(place, weight)


def place_heads_kernel(nz, place_ref, *refs):
    *pieces, out_ref = refs
    tiles = len(pieces) // 2
    even = lax.rem(place_ref[0], 2) == 0
    for d in range(0, len(pieces), 2):
        tile = lax.div(place_ref[0] ^ d, 2)
        for j in range(3):
            for p in range(nz // 2):
                at = (p * 3 + j) * PAIR
                for c in range(CORES):
                    one = pieces[d][c, :, at : at + PAIR].astype(f32)
                    two = pieces[d + 1][c, :, at : at + PAIR].astype(f32)
                    first, second = jnp.where(even, one, two), jnp.where(even, two, one)
                    for q, value in ((2 * p, lows(first, second)), (2 * p + 1, highs(first, second))):
                        to = (((j * nz + q) * CORES + c) * tiles + tile) * PAIR
                        out_ref[:, pl.ds(pl.multiple_of(to, PAIR), PAIR)] = value


def place_heads(place, pieces, nz):
    cores, rows, width = pieces[0].shape
    block = row_blocks(rows)
    whole = width * cores * len(pieces)
    return pl.pallas_call(
        functools.partial(place_heads_kernel, nz),
        grid_spec=pltpu.PrefetchScalarGridSpec(
            num_scalar_prefetch=1,
            grid=(rows // block,),
            in_specs=[pl.BlockSpec((cores, block, width), lambda i, place: (0, i, 0)) for _ in pieces],
            out_specs=pl.BlockSpec((block, whole), lambda i, place: (i, 0)),
        ),
        out_shape=jax.ShapeDtypeStruct((rows, whole), f32),
        name="place_heads",
    )(place, *pieces)


def gelu_and_slope(u):
    cubic = 0.044715
    root = 0.7978845608
    square = u * u
    t = jnp.tanh(root * u * (1.0 + cubic * square))
    value = 0.5 * u * (1.0 + t)
    slope = 0.5 * (1.0 + t) + 0.5 * u * (1.0 - t * t) * root * (1.0 + 3.0 * cubic * square)
    return value, slope


def on_device(
    ns,
    nf,
    tokens,
    qkv_weight,
    out_weight,
    up_weight,
    down_weight,
    norm_gain,
    norm_bias,
    qkv_bias,
    out_bias,
    up_bias,
    down_bias,
    cotangent,
):
    nz = nf // CORES
    ranks = CORES * ns
    s = lax.axis_index("seq")
    f = lax.axis_index("fsdp")
    k = f % CORES
    z = f // CORES
    local, d = tokens.shape[1:]
    length = ns * local
    rows = qkv_weight.shape[0]
    ff = up_weight.shape[1]
    w = ff // (nf * ns)
    shard_heads = rows // HD
    spread = shard_heads % ns == 0 and (shard_heads // ns * nz) % 2 == 0
    hw = shard_heads // ns * HD
    one_each = spread and hw == HD and ns % 2 == 0 and nz % 2 == 0
    tiled = w % PAIR == 0
    place = s[None].astype(jnp.int32)
    rank_cols = d // ranks
    pairs = rank_cols // PAIR
    lines = [[CORES * z + c for z in range(nz)] for c in range(CORES)]
    swap = [(i, i ^ 1) for i in range(nf)]
    everyone = ("seq", "fsdp")

    def after(x, *others):
        return lax.optimization_barrier((x,) + others)[0]

    def other_core(x):
        return lax.ppermute(x, "fsdp", swap)

    def plane_send(x, d):
        return lax.ppermute(x, "seq", [(i, i ^ d) for i in range(ns)])

    def plane_pieces(x):
        return [x] + [plane_send(x, d) for d in range(1, ns)]

    def arrange(pieces, dtype):
        size = pieces[0].shape[0]
        whole = jnp.zeros((ns * size,) + pieces[0].shape[1:], dtype)
        for d, piece in enumerate(pieces):
            whole = lax.dynamic_update_slice_in_dim(whole, piece.astype(dtype), (s ^ d) * size, 0)
        return whole

    def pick(x, index, axis):
        return lax.dynamic_index_in_dim(x, index, axis, keepdims=False)

    vectors = (norm_gain, norm_bias, qkv_bias, out_bias, up_bias, down_bias)
    sizes = [v.shape[0] for v in vectors]
    small = jnp.concatenate(vectors)
    small = jnp.broadcast_to(small[None], (nf,) + small.shape)
    small = lax.all_to_all(small, "fsdp", split_axis=0, concat_axis=0, tiled=True)
    cuts, at = [], 0
    for size in sizes:
        cuts.append(small[:, at : at + size].reshape(-1).astype(f32))
        at += size
    gain, nbias, qkvb, outb, upb, downb = cuts

    def heads_of(weight):
        lead = weight.shape[0]
        if spread:
            part = pick(weight.reshape(lead, 3, nz, CORES, ns, hw), s, 4)
            part = part.transpose(0, 3, 1, 2, 4).reshape(lead, CORES, 3, pairs, PAIR)
        else:
            part = pick(weight.reshape(lead, 3, ns, CORES, pairs, PAIR), s, 2)
            part = part.transpose(0, 2, 1, 3, 4)
        return part.transpose(0, 1, 3, 2, 4).reshape(lead, CORES, 3 * rank_cols)

    def units_of(weight):
        lead = weight.shape[0]
        part = pick(weight.reshape(lead, nz, CORES, ns, w), s, 3)
        return part.transpose(0, 2, 1, 3).reshape(lead, CORES, nz * w)

    def core_half(x):
        return lax.dynamic_slice_in_dim(x, k * (x.shape[1] // CORES), x.shape[1] // CORES, 1)

    qkvb_mine = pick(heads_of(qkvb[None])[0], k, 0)
    upb_mine = pick(units_of(upb[None])[0], k, 0)
    tables = rotary_lanes(length)

    up_both = units_of(up_weight) if not tiled else unit_columns(up_weight, place, nz, ns, w)
    up_both = lax.all_gather(up_both.reshape(rows, -1), "fsdp", axis=0, tiled=True)
    up_mine = core_half(up_both)

    qkv_part = heads_of(qkv_weight) if not one_each else head_columns(qkv_weight, place, nz, ns)
    qkv_part = qkv_part.reshape(rows, CORES, -1)
    down_part = lax.dynamic_slice_in_dim(down_weight, s * w, w, 0)
    out_part = lax.dynamic_slice_in_dim(out_weight, s * hw, hw, 0)

    x_pieces = plane_pieces(tokens[0])
    ready = (gain, nbias, qkvb_mine, upb_mine, qkv_part, down_part, out_part) + tuple(tables)
    x_pieces = x_pieces[:1] + [after(piece, *ready) for piece in x_pieces[1:]]
    c_pieces = plane_pieces(after(cotangent[0], *x_pieces[1:]))
    x_pieces = x_pieces + [other_core(piece) for piece in x_pieces]

    down_part = after(down_part, x_pieces[ns - 1])
    down_mine = lax.all_gather(down_part, "fsdp", axis=0, tiled=True, axis_index_groups=lines)

    normed = norm_both(place, x_pieces, gain, nbias)

    qkv_part = after(qkv_part, normed)
    if one_each:
        keep = pick(qkv_part, k, 1)
        got = other_core(pick(qkv_part, 1 - k, 1))
        both = jnp.concatenate([jnp.where(k == 0, keep, got), jnp.where(k == 0, got, keep)])
        wide = hw * d // (CORES * rows)
        beside = out_part.reshape(hw, -1, wide).transpose(1, 0, 2).reshape(CORES * rows, wide)
        both = jnp.concatenate([both, beside], axis=1)
        both = lax.all_gather(both, "fsdp", axis=0, tiled=True, axis_index_groups=lines)
    else:
        qkv_both = lax.all_gather(qkv_part.reshape(rows, -1), "fsdp", axis=0, tiled=True)
        qkv_mine = core_half(qkv_both)
        if spread:
            out_mine = lax.all_gather(out_part, "fsdp", axis=0, tiled=True, axis_index_groups=lines)
        else:
            out_full = lax.all_gather(out_weight, "fsdp", axis=0, tiled=True)
            out_mine = lax.dynamic_slice_in_dim(out_full, (CORES * s + k) * rank_cols, rank_cols, 0)

    def first_first(left, right):
        return lax.dot_general(left, right, (((0,), (0,)), ((), ())), preferred_element_type=f32)

    pinned = after

    class Walk:
        def __init__(self, x):
            self.blocks = x.reshape((nz, -1) + x.shape[1:])
            self.hop = 0
            self.got = None

        def parts(self):
            hop = self.hop + 1
            ends = (jnp.minimum(nz - hop + z, nz - 1), jnp.maximum(hop + z - nz, 0))
            parts = [pick(self.blocks, end, 0) for end in ends]
            if self.got is not None:
                parts = [(p.astype(f32) + g.astype(f32)).astype(bf16) for p, g in zip(parts, self.got)]
            return parts

        def step(self, hops=1, after=None):
            parts = []
            for _ in range(hops):
                if after is not None:
                    self.got = [pinned(g, after) for g in self.got]
                parts = self.parts()
                self.hop += 1
                self.got = [step_line(p, self.hop, way) for p, way in zip(parts, (True, False))]
            return parts

        def rest(self, after=None):
            return self.step(nz - 1 - self.hop, after)

        def own(self):
            own = pick(self.blocks, z, 0).astype(f32)
            return (own + self.got[0].astype(f32) + self.got[1].astype(f32)).astype(bf16)

    def step_line(part, hops, forward):
        hops_ = []
        for c in range(CORES):
            for q in range(hops):
                at, to = (q, q + 1) if forward else (nz - 1 - q, nz - 2 - q)
                hops_.append((CORES * at + c, CORES * to + c))
        return lax.ppermute(part, "fsdp", hops_)

    def both_cores(x):
        keep = lax.dynamic_slice_in_dim(x, k * rows, rows, 0)
        got = other_core(lax.dynamic_slice_in_dim(x, (1 - k) * rows, rows, 0))
        return jnp.stack([jnp.where(k == 0, keep, got), jnp.where(k == 0, got, keep)])

    hidden = plain_dot(normed, up_mine) + upb_mine
    activated, slope = gelu_and_slope(hidden)
    activated = activated.astype(bf16)
    c_pieces = c_pieces[:1] + [after(piece, activated) for piece in c_pieces[1:]]
    c2 = order_both(place, c_pieces + [other_core(piece) for piece in c_pieces])
    down_local = first_first(activated, c2).astype(bf16)
    down_walk = Walk(down_local)
    down_walk.step()
    c2, down_mine = after(c2, down_local), after(down_mine, down_local)
    hidden_grad = (last_last(c2, down_mine) * slope).astype(bf16)
    hidden_grad = after(hidden_grad, *down_walk.step())
    up_local = first_first(normed, hidden_grad).astype(bf16)
    up_walk = Walk(up_local)
    up_walk.step()
    activated = after(activated, up_local)
    ff_branch = plain_dot(activated, down_mine).astype(bf16)
    hidden_grad = after(hidden_grad, ff_branch)
    ff_back = last_last(hidden_grad, up_mine).astype(bf16)

    if one_each:
        both = after(both, ff_back)
        qkv_mine = both[:, : 3 * rank_cols]
        out_mine = both[:, 3 * rank_cols :].reshape(nz, -1, hw, wide).transpose(0, 2, 1, 3)
        out_mine = out_mine.reshape(rank_cols, d)
    normed = after(normed, ff_back, *down_walk.rest())
    mixed = plain_dot(normed, qkv_mine) + qkvb_mine
    mixed = after(mixed, *up_walk.step())
    heads, attended, logsums = attend(mixed, tables, length)
    down_own = down_walk.own()
    down_pieces = plane_pieces(down_own)
    attended = after(attended, down_own)
    out_local = first_first(attended, c2).astype(bf16)
    if spread:
        out_walk = Walk(out_local)
        out_walk.step()
    c2 = after(c2, out_local)
    attended_grad = last_last(c2, out_mine).astype(bf16)
    attended = after(attended, attended_grad)

    def both_halves(left, right, dot, more):
        far = (dot(left[length:], right) + more[length:].astype(f32)).astype(bf16)
        got = other_core(far)
        near = (dot(after(left, far)[:length], right) + more[:length].astype(f32)).astype(bf16)
        return near, got

    def rank_parts(near, got):
        parts = []
        for d in range(ns):
            at = (s ^ d) * local
            part = lax.dynamic_slice_in_dim(near, at, local, 0).astype(f32)
            part = part + lax.dynamic_slice_in_dim(got, at, local, 0).astype(f32)
            parts.append(part if d == 0 else part.astype(bf16))
        return parts

    def rank_sum(parts, *passed):
        total = parts[0]
        for d in range(1, ns):
            total = total + after(plane_send(parts[d], d), *passed).astype(f32)
        return total

    near, got = both_halves(attended, out_mine, plain_dot, ff_branch)
    attended_grad = after(attended_grad, near, *up_walk.rest())
    mixed_grad = attend_back(heads, attended_grad, logsums, tables, length)
    normed = after(normed, mixed_grad)
    qkv_local = first_first(normed, mixed_grad).astype(bf16)
    if spread:
        qkv_walk = Walk(qkv_local)
        qkv_walk.step()
    branch_parts = rank_parts(near, after(got, qkv_local))
    mixed_grad = after(mixed_grad, *branch_parts)
    near, got = both_halves(mixed_grad, qkv_mine, last_last, ff_back)
    up_walk.got = [after(g, near) for g in up_walk.got]
    up_own = up_walk.own()
    up_both = both_cores(up_own)
    passed = [up_both]
    if spread:
        passed += qkv_walk.step(after=up_own)
        passed += out_walk.step(after=up_own)
    up_pieces = plane_pieces(up_both)
    grad_parts = rank_parts(near, after(got, *passed))
    branches = rank_sum(branch_parts, *grad_parts)
    if spread:
        passed = qkv_walk.rest(after=grad_parts[1]) + out_walk.rest(after=grad_parts[1])
    normed_grad = rank_sum(grad_parts, *passed)
    if spread:
        qkv_own, out_own = qkv_walk.own(), out_walk.own()
        out_pieces = plane_pieces(out_own)
    else:
        qkv_own = lax.psum_scatter(
            qkv_local, "fsdp", scatter_dimension=0, tiled=True, axis_index_groups=lines
        )
    qkv_both = both_cores(qkv_own)
    qkv_pieces = plane_pieces(qkv_both)
    up_pieces = up_pieces[:1] + [after(piece, qkv_both) for piece in up_pieces[1:]]
    down_pieces = down_pieces[:1] + [after(piece, near) for piece in down_pieces[1:]]

    token_rows = tokens[0].astype(f32)
    block_out = (token_rows + branches + outb + downb).astype(bf16)[None]

    centred_own = token_rows - jnp.mean(token_rows, axis=-1, keepdims=True)
    variance_own = jnp.mean(centred_own * centred_own, axis=-1, keepdims=True)
    inverse = lax.rsqrt(variance_own + epsilon)
    xhat = centred_own * inverse
    g = normed_grad * gain
    rows_grad = inverse * (
        g - jnp.mean(g, axis=-1, keepdims=True) - xhat * jnp.mean(g * xhat, axis=-1, keepdims=True)
    )
    upstream = cotangent[0].astype(f32)
    tokens_grad = (upstream + rows_grad).astype(bf16)[None]

    if spread and one_each:
        qkv_wgrad = place_heads(place, qkv_pieces, nz)
    elif spread:
        qkv_all = arrange([piece[None] for piece in qkv_pieces], bf16)
        qkv_all = qkv_all.reshape(ns, CORES, rows, pairs, 3, PAIR).transpose(0, 1, 2, 4, 3, 5)
        qkv_all = qkv_all.reshape(ns, CORES, rows, 3, nz, hw)
        qkv_wgrad = qkv_all.transpose(2, 3, 4, 1, 0, 5).reshape(rows, 3 * d).astype(f32)
    else:
        qkv_all = arrange([piece[None] for piece in qkv_pieces], bf16)
        qkv_all = qkv_all.reshape(ns, CORES, rows, pairs, 3, PAIR)
        qkv_wgrad = qkv_all.transpose(2, 4, 0, 1, 3, 5).reshape(rows, 3 * d).astype(f32)
    if spread:
        out_wgrad = arrange(out_pieces, f32)
    else:
        rank = CORES * s + k
        out_padded = lax.dynamic_update_slice_in_dim(
            jnp.zeros((d, d), bf16), out_local, rank * rank_cols, 0
        )
        out_shard = lax.psum_scatter(out_padded, "fsdp", scatter_dimension=0, tiled=True)
        out_wgrad = lax.psum(out_shard.astype(f32), "seq")
    if tiled:
        up_wgrad = place_units(place, up_pieces, nz, w)
    else:
        up_all = arrange([piece[None] for piece in up_pieces], bf16)
        up_all = up_all.reshape(ns, CORES, rows, nz, w)
        up_wgrad = up_all.transpose(2, 3, 1, 0, 4).reshape(rows, ff).astype(f32)
    down_wgrad = arrange(down_pieces, f32)

    mixed_sum = jnp.sum(mixed_grad.astype(f32), axis=0).reshape(pairs, 3, PAIR).transpose(1, 0, 2)
    if spread:
        mixed_sum = mixed_sum.reshape(3, nz, 1, 1, hw)
        mixed_full = jnp.zeros((3, nz, CORES, ns, hw), f32)
        mixed_full = lax.dynamic_update_slice(mixed_full, mixed_sum, (0, 0, k, s, 0))
    else:
        mixed_full = jnp.zeros((3, ns, CORES, rank_cols), f32)
        mixed_full = lax.dynamic_update_slice(
            mixed_full, mixed_sum.reshape(3, 1, 1, rank_cols), (0, s, k, 0)
        )
    hidden_sum = jnp.sum(hidden_grad.astype(f32), axis=0).reshape(nz, 1, 1, w)
    hidden_full = lax.dynamic_update_slice(
        jnp.zeros((nz, CORES, ns, w), f32), hidden_sum, (0, k, s, 0)
    )
    gain_local = jnp.sum(xhat * normed_grad, axis=0)
    nbias_local = jnp.sum(normed_grad, axis=0)
    c_local = jnp.sum(upstream, axis=0)
    sums = (
        mixed_full.reshape(-1)[: 2 * d],
        mixed_full.reshape(-1)[2 * d :],
        hidden_full.reshape(-1),
        gain_local,
        nbias_local,
        c_local,
    )
    flat = jnp.concatenate([v.reshape(nf, -1) for v in sums], axis=1)
    flat = jnp.broadcast_to(flat[None], (ns,) + flat.shape).reshape(ns * nf, -1)
    flat = lax.all_to_all(flat, everyone, split_axis=0, concat_axis=0, tiled=True)
    flat = jnp.sum(flat, axis=0)
    shards, at = [], 0
    for v in sums:
        size = v.shape[0] // nf
        shards.append(flat[at : at + size])
        at += size
    qkv_bgrad, value_bgrad, up_bgrad, gain_grad, norm_bgrad, out_bgrad = shards

    return (
        block_out,
        tokens_grad,
        qkv_wgrad,
        out_wgrad,
        up_wgrad,
        down_wgrad,
        gain_grad,
        norm_bgrad,
        qkv_bgrad,
        value_bgrad,
        out_bgrad,
        up_bgrad,
        out_bgrad,
    )


def solution(mesh):
    sharded = P("fsdp", "seq", None)
    matrix = P("fsdp", None)
    vector = P("fsdp")
    return jax.shard_map(
        functools.partial(on_device, mesh.shape["seq"], mesh.shape["fsdp"]),
        mesh=mesh,
        in_specs=(sharded,) + (matrix,) * 4 + (vector,) * 6 + (sharded,),
        out_specs=(sharded,) * 2 + (matrix,) * 4 + (vector,) * 7,
        check_vma=False,
    )
```

time: 3370 us -> 735 us (0.22)
  waiting for transfers between devices: 2690 us -> 277 us
  matrix products: 294 us -> 132 us
  blocking collectives: 160 us -> 0 us
  starting transfers between devices: 19.3 us -> 126 us
  local copies, waits for them, and re-layouts: 124 us -> 34.8 us
  Pallas kernels: 0 us -> 75.2 us
    reduce_scatter x4 -> x0, waiting for transfers between devices: 1820 us -> none  [the longest x1 641 us: on_device(): lax.psum_scatter(up_local, 'fsdp', scatter_dimension=0, tiled=True)]
    psum x1 -> x0, waiting for transfers between devices: 433 us -> none  [on_device(): lax.psum((shards[0], shards[1], shards[2], shards[3], shards[4], shards[5...]
    all_gather x4 -> x3, waiting for transfers between devices: 391 us -> 60.1 us  [the longest x1 32.8 us: on_device(): lax.all_gather(both, 'fsdp', axis=0, tiled=True, axis_index_groups=lines)]
    ppermute x0 -> x61, waiting for transfers between devices: none -> 217 us  [the longest x24 169 us: plane_send(): return lax.ppermute(x, 'seq', [(i, i ^ d) for i in range(ns)])]
    dot_general x26 -> x14, matrix products: 294 us -> 132 us  [the longest x5 50.2 us: plain_dot(): return jnp.dot(left, right, preferred_element_type=f32)]
    ppermute x0 -> x61, starting transfers between devices: none -> 115 us  [the longest x24 73.8 us: step_line(): return lax.ppermute(part, 'fsdp', hops_)]
    all_gather x6 -> x0, blocking collectives: 80 us -> none  [the longest x1 22.2 us: on_device(): lax.all_gather(up_bias, 'fsdp', axis=0, tiled=True)]
    pallas_call x0 -> x8, Pallas kernels: none -> 75.2 us  [the longest x1 20.2 us: attend_back(): pl.pallas_call(attend_back_kernel, grid=(count, pairs), in_specs=[wide, p...]
  transfers between devices with their start and end apart: 15 -> 66, of which waited for: 13 -> 26; matrix products, arithmetic and copies ran while one was open for 13% -> 31% of each run, Pallas kernels for 0% -> 9%
where the time goes in v1:
time: 735 us; the launch traced here: 729 us
  waiting for transfers between devices  277 us (38%)
  matrix products  132 us (18%)
  starting transfers between devices  126 us (17%)
  Pallas kernels  75.2 us (10%)
  other arithmetic  68.6 us (9%)
  local copies, waits for them, and re-layouts  34.8 us (5%)
  between operations  15.3 us (2%)
    ppermute x24, waiting for transfers between devices, plane_send(): return lax.ppermute(x, 'seq', [(i, i ^ d) for i in range(ns)])  169 us
    ppermute x24, starting transfers between devices, step_line(): return lax.ppermute(part, 'fsdp', hops_)  73.8 us
    dot_general x5, matrix products, plain_dot(): return jnp.dot(left, right, preferred_element_type=f32)  50.2 us
    dot_general x5, matrix products, last_last(): lax.dot_general(left, right, (((1,), (1,)), ((), ())), preferred_element_...  48 us
    ppermute x24, waiting for transfers between devices, step_line(): return lax.ppermute(part, 'fsdp', hops_)  43.3 us
    ppermute x24, starting transfers between devices, plane_send(): return lax.ppermute(x, 'seq', [(i, i ^ d) for i in range(ns)])  38.7 us
    dot_general x4, matrix products, first_first(): lax.dot_general(left, right, (((0,), (0,)), ((), ())), preferred_element_...  33.3 us
    all_gather x1, waiting for transfers between devices, on_device(): lax.all_gather(both, 'fsdp', axis=0, tiled=True, axis_index_groups=lines)  32.8 us
  transfers between devices with their start and end apart: 66, of which 26 were waited for; matrix products, arithmetic and copies ran while one was open for 31% of the time, Pallas kernels for 9%

profile of v1, /device:TPU:0, one launch (start us, length us, event | category | flops | bytes accessed | tf_op | source)
XLA Modules:
  0.0 728.9 jit_solution(12191645273202367838)
XLA Ops:
  38.3 9.6 %collective-permute-done.2.refs_3_ = bf16[256,2048]{1,0:T(8,128)(2,1)} collective-permute-done((bf16[256,2048]{1,0:T(8,128)(2,1)S(1)}, bf16[256,2048]{1,0:T(8,128)(2,1)}, u32[]{:S(2)}, u32[]{:S(2)}) %collective-permute-start.2) | collective-permute-done | bytes 1048608 | tf_op jit(solution)/shard_map/ppermute | solution.py:468
  51.1 21.8 %collective-permute-done.1.refs_2_ = bf16[256,2048]{1,0:T(8,128)(2,1)} collective-permute-done((bf16[256,2048]{1,0:T(8,128)(2,1)S(1)}, bf16[256,2048]{1,0:T(8,128)(2,1)}, u32[]{:S(2)}, u32[]{:S(2)}) %collective-permute-start.1) | collective-permute-done | bytes 1048608 | tf_op jit(solution)/shard_map/ppermute | solution.py:468
  81.8 11.6 %norm_both.1 = bf16[2048,2048]{1,0:T(8,128)(2,1)} custom-call(s32[1]{0:T(128)} %bitcast.1.place_ref, f32[1,2048]{1,0:T(1,128)S(1)} %bitcast.194, f32[1,2048]{1,0:T(1,128)S(1)} %bitcast.193, bf16[256,2048]{1,0:T(8,128)(2,1)S(1)} %bitcast.187, bf16[256,2048]{1,0:T(8,128)(2,1)} %collective-permute-done.refs_1_, ...), custom_call_target="tpu_custom_call" | custom-call | tf_op jit(solution)/shard_map/norm_both/pallas_call | solution.py:226
  96.7 16.7 %multiply_convert_fusion.1 = (bf16[2048,1024]{1,0:T(8,128)(2,1)}, f32[2048,1024]{1,0:T(8,128)}) fusion(f32[1024]{0:T(1024)S(1)} %bitcast.243, bf16[2048,2048]{1,0:T(8,128)(2,1)} %norm_both.1, bf16[2048,2048]{1,0:T(8,128)(2,1)} %all-gather.4.cloned.1.call-done, s32[]{:T(128)S(6)} %select_n.275), kind=kOutput, calls=%fused_computation.6 | convolution fusion | flops 8610906112 | bytes 25169924 | tf_op jit(solution)/shard_map/dot_general | solution.py:50
  113.4 10.6 %collective-permute-done.8.refs_2_ = bf16[256,2048]{1,0:T(8,128)(2,1)} collective-permute-done((bf16[256,2048]{1,0:T(8,128)(2,1)S(1)}, bf16[256,2048]{1,0:T(8,128)(2,1)}, u32[]{:S(2)}, u32[]{:S(2)}) %collective-permute-start.8) | collective-permute-done | bytes 1048608 | tf_op jit(solution)/shard_map/ppermute | solution.py:468
  140.8 13.1 %convolution_convert_fusion.2 = bf16[1024,2048]{1,0:T(8,128)(2,1)} fusion(bf16[2048,1024]{1,0:T(8,128)(2,1)S(1)} %copy-done.52, bf16[2048,2048]{1,0:T(8,128)(2,1)} %order_both.1), kind=kOutput, calls=%fused_computation.11 | convolution fusion | flops 8592031744 | bytes 16777216 | tf_op jit(solution)/shard_map/dot_general | solution.py:555
  153.9 24.0 %all-gather.6.cloned.1.call-done = bf16[1024,2048]{1,0:T(8,128)(2,1)} async-done(((bf16[256,2048]{1,0:T(8,128)(2,1)}), bf16[1024,2048]{1,0:T(8,128)(2,1)}) %all-gather.6.cloned.1.call-update) | async-done | bytes 4194320 | tf_op jit(solution)/shard_map/all_gather | solution.py:532
  184.5 20.1 %multiply_convert_fusion = bf16[2048,1024]{1,0:T(8,128)(2,1)S(1)} fusion(f32[2048,1024]{1,0:T(8,128)} %get-tuple-element.181, bf16[2048,2048]{1,0:T(8,128)(2,1)} %order_both.1, bf16[1024,2048]{1,0:T(8,128)(2,1)} %all-gather.6.cloned.1.call-done, f32[1024]{0:T(1024)S(1)} %bitcast.244), kind=kOutput, calls=%fused_computation.5 | convolution fusion | flops 8629780480 | bytes 25169920 | tf_op jit(solution)/shard_map/dot_general | solution.py:46
  204.7 21.1 %collective-permute-done.14 = bf16[256,2048]{1,0:T(8,128)(2,1)} collective-permute-done((bf16[256,2048]{1,0:T(8,128)(2,1)S(1)}, bf16[256,2048]{1,0:T(8,128)(2,1)}, u32[]{:S(2)}, u32[]{:S(2)}) %collective-permute-start.14) | collective-permute-done | bytes 1048608 | tf_op jit(solution)/shard_map/ppermute | solution.py:596
  236.3 9.8 %convolution_convert_fusion.3 = bf16[2048,1024]{1,0:T(8,128)(2,1)S(1)} fusion(bf16[2048,2048]{1,0:T(8,128)(2,1)S(1)} %bitcast.210, bf16[2048,1024]{1,0:T(8,128)(2,1)S(1)} %multiply_convert_fusion), kind=kOutput, calls=%fused_computation.12 | convolution fusion | flops 8592031744 | bytes 16777216 | tf_op jit(solution)/shard_map/dot_general | solution.py:555
  246.1 15.5 %convolution_convert_fusion.1 = bf16[2048,2048]{1,0:T(8,128)(2,1)} fusion(bf16[2048,1024]{1,0:T(8,128)(2,1)} %get-tuple-element.76, bf16[1024,2048]{1,0:T(8,128)(2,1)} %all-gather.6.cloned.1.call-done), kind=kOutput, calls=%fused_computation.9 | convolution fusion | flops 8594128896 | bytes 16777216 | tf_op jit(solution)/shard_map/dot_general | solution.py:50
  268.9 11.3 %convolution_convert_fusion = bf16[2048,2048]{1,0:T(8,128)(2,1)} fusion(bf16[2048,1024]{1,0:T(8,128)(2,1)S(1)} %multiply_convert_fusion, bf16[2048,2048]{1,0:T(8,128)(2,1)S(1)} %bitcast.246, s32[]{:T(128)S(6)} %select_n.275), kind=kOutput, calls=%fused_computation.8 | convolution fusion | flops 8594128896 | bytes 16777220 | tf_op jit(solution)/shard_map/dot_general | solution.py:46
  280.3 32.8 %all-gather.8.cloned.1.call-done = bf16[2048,1024]{1,0:T(8,128)(2,1)} async-done(((bf16[512,1024]{1,0:T(8,128)(2,1)}), bf16[2048,1024]{1,0:T(8,128)(2,1)}) %all-gather.8.cloned.1.call-update) | async-done | bytes 4194320 | tf_op jit(solution)/shard_map/all_gather | solution.py:544
  339.3 9.1 %broadcast_add_fusion.mixed_ref = f32[2048,768]{1,0:T(8,128)S(1)} fusion(f32[768]{0:T(1024)S(1)} %fusion.56, bf16[2048,2048]{1,0:T(8,128)(2,1)} %norm_both.1, bf16[2048,1024]{1,0:T(8,128)(2,1)S(1)} %copy-done.34), kind=kOutput, calls=%fused_computation.17 | convolution fusion | flops 6444023808 | bytes 17829888 | tf_op jit(solution)/shard_map/dot_general | solution.py:50
  348.5 15.4 %attend.1 = (bf16[2048,768]{1,0:T(8,128)(2,1)S(1)}, bf16[2048,256]{1,0:T(8,128)(2,1)S(1)}, f32[2,2,2,1024]{3,2,1,0:T(2,128)S(1)}) custom-call(f32[2048,768]{1,0:T(8,128)S(1)} %broadcast_add_fusion.mixed_ref, f32[1024,128]{1,0:T(8,128)S(1)} %copy-done.8, f32[1024,128]{1,0:T(8,128)S(1)} %copy-done.6, f32[1024,128]{1,0:T(8,128)S(1)} %copy-done.4), custom_call_target="tpu_custom_call" | custom-call | flops 2147483648 | bytes 12582912 | tf_op jit(solution)/shard_map/attend/pallas_call | solution.py:150
  401.5 20.2 %attend_back.1 = bf16[2048,768]{1,0:T(8,128)(2,1)S(1)} custom-call(bf16[2048,768]{1,0:T(8,128)(2,1)S(1)} %copy-done.11, bf16[2048,256]{1,0:T(8,128)(2,1)S(1)} %copy-done.12, f32[2,2,2,1024]{3,2,1,0:T(2,128)S(1)} %get-tuple-element.89.logsum_ref, f32[1024,128]{1,0:T(8,128)S(1)} %copy-done.9, f32[1024,128]{1,0:T(8,128)S(1)} %copy-done.7, f32[1024,128]{1,0:T(8,128)S(1)} %copy-done.5), custom_call_target="tpu_custom_call" | custom-call | flops 5368709120 | bytes 9437184 | tf_op jit(solution)/shard_map/attend_back/pallas_call | solution.py:180
  465.4 13.2 %collective-permute-done.33 = bf16[64,2048]{1,0:T(8,128)(2,1)S(1)} collective-permute-done((bf16[64,2048]{1,0:T(8,128)(2,1)S(1)}, bf16[64,2048]{1,0:T(8,128)(2,1)S(1)}, u32[]{:S(2)}, u32[]{:S(2)}) %collective-permute-start.33) | collective-permute-done | bytes 262176 | tf_op jit(solution)/shard_map/ppermute | solution.py:596
  501.6 9.0 %collective-permute-done.40 = bf16[64,2048]{1,0:T(8,128)(2,1)S(1)} collective-permute-done((bf16[64,2048]{1,0:T(8,128)(2,1)S(1)}, bf16[64,2048]{1,0:T(8,128)(2,1)S(1)}, u32[]{:S(2)}, u32[]{:S(2)}) %collective-permute-start.40) | collective-permute-done | bytes 262176 | tf_op jit(solution)/shard_map/ppermute | solution.py:596
  557.5 27.5 %collective-permute-done.43 = bf16[256,2048]{1,0:T(8,128)(2,1)S(1)} collective-permute-done((bf16[256,2048]{1,0:T(8,128)(2,1)}, bf16[256,2048]{1,0:T(8,128)(2,1)S(1)}, u32[]{:S(2)}, u32[]{:S(2)}) %collective-permute-start.43) | collective-permute-done | bytes 1048608 | tf_op jit(solution)/shard_map/ppermute | solution.py:468
  592.2 15.2 %collective-permute-done.36 = bf16[256,2048]{1,0:T(8,128)(2,1)S(1)} collective-permute-done((bf16[256,2048]{1,0:T(8,128)(2,1)}, bf16[256,2048]{1,0:T(8,128)(2,1)S(1)}, u32[]{:S(2)}, u32[]{:S(2)}) %collective-permute-start.36) | collective-permute-done | bytes 1048608 | tf_op jit(solution)/shard_map/ppermute | solution.py:468
  609.0 11.4 %collective-permute-done.35 = bf16[256,2048]{1,0:T(8,128)(2,1)S(1)} collective-permute-done((bf16[256,2048]{1,0:T(8,128)(2,1)}, bf16[256,2048]{1,0:T(8,128)(2,1)S(1)}, u32[]{:S(2)}, u32[]{:S(2)}) %collective-permute-start.35) | collective-permute-done | bytes 1048608 | tf_op jit(solution)/shard_map/ppermute | solution.py:468
  657.7 14.4 %collective-permute-done.53 = bf16[64,2048]{1,0:T(8,128)(2,1)} collective-permute-done((bf16[64,2048]{1,0:T(8,128)(2,1)}, bf16[64,2048]{1,0:T(8,128)(2,1)}, u32[]{:S(2)}, u32[]{:S(2)}) %collective-permute-start.53) | collective-permute-done | bytes 262176 | tf_op jit(solution)/shard_map/ppermute | solution.py:468
  673.6 10.4 %collective-permute-done.54 = bf16[64,2048]{1,0:T(8,128)(2,1)S(1)} collective-permute-done((bf16[64,2048]{1,0:T(8,128)(2,1)}, bf16[64,2048]{1,0:T(8,128)(2,1)S(1)}, u32[]{:S(2)}, u32[]{:S(2)}) %collective-permute-start.54) | collective-permute-done | bytes 262176 | tf_op jit(solution)/shard_map/ppermute | solution.py:468
  700.8 11.8 %collective-permute-done.48.refs_2_ = bf16[2,256,768]{2,1,0:T(8,128)(2,1)} collective-permute-done((bf16[2,256,768]{2,1,0:T(8,128)(2,1)S(1)}, bf16[2,256,768]{2,1,0:T(8,128)(2,1)}, u32[]{:S(2)}, u32[]{:S(2)}) %collective-permute-start.48) | collective-permute-done | bytes 786464 | tf_op jit(solution)/shard_map/ppermute | solution.py:468
  (389 shorter events, 337.9 us)
Async XLA Ops:
  7.3 89.4 %all-gather.4.cloned.1.call-start = ((), (), s32[]{:S(2)}) async-start(), calls=%async_computation.2 | async-start | bytes 9437184 | tf_op jit(solution)/shard_map/all_gather | solution.py:517
  21.3 156.6 %all-gather.6.cloned.1.call-start = ((), (), s32[]{:S(2)}) async-start(), calls=%async_computation.3 | async-start | bytes 5242880 | tf_op jit(solution)/shard_map/all_gather | solution.py:532
  48.0 265.2 %all-gather.8.cloned.1.call-start = ((), (), s32[]{:S(2)}) async-start(), calls=%async_computation.4 | async-start | bytes 5242880 | tf_op jit(solution)/shard_map/all_gather | solution.py:544
  74.7 58.1 %collective-permute-start.10 = (bf16[256,2048]{1,0:T(8,128)(2,1)S(1)}, bf16[256,2048]{1,0:T(8,128)(2,1)S(1)}, u32[]{:S(2)}, u32[]{:S(2)}) collective-permute-start(bf16[256,2048]{1,0:T(8,128)(2,1)S(1)} %bitcast.188), channel_id=1, source_target_pairs={{0,1},{1,0},{2,3},{3,2},{4,5},{5,4},{6,7},{7,6},{8,9},{9,8},{10,11... | collective-permute-start | bytes 3145736 | tf_op jit(solution)/shard_map/ppermute | solution.py:465
  229.5 86.0 %collective-permute-start.17 = (bf16[256,2048]{1,0:T(8,128)(2,1)}, bf16[256,2048]{1,0:T(8,128)(2,1)}, u32[]{:S(2)}, u32[]{:S(2)}) collective-permute-start(bf16[256,2048]{1,0:T(8,128)(2,1)} %get-tuple-element.142), channel_id=1, source_target_pairs={{6,4},{4,2},{7,5},{5,3},{14,12},{12,10},{15,13},{13,11},{22,20},{2... | collective-permute-start | bytes 3145736 | tf_op jit(solution)/shard_map/ppermute | solution.py:596
  231.1 84.4 %collective-permute-start.16 = (bf16[256,2048]{1,0:T(8,128)(2,1)}, bf16[256,2048]{1,0:T(8,128)(2,1)}, u32[]{:S(2)}, u32[]{:S(2)}) collective-permute-start(bf16[256,2048]{1,0:T(8,128)(2,1)} %get-tuple-element.143), channel_id=1, source_target_pairs={{0,2},{2,4},{1,3},{3,5},{8,10},{10,12},{9,11},{11,13},{16,18},{18,... | collective-permute-start | bytes 3145736 | tf_op jit(solution)/shard_map/ppermute | solution.py:596
  262.7 65.0 %collective-permute-start.20 = (bf16[512,1024]{1,0:T(8,128)(2,1)}, bf16[512,1024]{1,0:T(8,128)(2,1)}, u32[]{:S(2)}, u32[]{:S(2)}) collective-permute-start(bf16[512,1024]{1,0:T(8,128)(2,1)} %get-tuple-element.138), channel_id=1, source_target_pairs={{6,4},{7,5},{14,12},{15,13},{22,20},{23,21},{30,28},{31,29}} | collective-permute-start | bytes 3145736 | tf_op jit(solution)/shard_map/ppermute | solution.py:596
  264.3 63.4 %collective-permute-start.19 = (bf16[512,1024]{1,0:T(8,128)(2,1)S(1)}, bf16[512,1024]{1,0:T(8,128)(2,1)}, u32[]{:S(2)}, u32[]{:S(2)}) collective-permute-start(bf16[512,1024]{1,0:T(8,128)(2,1)S(1)} %get-tuple-element.139), channel_id=1, source_target_pairs={{0,2},{1,3},{8,10},{9,11},{16,18},{17,19},{24,26},{25,27}} | collective-permute-start | bytes 3145736 | tf_op jit(solution)/shard_map/ppermute | solution.py:596
  331.7 57.4 %collective-permute-start.25 = (bf16[512,1024]{1,0:T(8,128)(2,1)}, bf16[512,1024]{1,0:T(8,128)(2,1)}, u32[]{:S(2)}, u32[]{:S(2)}) collective-permute-start(bf16[512,1024]{1,0:T(8,128)(2,1)} %get-tuple-element.136), channel_id=1, source_target_pairs={{6,4},{4,2},{7,5},{5,3},{14,12},{12,10},{15,13},{13,11},{22,20},{2... | collective-permute-start | bytes 3145736 | tf_op jit(solution)/shard_map/ppermute | solution.py:596
  333.3 56.3 %collective-permute-start.24 = (bf16[512,1024]{1,0:T(8,128)(2,1)}, bf16[512,1024]{1,0:T(8,128)(2,1)}, u32[]{:S(2)}, u32[]{:S(2)}) collective-permute-start(bf16[512,1024]{1,0:T(8,128)(2,1)} %get-tuple-element.137), channel_id=1, source_target_pairs={{0,2},{2,4},{1,3},{3,5},{8,10},{10,12},{9,11},{11,13},{16,18},{18,... | collective-permute-start | bytes 3145736 | tf_op jit(solution)/shard_map/ppermute | solution.py:596
  386.1 61.3 %collective-permute-start.59 = (bf16[256,2048]{1,0:T(8,128)(2,1)}, bf16[256,2048]{1,0:T(8,128)(2,1)}, u32[]{:S(2)}, u32[]{:S(2)}) collective-permute-start(bf16[256,2048]{1,0:T(8,128)(2,1)} %get-tuple-element.122), channel_id=1, source_target_pairs={{0,16},{8,24},{16,0},{24,8},{1,17},{9,25},{17,1},{25,9},{2,18},{10... | collective-permute-start | bytes 3145736 | tf_op jit(solution)/shard_map/ppermute | solution.py:468
  387.7 61.0 %collective-permute-start.58 = (bf16[256,2048]{1,0:T(8,128)(2,1)}, bf16[256,2048]{1,0:T(8,128)(2,1)}, u32[]{:S(2)}, u32[]{:S(2)}) collective-permute-start(bf16[256,2048]{1,0:T(8,128)(2,1)} %get-tuple-element.122), channel_id=1, source_target_pairs={{0,8},{8,0},{16,24},{24,16},{1,9},{9,1},{17,25},{25,17},{2,10},{10... | collective-permute-start | bytes 3145736 | tf_op jit(solution)/shard_map/ppermute | solution.py:468
  389.1 61.2 %collective-permute-start.60 = (bf16[256,2048]{1,0:T(8,128)(2,1)}, bf16[256,2048]{1,0:T(8,128)(2,1)}, u32[]{:S(2)}, u32[]{:S(2)}) collective-permute-start(bf16[256,2048]{1,0:T(8,128)(2,1)} %get-tuple-element.122), channel_id=1, source_target_pairs={{0,24},{8,16},{16,8},{24,0},{1,25},{9,17},{17,9},{25,1},{2,26},{10... | collective-permute-start | bytes 3145736 | tf_op jit(solution)/shard_map/ppermute | solution.py:468
  394.2 66.7 %collective-permute-start.29 = (bf16[512,1024]{1,0:T(8,128)(2,1)}, bf16[512,1024]{1,0:T(8,128)(2,1)}, u32[]{:S(2)}, u32[]{:S(2)}) collective-permute-start(bf16[512,1024]{1,0:T(8,128)(2,1)} %get-tuple-element.134), channel_id=1, source_target_pairs={{6,4},{4,2},{2,0},{7,5},{5,3},{3,1},{14,12},{12,10},{10,8},{15,13}... | collective-permute-start | bytes 3145736 | tf_op jit(solution)/shard_map/ppermute | solution.py:596
  447.4 51.2 %collective-permute-start.27 = (bf16[1024,2048]{1,0:T(8,128)(2,1)}, bf16[1024,2048]{1,0:T(8,128)(2,1)S(1)}, u32[]{:S(2)}, u32[]{:S(2)}) collective-permute-start(bf16[1024,2048]{1,0:T(8,128)(2,1)} %add_convert_fusion.1), channel_id=1, source_target_pairs={{0,1},{1,0},{2,3},{3,2},{4,5},{5,4},{6,7},{7,6},{8,9},{9,8},{10,11... | collective-permute-start | bytes 12582920 | tf_op jit(solution)/shard_map/ppermute | solution.py:465
  534.5 53.0 %collective-permute-start.37 = (bf16[256,2048]{1,0:T(8,128)(2,1)}, bf16[256,2048]{1,0:T(8,128)(2,1)S(1)}, u32[]{:S(2)}, u32[]{:S(2)}) collective-permute-start(bf16[256,2048]{1,0:T(8,128)(2,1)} %get-tuple-element.129), channel_id=1, source_target_pairs={{0,8},{8,0},{16,24},{24,16},{1,9},{9,1},{17,25},{25,17},{2,10},{10... | collective-permute-start | bytes 3145736 | tf_op jit(solution)/shard_map/ppermute | solution.py:468
  541.6 78.9 %collective-permute-start.35 = (bf16[256,2048]{1,0:T(8,128)(2,1)}, bf16[256,2048]{1,0:T(8,128)(2,1)S(1)}, u32[]{:S(2)}, u32[]{:S(2)}) collective-permute-start(bf16[256,2048]{1,0:T(8,128)(2,1)} %get-tuple-element.130), channel_id=1, source_target_pairs={{0,16},{8,24},{16,0},{24,8},{1,17},{9,25},{17,1},{25,9},{2,18},{10... | collective-permute-start | bytes 3145736 | tf_op jit(solution)/shard_map/ppermute | solution.py:468
  543.1 64.2 %collective-permute-start.36 = (bf16[256,2048]{1,0:T(8,128)(2,1)}, bf16[256,2048]{1,0:T(8,128)(2,1)S(1)}, u32[]{:S(2)}, u32[]{:S(2)}) collective-permute-start(bf16[256,2048]{1,0:T(8,128)(2,1)} %get-tuple-element.131), channel_id=1, source_target_pairs={{0,24},{8,16},{16,8},{24,0},{1,25},{9,17},{17,9},{25,1},{2,26},{10... | collective-permute-start | bytes 3145736 | tf_op jit(solution)/shard_map/ppermute | solution.py:468
  553.2 76.7 %collective-permute-start.26 = (bf16[256,2048]{1,0:T(8,128)(2,1)}, bf16[256,2048]{1,0:T(8,128)(2,1)S(1)}, u32[]{:S(2)}, u32[]{:S(2)}) collective-permute-start(bf16[256,2048]{1,0:T(8,128)(2,1)} %get-tuple-element.132), channel_id=1, source_target_pairs={{0,8},{8,0},{16,24},{24,16},{1,9},{9,1},{17,25},{25,17},{2,10},{10... | collective-permute-start | bytes 3145736 | tf_op jit(solution)/shard_map/ppermute | solution.py:468
  584.9 69.4 %collective-permute-start.57 = (bf16[2,256,1024]{2,1,0:T(8,128)(2,1)S(1)}, bf16[2,256,1024]{2,1,0:T(8,128)(2,1)}, u32[]{:S(2)}, u32[]{:S(2)}) collective-permute-start(bf16[2,256,1024]{2,1,0:T(8,128)(2,1)S(1)} %copy-done.24), channel_id=1, source_target_pairs={{0,24},{8,16},{16,8},{24,0},{1,25},{9,17},{17,9},{25,1},{2,26},{10... | collective-permute-start | bytes 3145736 | tf_op jit(solution)/shard_map/ppermute | solution.py:468
  587.5 100.7 %collective-permute-start.56 = (bf16[2,256,1024]{2,1,0:T(8,128)(2,1)S(1)}, bf16[2,256,1024]{2,1,0:T(8,128)(2,1)}, u32[]{:S(2)}, u32[]{:S(2)}) collective-permute-start(bf16[2,256,1024]{2,1,0:T(8,128)(2,1)S(1)} %copy-done.24), channel_id=1, source_target_pairs={{0,16},{8,24},{16,0},{24,8},{1,17},{9,25},{17,1},{25,9},{2,18},{10... | collective-permute-start | bytes 3145736 | tf_op jit(solution)/shard_map/ppermute | solution.py:468
  607.4 80.9 %collective-permute-start.55 = (bf16[2,256,1024]{2,1,0:T(8,128)(2,1)S(1)}, bf16[2,256,1024]{2,1,0:T(8,128)(2,1)}, u32[]{:S(2)}, u32[]{:S(2)}) collective-permute-start(bf16[2,256,1024]{2,1,0:T(8,128)(2,1)S(1)} %copy-done.24), channel_id=1, source_target_pairs={{0,8},{8,0},{16,24},{24,16},{1,9},{9,1},{17,25},{25,17},{2,10},{10... | collective-permute-start | bytes 3145736 | tf_op jit(solution)/shard_map/ppermute | solution.py:468
  620.5 51.6 %collective-permute-start.53 = (bf16[64,2048]{1,0:T(8,128)(2,1)}, bf16[64,2048]{1,0:T(8,128)(2,1)}, u32[]{:S(2)}, u32[]{:S(2)}) collective-permute-start(bf16[64,2048]{1,0:T(8,128)(2,1)} %get-tuple-element.124), channel_id=1, source_target_pairs={{0,16},{8,24},{16,0},{24,8},{1,17},{9,25},{17,1},{25,9},{2,18},{10... | collective-permute-start | bytes 786440 | tf_op jit(solution)/shard_map/ppermute | solution.py:468
  639.1 55.1 %all-to-all-start.1 = ((f32[32,1,2560]{2,1,0:T(1,128)}), f32[32,1,2560]{2,1,0:T(1,128)S(1)}, u32[]{:S(2)}, u32[]{:S(2)}) async-start(f32[32,1,2560]{2,1,0:T(1,128)} %all_to_all.14), calls=%async_computation.1 | async-start | bytes 655360 | tf_op jit(solution)/shard_map/all_to_all | solution.py:768
  (107 other events, 2887.7 us)
Sparse Core Ops, SparseCore 0:
  11.6 84.9 all-gather.3
  98.8 79.0 all-gather.5
  180.0 133.0 all-gather.7

commit v2 on v1

--- a/solution.py
+++ b/solution.py
@@ -205,12 +205,11 @@
     )(heads, grad, logsums, *tables)
 
 
-def norm_kernel(place_ref, gain_ref, bias_ref, *refs):
+def norm_kernel(places_ref, gain_ref, bias_ref, *refs):
     *pieces, out_ref = refs
-    half = len(pieces) // 2
     for i, piece in enumerate(pieces):
 
-        @pl.when(pl.program_id(0) == i // half * half + ((i % half) ^ place_ref[0]))
+        @pl.when(pl.program_id(0) == i)
         def _(piece=piece):
             x = piece[...].astype(f32)
             centred = x - jnp.mean(x, axis=-1, keepdims=True)
@@ -220,53 +219,31 @@
             ).astype(bf16)
 
 
-def norm_both(place, pieces, gain, bias):
+def order_kernel(places_ref, *refs):
+    *pieces, out_ref = refs
+    for i, piece in enumerate(pieces):
+
+        @pl.when(pl.program_id(0) == i)
+        def _(piece=piece):
+            out_ref[...] = piece[...].astype(out_ref.dtype)
+
+
+def order_pieces(kernel, name, places, pieces, vectors=(), dtype=bf16):
     local, d = pieces[0].shape
-    fixed = lambda i, place: (0, 0)
+    fixed = lambda i, places: (0, 0)
     return pl.pallas_call(
-        norm_kernel,
+        kernel,
         grid_spec=pltpu.PrefetchScalarGridSpec(
             num_scalar_prefetch=1,
             grid=(len(pieces),),
-            in_specs=[pl.BlockSpec((1, d), fixed)] * 2 + [pl.BlockSpec((local, d), fixed)] * len(pieces),
-            out_specs=pl.BlockSpec((local, d), lambda i, place: (i, 0)),
+            in_specs=[pl.BlockSpec((1, d), fixed)] * len(vectors)
+            + [pl.BlockSpec((local, d), fixed)] * len(pieces),
+            out_specs=pl.BlockSpec((local, d), lambda i, places: (places[i], 0)),
         ),
-        out_shape=jax.ShapeDtypeStruct((len(pieces) * local, d), bf16),
+        out_shape=jax.ShapeDtypeStruct((len(pieces) * local, d), dtype),
         compiler_params=pltpu.CompilerParams(vmem_limit_bytes=48 * 1024 * 1024),
-        name="norm_both",
-    )(place, gain[None], bias[None], *pieces)
-
-
-def order_kernel(place_ref, *refs):
-    *pieces, out_ref = refs
-    for i, piece in enumerate(pieces):
-
-        @pl.when(pl.program_id(0) == i)
-        def _(piece=piece):
-            out_ref[...] = piece[...]
-
-
-def order_both(place, pieces):
-    local, d = pieces[0].shape
-    half = len(pieces) // 2
-    return pl.pallas_call(
-        order_kernel,
-        grid_spec=pltpu.PrefetchScalarGridSpec(
-            num_scalar_prefetch=1,
-            grid=(len(pieces),),
-            in_specs=[pl.BlockSpec((local, d), lambda i, place: (0, 0))] * len(pieces),
-            out_specs=pl.BlockSpec(
-                (local, d),
-                lambda i, place: (
-                    jnp.where(i < half, i ^ place[0], half + ((i - half) ^ place[0])),
-                    0,
-                ),
-            ),
-        ),
-        out_shape=jax.ShapeDtypeStruct((len(pieces) * local, d), pieces[0].dtype),
-        compiler_params=pltpu.CompilerParams(vmem_limit_bytes=48 * 1024 * 1024),
-        name="order_both",
-    )(place, *pieces)
+        name=name,
+    )(places, *[v[None] for v in vectors], *pieces)
 
 
 def row_blocks(rows):
@@ -298,18 +275,18 @@
     )(place, weight)
 
 
-def place_units_kernel(nz, w, place_ref, *refs):
+def place_units_kernel(nz, w, places_ref, *refs):
     *pieces, out_ref = refs
     ns = len(pieces)
-    for d, piece in enumerate(pieces):
-        device = place_ref[0] ^ d
+    for i, piece in enumerate(pieces):
+        device = places_ref[i]
         for q in range(nz):
             for c in range(CORES):
                 to = pl.multiple_of(((q * CORES + c) * ns + device) * w, w)
                 out_ref[:, pl.ds(to, w)] = piece[c, :, q * w : (q + 1) * w].astype(f32)
 
 
-def place_units(place, pieces, nz, w):
+def place_units(places, pieces, nz, w):
     cores, rows, width = pieces[0].shape
     block = row_blocks(rows)
     ff = width * cores * len(pieces)
@@ -318,12 +295,12 @@
         grid_spec=pltpu.PrefetchScalarGridSpec(
             num_scalar_prefetch=1,
             grid=(rows // block,),
-            in_specs=[pl.BlockSpec((cores, block, width), lambda i, place: (0, i, 0)) for _ in pieces],
-            out_specs=pl.BlockSpec((block, ff), lambda i, place: (i, 0)),
+            in_specs=[pl.BlockSpec((cores, block, width), lambda i, places: (0, i, 0)) for _ in pieces],
+            out_specs=pl.BlockSpec((block, ff), lambda i, places: (i, 0)),
         ),
         out_shape=jax.ShapeDtypeStruct((rows, ff), f32),
         name="place_units",
-    )(place, *pieces)
+    )(places, *pieces)
 
 
 def low_half():
@@ -374,25 +351,33 @@
     )(place, weight)
 
 
-def place_heads_kernel(nz, place_ref, *refs):
+def place_heads_kernel(nz, places_ref, *refs):
     *pieces, out_ref = refs
-    tiles = len(pieces) // 2
-    even = lax.rem(place_ref[0], 2) == 0
-    for d in range(0, len(pieces), 2):
-        tile = lax.div(place_ref[0] ^ d, 2)
+    ns = len(pieces)
+    tiles = ns // 2
+    even = lax.rem(places_ref[0], 2) == 0
+    straight = (places_ref[0] ^ places_ref[1]) == 1
+    for a in range(0, ns, 2):
+        mates = [(a, a + 1)] if ns != 4 else [((0, 1), (0, 2)), ((2, 3), (1, 3))][a // 2]
+        tile = lax.div(places_ref[mates[0][0]] if ns == 4 else places_ref[a], 2)
+        if ns == 4:
+            tile = jnp.where(straight, tile, lax.div(places_ref[mates[1][0]], 2))
         for j in range(3):
             for p in range(nz // 2):
                 at = (p * 3 + j) * PAIR
                 for c in range(CORES):
-                    one = pieces[d][c, :, at : at + PAIR].astype(f32)
-                    two = pieces[d + 1][c, :, at : at + PAIR].astype(f32)
+                    loaded = [[pieces[i][c, :, at : at + PAIR].astype(f32) for i in pair] for pair in mates]
+                    one, two = loaded[0]
+                    if ns == 4:
+                        one = jnp.where(straight, one, loaded[1][0])
+                        two = jnp.where(straight, two, loaded[1][1])
                     first, second = jnp.where(even, one, two), jnp.where(even, two, one)
                     for q, value in ((2 * p, lows(first, second)), (2 * p + 1, highs(first, second))):
                         to = (((j * nz + q) * CORES + c) * tiles + tile) * PAIR
                         out_ref[:, pl.ds(pl.multiple_of(to, PAIR), PAIR)] = value
 
 
-def place_heads(place, pieces, nz):
+def place_heads(places, pieces, nz):
     cores, rows, width = pieces[0].shape
     block = row_blocks(rows)
     whole = width * cores * len(pieces)
@@ -401,12 +386,12 @@
         grid_spec=pltpu.PrefetchScalarGridSpec(
             num_scalar_prefetch=1,
             grid=(rows // block,),
-            in_specs=[pl.BlockSpec((cores, block, width), lambda i, place: (0, i, 0)) for _ in pieces],
-            out_specs=pl.BlockSpec((block, whole), lambda i, place: (i, 0)),
+            in_specs=[pl.BlockSpec((cores, block, width), lambda i, places: (0, i, 0)) for _ in pieces],
+            out_specs=pl.BlockSpec((block, whole), lambda i, places: (i, 0)),
         ),
         out_shape=jax.ShapeDtypeStruct((rows, whole), f32),
         name="place_heads",
-    )(place, *pieces)
+    )(places, *pieces)
 
 
 def gelu_and_slope(u):
@@ -464,17 +449,36 @@
     def other_core(x):
         return lax.ppermute(x, "fsdp", swap)
 
+    two_steps = ns == 4
+
     def plane_send(x, d):
         return lax.ppermute(x, "seq", [(i, i ^ d) for i in range(ns)])
 
-    def plane_pieces(x):
-        return [x] + [plane_send(x, d) for d in range(1, ns)]
+    def plane_hop(x, second):
+        hops = []
+        for i in range(ns):
+            for g in range(nf):
+                hops.append((i * nf + g, (i ^ (1 + (g % CORES ^ second))) * nf + g))
+        return lax.ppermute(x, everyone, hops)
+
+    first_hop, second_hop = 1 + k, 2 - k
+    steps = [0, first_hop, second_hop, 3] if two_steps else list(range(ns))
+    other_steps = [0, second_hop, first_hop, 3] if two_steps else steps
+    places = jnp.stack([s ^ step for step in steps]).astype(jnp.int32)
+    other_places = jnp.stack([s ^ step for step in other_steps]).astype(jnp.int32)
+    both_places = jnp.concatenate([places, ns + other_places])
+
+    def plane_pieces(x, *passed):
+        if not two_steps:
+            return [x] + [plane_send(x, d) for d in range(1, ns)]
+        near, far = plane_hop(x, 0), plane_hop(x, 1)
+        return [x, near, far, plane_hop(after(near, *passed), 1)]
 
     def arrange(pieces, dtype):
         size = pieces[0].shape[0]
         whole = jnp.zeros((ns * size,) + pieces[0].shape[1:], dtype)
-        for d, piece in enumerate(pieces):
-            whole = lax.dynamic_update_slice_in_dim(whole, piece.astype(dtype), (s ^ d) * size, 0)
+        for at, piece in zip(steps, pieces):
+            whole = lax.dynamic_update_slice_in_dim(whole, piece.astype(dtype), (s ^ at) * size, 0)
         return whole
 
     def pick(x, index, axis):
@@ -528,10 +532,10 @@
     c_pieces = plane_pieces(after(cotangent[0], *x_pieces[1:]))
     x_pieces = x_pieces + [other_core(piece) for piece in x_pieces]
 
+    normed = order_pieces(norm_kernel, "norm_both", both_places, x_pieces, (gain, nbias))
+
     down_part = after(down_part, x_pieces[ns - 1])
     down_mine = lax.all_gather(down_part, "fsdp", axis=0, tiled=True, axis_index_groups=lines)
-
-    normed = norm_both(place, x_pieces, gain, nbias)
 
     qkv_part = after(qkv_part, normed)
     if one_each:
@@ -600,101 +604,102 @@
         got = other_core(lax.dynamic_slice_in_dim(x, (1 - k) * rows, rows, 0))
         return jnp.stack([jnp.where(k == 0, keep, got), jnp.where(k == 0, got, keep)])
 
+    def halves(left, right, dot, more=None):
+        far = dot(left[length:], right)
+        near = dot(left[:length], right)
+        if more is not None:
+            far, near = far + more[0].astype(f32), near + more[1].astype(f32)
+        return far.astype(bf16), near.astype(bf16)
+
+    def rank_parts(near, got):
+        parts = []
+        for step in steps:
+            at = (s ^ step) * local
+            part = lax.dynamic_slice_in_dim(near, at, local, 0).astype(f32)
+            parts.append(part + lax.dynamic_slice_in_dim(got, at, local, 0).astype(f32))
+        return parts[:1] + [part.astype(bf16) for part in parts[1:]]
+
+    def rank_sum(parts, *passed):
+        if not two_steps:
+            total = parts[0]
+            for d in range(1, ns):
+                total = total + plane_send(parts[d], d).astype(f32)
+            return total
+        across = plane_hop(parts[3], 0)
+        beside = plane_hop(parts[1], 0)
+        across = after(across, *passed)
+        rest = plane_hop((parts[2].astype(f32) + across.astype(f32)).astype(bf16), 1)
+        return parts[0] + beside.astype(f32) + rest.astype(f32)
+
     hidden = plain_dot(normed, up_mine) + upb_mine
     activated, slope = gelu_and_slope(hidden)
     activated = activated.astype(bf16)
     c_pieces = c_pieces[:1] + [after(piece, activated) for piece in c_pieces[1:]]
-    c2 = order_both(place, c_pieces + [other_core(piece) for piece in c_pieces])
+    c2 = order_pieces(order_kernel, "order_both", both_places, c_pieces + [other_core(piece) for piece in c_pieces])
     down_local = first_first(activated, c2).astype(bf16)
     down_walk = Walk(down_local)
     down_walk.step()
+
+    def line_sum(x):
+        return lax.psum_scatter(
+            x, "fsdp", scatter_dimension=0, tiled=True, axis_index_groups=lines
+        )
+
     c2, down_mine = after(c2, down_local), after(down_mine, down_local)
     hidden_grad = (last_last(c2, down_mine) * slope).astype(bf16)
-    hidden_grad = after(hidden_grad, *down_walk.step())
     up_local = first_first(normed, hidden_grad).astype(bf16)
-    up_walk = Walk(up_local)
-    up_walk.step()
-    activated = after(activated, up_local)
-    ff_branch = plain_dot(activated, down_mine).astype(bf16)
-    hidden_grad = after(hidden_grad, ff_branch)
-    ff_back = last_last(hidden_grad, up_mine).astype(bf16)
+    up_own = line_sum(up_local)
+    activated = after(activated, up_local, *down_walk.step(after=up_local))
+    branch_more = halves(activated, down_mine, plain_dot)
+    hidden_grad = after(hidden_grad, *branch_more)
+    back_more = halves(hidden_grad, up_mine, last_last)
 
     if one_each:
-        both = after(both, ff_back)
+        both = after(both, *back_more)
         qkv_mine = both[:, : 3 * rank_cols]
         out_mine = both[:, 3 * rank_cols :].reshape(nz, -1, hw, wide).transpose(0, 2, 1, 3)
         out_mine = out_mine.reshape(rank_cols, d)
-    normed = after(normed, ff_back, *down_walk.rest())
+    normed = after(normed, *down_walk.rest(after=back_more[0]))
     mixed = plain_dot(normed, qkv_mine) + qkvb_mine
-    mixed = after(mixed, *up_walk.step())
     heads, attended, logsums = attend(mixed, tables, length)
-    down_own = down_walk.own()
-    down_pieces = plane_pieces(down_own)
-    attended = after(attended, down_own)
-    out_local = first_first(attended, c2).astype(bf16)
-    if spread:
-        out_walk = Walk(out_local)
-        out_walk.step()
-    c2 = after(c2, out_local)
+    c2 = after(c2, attended)
     attended_grad = last_last(c2, out_mine).astype(bf16)
     attended = after(attended, attended_grad)
-
-    def both_halves(left, right, dot, more):
-        far = (dot(left[length:], right) + more[length:].astype(f32)).astype(bf16)
-        got = other_core(far)
-        near = (dot(after(left, far)[:length], right) + more[:length].astype(f32)).astype(bf16)
-        return near, got
-
-    def rank_parts(near, got):
-        parts = []
-        for d in range(ns):
-            at = (s ^ d) * local
-            part = lax.dynamic_slice_in_dim(near, at, local, 0).astype(f32)
-            part = part + lax.dynamic_slice_in_dim(got, at, local, 0).astype(f32)
-            parts.append(part if d == 0 else part.astype(bf16))
-        return parts
-
-    def rank_sum(parts, *passed):
-        total = parts[0]
-        for d in range(1, ns):
-            total = total + after(plane_send(parts[d], d), *passed).astype(f32)
-        return total
-
-    near, got = both_halves(attended, out_mine, plain_dot, ff_branch)
-    attended_grad = after(attended_grad, near, *up_walk.rest())
+    branch_far, branch_near = halves(attended, out_mine, plain_dot, branch_more)
+    branch_got = other_core(branch_far)
+    attended = after(attended, branch_near)
+    out_local = first_first(attended, c2).astype(bf16)
+    branch_parts = rank_parts(branch_near, after(branch_got, out_local))
+    attended_grad = after(attended_grad, *branch_parts)
     mixed_grad = attend_back(heads, attended_grad, logsums, tables, length)
     normed = after(normed, mixed_grad)
     qkv_local = first_first(normed, mixed_grad).astype(bf16)
-    if spread:
-        qkv_walk = Walk(qkv_local)
-        qkv_walk.step()
-    branch_parts = rank_parts(near, after(got, qkv_local))
-    mixed_grad = after(mixed_grad, *branch_parts)
-    near, got = both_halves(mixed_grad, qkv_mine, last_last, ff_back)
-    up_walk.got = [after(g, near) for g in up_walk.got]
-    up_own = up_walk.own()
-    up_both = both_cores(up_own)
-    passed = [up_both]
-    if spread:
-        passed += qkv_walk.step(after=up_own)
-        passed += out_walk.step(after=up_own)
-    up_pieces = plane_pieces(up_both)
-    grad_parts = rank_parts(near, after(got, *passed))
-    branches = rank_sum(branch_parts, *grad_parts)
-    if spread:
-        passed = qkv_walk.rest(after=grad_parts[1]) + out_walk.rest(after=grad_parts[1])
-    normed_grad = rank_sum(grad_parts, *passed)
-    if spread:
-        qkv_own, out_own = qkv_walk.own(), out_walk.own()
-        out_pieces = plane_pieces(out_own)
+    if one_each:
+        beside = out_local.reshape(nz, hw, -1, wide).transpose(0, 2, 1, 3).reshape(d, wide)
+        beside = jnp.concatenate([qkv_local, beside], axis=1)
+        own = line_sum(after(beside, up_own))
+        qkv_own = own[:, : 3 * rank_cols]
+        out_own = own[:, 3 * rank_cols :].reshape(-1, hw, wide).transpose(1, 0, 2).reshape(hw, d)
     else:
-        qkv_own = lax.psum_scatter(
-            qkv_local, "fsdp", scatter_dimension=0, tiled=True, axis_index_groups=lines
-        )
+        qkv_own = line_sum(qkv_local)
+        out_own = line_sum(out_local) if spread else None
+    down_walk.got = [after(g, qkv_local) for g in down_walk.got]
+    down_own = down_walk.own()
+    branches = rank_sum(branch_parts, down_own)
+    mixed_grad = after(mixed_grad, down_own)
+    far, near = halves(mixed_grad, qkv_mine, last_last, back_more)
+    got = other_core(far)
+    down_pieces = plane_pieces(down_own, near)
+    up_both = both_cores(after(up_own, near))
+    grad_parts = rank_parts(near, after(got, up_both))
+    branches = after(branches, *grad_parts)
+    up_pieces = plane_pieces(up_both, *grad_parts)
+    normed_grad = rank_sum(grad_parts, branches)
+    up_pieces = [up_both] + [after(piece, normed_grad) for piece in up_pieces[1:]]
+    down_pieces = down_pieces[:1] + [after(piece, *grad_parts) for piece in down_pieces[1:]]
     qkv_both = both_cores(qkv_own)
     qkv_pieces = plane_pieces(qkv_both)
-    up_pieces = up_pieces[:1] + [after(piece, qkv_both) for piece in up_pieces[1:]]
-    down_pieces = down_pieces[:1] + [after(piece, near) for piece in down_pieces[1:]]
+    out_pieces = plane_pieces(after(out_own, qkv_both)) if spread else None
 
     token_rows = tokens[0].astype(f32)
     block_out = (token_rows + branches + outb + downb).astype(bf16)[None]
@@ -711,7 +716,7 @@
     tokens_grad = (upstream + rows_grad).astype(bf16)[None]
 
     if spread and one_each:
-        qkv_wgrad = place_heads(place, qkv_pieces, nz)
+        qkv_wgrad = place_heads(places, qkv_pieces, nz)
     elif spread:
         qkv_all = arrange([piece[None] for piece in qkv_pieces], bf16)
         qkv_all = qkv_all.reshape(ns, CORES, rows, pairs, 3, PAIR).transpose(0, 1, 2, 4, 3, 5)
@@ -722,7 +727,7 @@
         qkv_all = qkv_all.reshape(ns, CORES, rows, pairs, 3, PAIR)
         qkv_wgrad = qkv_all.transpose(2, 4, 0, 1, 3, 5).reshape(rows, 3 * d).astype(f32)
     if spread:
-        out_wgrad = arrange(out_pieces, f32)
+        out_wgrad = order_pieces(order_kernel, "place_out", places, out_pieces, dtype=f32)
     else:
         rank = CORES * s + k
         out_padded = lax.dynamic_update_slice_in_dim(
@@ -731,12 +736,12 @@
         out_shard = lax.psum_scatter(out_padded, "fsdp", scatter_dimension=0, tiled=True)
         out_wgrad = lax.psum(out_shard.astype(f32), "seq")
     if tiled:
-        up_wgrad = place_units(place, up_pieces, nz, w)
+        up_wgrad = place_units(places, up_pieces, nz, w)
     else:
         up_all = arrange([piece[None] for piece in up_pieces], bf16)
         up_all = up_all.reshape(ns, CORES, rows, nz, w)
         up_wgrad = up_all.transpose(2, 3, 1, 0, 4).reshape(rows, ff).astype(f32)
-    down_wgrad = arrange(down_pieces, f32)
+    down_wgrad = order_pieces(order_kernel, "place_down", places, down_pieces, dtype=f32)
 
     mixed_sum = jnp.sum(mixed_grad.astype(f32), axis=0).reshape(pairs, 3, PAIR).transpose(1, 0, 2)
     if spread:

time: 735 us -> 611 us (0.83)
  starting transfers between devices: 126 us -> 60.2 us
  waiting for transfers between devices: 277 us -> 219 us
  Pallas kernels: 75.2 us -> 97.9 us
  other arithmetic: 68.6 us -> 51.7 us
    ppermute x24 -> x6, starting transfers between devices: 73.8 us -> 17.7 us  [step_line(): return lax.ppermute(part, 'fsdp', hops_)]
    ppermute x24, waiting for transfers between devices: 169 us -> 129 us  [plane_hop(): return lax.ppermute(x, everyone, hops)]
    pallas_call x2 -> x4, Pallas kernels: 19.5 us -> 40.9 us  [order_pieces(): pl.pallas_call(kernel, grid_spec=pltpu.PrefetchScalarGridSpec(num_scalar_...]
    ppermute x24 -> x6, waiting for transfers between devices: 43.3 us -> 22.2 us  [step_line(): return lax.ppermute(part, 'fsdp', hops_)]
    dynamic_update_slice x8 -> x0, other arithmetic: 12.7 us -> none  [arrange(): lax.dynamic_update_slice_in_dim(whole, piece.astype(dtype), (s ^ d) * siz...]
    convert_element_type x8 -> x2, other arithmetic: 20.1 us -> 8.63 us  [parts(): (p.astype(f32) + g.astype(f32)).astype(bf16)]
    convert_element_type x2 -> x4, other arithmetic: 9.02 us -> 15 us  [the longest x2 12 us: rank_parts(): return parts[:1] + [part.astype(bf16) for part in parts[1:]]]
    dot_general x5 -> x6, matrix products: 50.2 us -> 48.1 us  [plain_dot(): return jnp.dot(left, right, preferred_element_type=f32)]
  transfers between devices with their start and end apart: 66 -> 50, of which waited for: 26 -> 20; matrix products, arithmetic and copies ran while one was open for 31% -> 34% of each run, Pallas kernels for 9% -> 14%
where the time goes in v2:
time: 611 us; the launch traced here: 605 us
  waiting for transfers between devices  219 us (36%)
  matrix products  133 us (22%)
  Pallas kernels  97.9 us (16%)
  starting transfers between devices  60.2 us (10%)
  other arithmetic  51.7 us (8%)
  local copies, waits for them, and re-layouts  28.8 us (5%)
  between operations  15 us (2%)
    ppermute x24, waiting for transfers between devices, plane_hop(): return lax.ppermute(x, everyone, hops)  129 us
    dot_general x6, matrix products, plain_dot(): return jnp.dot(left, right, preferred_element_type=f32)  48.1 us
    dot_general x6, matrix products, last_last(): lax.dot_general(left, right, (((1,), (1,)), ((), ())), preferred_element_...  47.9 us
    pallas_call x4, Pallas kernels, order_pieces(): pl.pallas_call(kernel, grid_spec=pltpu.PrefetchScalarGridSpec(num_scalar_...  40.9 us
    dot_general x4, matrix products, first_first(): lax.dot_general(left, right, (((0,), (0,)), ((), ())), preferred_element_...  36.6 us
    all_gather x1, waiting for transfers between devices, on_device(): lax.all_gather(both, 'fsdp', axis=0, tiled=True, axis_index_groups=lines)  32.1 us
    ppermute x24, starting transfers between devices, plane_hop(): return lax.ppermute(x, everyone, hops)  31.6 us
    all_gather x1, waiting for transfers between devices, on_device(): lax.all_gather(down_part, 'fsdp', axis=0, tiled=True, axis_index_groups=l...  23.8 us
  transfers between devices with their start and end apart: 50, of which 20 were waited for; matrix products, arithmetic and copies ran while one was open for 34% of the time, Pallas kernels for 14%

profile of v2, /device:TPU:0, one launch (start us, length us, event | category | flops | bytes accessed | tf_op | source)
XLA Modules:
  0.0 605.3 jit_solution(7159141302966178398)
XLA Ops:
  45.2 13.3 %collective-permute-done.1.refs_2_ = bf16[256,2048]{1,0:T(8,128)(2,1)S(1)} collective-permute-done((bf16[256,2048]{1,0:T(8,128)(2,1)S(1)}, bf16[256,2048]{1,0:T(8,128)(2,1)S(1)}, u32[]{:S(2)}, u32[]{:S(2)}) %collective-permute-start.1) | collective-permute-done | bytes 1048608 | tf_op jit(solution)/shard_map/ppermute | solution.py:462
  61.6 11.8 %collective-permute-done.7.refs_1_ = bf16[256,2048]{1,0:T(8,128)(2,1)} collective-permute-done((bf16[256,2048]{1,0:T(8,128)(2,1)S(1)}, bf16[256,2048]{1,0:T(8,128)(2,1)}, u32[]{:S(2)}, u32[]{:S(2)}) %collective-permute-start.7) | collective-permute-done | bytes 1048608 | tf_op jit(solution)/shard_map/ppermute | solution.py:462
  76.7 11.6 %norm_both.1 = bf16[2048,2048]{1,0:T(8,128)(2,1)} custom-call(s32[8]{0:T(128)S(1)} %concatenate.19.places_ref, f32[1,2048]{1,0:T(1,128)S(1)} %bitcast.147, f32[1,2048]{1,0:T(1,128)S(1)} %bitcast.146, bf16[256,2048]{1,0:T(8,128)(2,1)S(1)} %bitcast.138, bf16[256,2048]{1,0:T(8,128)(2,1)} %collective-permute-done.refs_1_, bf16[256,2048]{1,0:T(8,128)(2,1)S(1)} %copy-done.7, ...), custom_call_target="tpu_custom_call" | custom-call | tf_op jit(solution)/shard_map/norm_both/pallas_call | solution.py:234
  88.3 9.1 %all-gather.4.cloned.1.call-done = bf16[2048,2048]{1,0:T(8,128)(2,1)} async-done(((bf16[256,2048]{1,0:T(8,128)(2,1)}), bf16[2048,2048]{1,0:T(8,128)(2,1)}) %all-gather.4.cloned.1.call-update) | async-done | bytes 8388624 | tf_op jit(solution)/shard_map/all_gather | solution.py:521
  97.4 16.7 %multiply_convert_fusion.1 = (bf16[2048,1024]{1,0:T(8,128)(2,1)}, f32[2048,1024]{1,0:T(8,128)}) fusion(f32[1024]{0:T(1024)S(1)} %bitcast.186, bf16[2048,2048]{1,0:T(8,128)(2,1)} %norm_both.1, bf16[2048,2048]{1,0:T(8,128)(2,1)} %all-gather.4.cloned.1.call-done, s32[]{:T(128)S(6)} %select_n.237), kind=kOutput, calls=%fused_computation.6 | convolution fusion | flops 8610906112 | bytes 25169924 | tf_op jit(solution)/shard_map/dot_general | solution.py:50
  121.9 19.7 %order_both.1 = bf16[2048,2048]{1,0:T(8,128)(2,1)} custom-call(s32[8]{0:T(128)S(1)} %concatenate.19.places_ref, bf16[256,2048]{1,0:T(8,128)(2,1)S(1)} %bitcast.142, bf16[256,2048]{1,0:T(8,128)(2,1)} %collective-permute-done.7.refs_1_, bf16[256,2048]{1,0:T(8,128)(2,1)} %collective-permute-done.8.refs_2_, bf16[256,2048]{1,0:T(8,128)(2,1)} %collective-permute-done.9.refs_3_, ...), custom_call_target="tpu_custom_call" | custom-call | tf_op jit(solution)/shard_map/order_both/pallas_call | solution.py:234
  141.7 12.8 %convolution_convert_fusion = bf16[1024,2048]{1,0:T(8,128)(2,1)} fusion(bf16[2048,1024]{1,0:T(8,128)(2,1)S(1)} %copy-done.46, bf16[2048,2048]{1,0:T(8,128)(2,1)} %order_both.1), kind=kOutput, calls=%fused_computation.10 | convolution fusion | flops 8592031744 | bytes 16777216 | tf_op jit(solution)/shard_map/dot_general | solution.py:559
  154.5 23.8 %all-gather.6.cloned.1.call-done = bf16[1024,2048]{1,0:T(8,128)(2,1)} async-done(((bf16[256,2048]{1,0:T(8,128)(2,1)}), bf16[1024,2048]{1,0:T(8,128)(2,1)}) %all-gather.6.cloned.1.call-update) | async-done | bytes 4194320 | tf_op jit(solution)/shard_map/all_gather | solution.py:538
  185.2 17.2 %multiply_convert_fusion = bf16[2048,1024]{1,0:T(8,128)(2,1)S(1)} fusion(f32[2048,1024]{1,0:T(8,128)} %get-tuple-element.147, bf16[2048,2048]{1,0:T(8,128)(2,1)} %order_both.1, bf16[1024,2048]{1,0:T(8,128)(2,1)S(1)} %copy-done.44, f32[1024]{0:T(1024)S(1)} %bitcast.187), kind=kOutput, calls=%fused_computation.5 | convolution fusion | flops 8629780480 | bytes 25169920 | tf_op jit(solution)/shard_map/dot_general | solution.py:46
  204.5 10.9 %convolution_convert_fusion.5 = bf16[2048,1024]{1,0:T(8,128)(2,1)} fusion(bf16[2048,2048]{1,0:T(8,128)(2,1)S(1)} %bitcast.158, bf16[2048,1024]{1,0:T(8,128)(2,1)S(1)} %multiply_convert_fusion), kind=kOutput, calls=%fused_computation.15 | convolution fusion | flops 8592031744 | bytes 16777216 | tf_op jit(solution)/shard_map/dot_general | solution.py:559
  215.4 11.3 %collective-permute-done.14 = bf16[256,2048]{1,0:T(8,128)(2,1)} collective-permute-done((bf16[256,2048]{1,0:T(8,128)(2,1)S(1)}, bf16[256,2048]{1,0:T(8,128)(2,1)}, u32[]{:S(2)}, u32[]{:S(2)}) %collective-permute-start.14) | collective-permute-done | bytes 1048608 | tf_op jit(solution)/shard_map/ppermute | solution.py:600
  238.2 8.3 %convolution_convert_fusion.3 = bf16[1024,2048]{1,0:T(8,128)(2,1)} fusion(bf16[1024,2048]{1,0:T(8,128)(2,1)S(1)} %copy-done.45, bf16[2048,1024]{1,0:T(8,128)(2,1)} %get-tuple-element.71), kind=kOutput, calls=%fused_computation.13 | convolution fusion | flops 4297064448 | bytes 10485760 | tf_op jit(solution)/shard_map/dot_general | solution.py:50
  264.9 32.1 %all-gather.8.cloned.1.call-done = bf16[2048,1024]{1,0:T(8,128)(2,1)} async-done(((bf16[512,1024]{1,0:T(8,128)(2,1)}), bf16[2048,1024]{1,0:T(8,128)(2,1)}) %all-gather.8.cloned.1.call-update) | async-done | bytes 4194320 | tf_op jit(solution)/shard_map/all_gather | solution.py:548
  303.7 9.9 %broadcast_add_fusion.mixed_ref = f32[2048,768]{1,0:T(8,128)S(1)} fusion(f32[768]{0:T(1024)S(1)} %fusion.44, bf16[2048,2048]{1,0:T(8,128)(2,1)} %norm_both.1, bf16[2048,1024]{1,0:T(8,128)(2,1)S(1)} %copy-done.33), kind=kOutput, calls=%fused_computation.21 | convolution fusion | flops 6444023808 | bytes 17829888 | tf_op jit(solution)/shard_map/dot_general | solution.py:50
  313.7 15.4 %attend.1 = (bf16[2048,768]{1,0:T(8,128)(2,1)S(1)}, bf16[2048,256]{1,0:T(8,128)(2,1)S(1)}, f32[2,2,2,1024]{3,2,1,0:T(2,128)S(1)}) custom-call(f32[2048,768]{1,0:T(8,128)S(1)} %broadcast_add_fusion.mixed_ref, f32[1024,128]{1,0:T(8,128)S(1)} %copy-done.12, f32[1024,128]{1,0:T(8,128)S(1)} %copy-done.10, f32[1024,128]{1,0:T(8,128)S(1)} %copy-done.8), custom_call_target="tpu_custom_call" | custom-call | flops 2147483648 | bytes 12582912 | tf_op jit(solution)/shard_map/attend/pallas_call | solution.py:150
  359.0 20.2 %attend_back.1 = bf16[2048,768]{1,0:T(8,128)(2,1)S(1)} custom-call(bf16[2048,768]{1,0:T(8,128)(2,1)S(1)} %copy-done.17, bf16[2048,256]{1,0:T(8,128)(2,1)S(1)} %copy-done.18, f32[2,2,2,1024]{3,2,1,0:T(2,128)S(1)} %get-tuple-element.85.logsum_ref, f32[1024,128]{1,0:T(8,128)S(1)} %copy-done.13, f32[1024,128]{1,0:T(8,128)S(1)} %copy-done.11, ...), custom_call_target="tpu_custom_call" | custom-call | flops 5368709120 | bytes 9437184 | tf_op jit(solution)/shard_map/attend_back/pallas_call | solution.py:180
  386.4 10.9 %collective-permute-done.23 = bf16[256,2048]{1,0:T(8,128)(2,1)S(1)} collective-permute-done((bf16[256,2048]{1,0:T(8,128)(2,1)}, bf16[256,2048]{1,0:T(8,128)(2,1)S(1)}, u32[]{:S(2)}, u32[]{:S(2)}) %collective-permute-start.23) | collective-permute-done | bytes 1048608 | tf_op jit(solution)/shard_map/ppermute | solution.py:600
  404.7 7.9 %add_convert_fusion = bf16[1024,2048]{1,0:T(8,128)(2,1)} fusion(bf16[1024,2048]{1,0:T(8,128)(2,1)} %convolution_convert_fusion.2, bf16[2048,1024]{1,0:T(8,128)(2,1)} %all-gather.8.cloned.1.call-done, bf16[2048,768]{1,0:T(8,128)(2,1)S(1)} %copy-done.5), kind=kOutput, calls=%fused_computation.1 | convolution fusion | flops 3227516928 | bytes 13107200 | tf_op jit(solution)/shard_map/dot_general | solution.py:46
  414.8 7.2 %add_convert_fusion.1 = bf16[1024,2048]{1,0:T(8,128)(2,1)S(1)} fusion(bf16[1024,2048]{1,0:T(8,128)(2,1)} %convolution_convert_fusion.1, bf16[2048,1024]{1,0:T(8,128)(2,1)} %all-gather.8.cloned.1.call-done, bf16[2048,768]{1,0:T(8,128)(2,1)} %copy-done.4), kind=kOutput, calls=%fused_computation.2 | convolution fusion | flops 3227516928 | bytes 13107200 | tf_op jit(solution)/shard_map/dot_general | solution.py:46
  445.1 10.7 %collective-permute-done.24 = bf16[256,2048]{1,0:T(8,128)(2,1)S(1)} collective-permute-done((bf16[256,2048]{1,0:T(8,128)(2,1)S(1)}, bf16[256,2048]{1,0:T(8,128)(2,1)S(1)}, u32[]{:S(2)}, u32[]{:S(2)}) %collective-permute-start.24) | collective-permute-done | bytes 1048608 | tf_op jit(solution)/shard_map/ppermute | solution.py:462
  468.7 11.4 %collective-permute-done.40.refs_1_ = bf16[256,2048]{1,0:T(8,128)(2,1)} collective-permute-done((bf16[256,2048]{1,0:T(8,128)(2,1)S(1)}, bf16[256,2048]{1,0:T(8,128)(2,1)}, u32[]{:S(2)}, u32[]{:S(2)}) %collective-permute-start.40) | collective-permute-done | bytes 1048608 | tf_op jit(solution)/shard_map/ppermute | solution.py:462
  481.6 21.0 %collective-permute-done.37.refs_1_ = bf16[2,256,1024]{2,1,0:T(8,128)(2,1)} collective-permute-done((bf16[2,256,1024]{2,1,0:T(8,128)(2,1)}, bf16[2,256,1024]{2,1,0:T(8,128)(2,1)}, u32[]{:S(2)}, u32[]{:S(2)}) %collective-permute-start.37) | collective-permute-done | bytes 1048608 | tf_op jit(solution)/shard_map/ppermute | solution.py:462
  505.3 19.8 %collective-permute-done.27 = bf16[256,2048]{1,0:T(8,128)(2,1)} collective-permute-done((bf16[256,2048]{1,0:T(8,128)(2,1)}, bf16[256,2048]{1,0:T(8,128)(2,1)}, u32[]{:S(2)}, u32[]{:S(2)}) %collective-permute-start.27) | collective-permute-done | bytes 1048608 | tf_op jit(solution)/shard_map/ppermute | solution.py:462
  536.7 15.3 %collective-permute-done.31.refs_1_ = bf16[2,256,768]{2,1,0:T(8,128)(2,1)} collective-permute-done((bf16[2,256,768]{2,1,0:T(8,128)(2,1)}, bf16[2,256,768]{2,1,0:T(8,128)(2,1)}, u32[]{:S(2)}, u32[]{:S(2)}) %collective-permute-start.31) | collective-permute-done | bytes 786464 | tf_op jit(solution)/shard_map/ppermute | solution.py:462
  (335 shorter events, 242.1 us)
Async XLA Ops:
  7.3 90.1 %all-gather.4.cloned.1.call-start = ((), (), s32[]{:S(2)}) async-start(), calls=%async_computation.4 | async-start | bytes 9437184 | tf_op jit(solution)/shard_map/all_gather | solution.py:521
  22.7 155.6 %all-gather.6.cloned.1.call-start = ((), (), s32[]{:S(2)}) async-start(), calls=%async_computation.5 | async-start | bytes 5242880 | tf_op jit(solution)/shard_map/all_gather | solution.py:538
  43.6 253.3 %all-gather.8.cloned.1.call-start = ((), (), s32[]{:S(2)}) async-start(), calls=%async_computation.6 | async-start | bytes 5242880 | tf_op jit(solution)/shard_map/all_gather | solution.py:548
  73.4 48.5 %collective-permute-start.10 = (bf16[256,2048]{1,0:T(8,128)(2,1)S(1)}, bf16[256,2048]{1,0:T(8,128)(2,1)}, u32[]{:S(2)}, u32[]{:S(2)}) collective-permute-start(bf16[256,2048]{1,0:T(8,128)(2,1)S(1)} %bitcast.140), channel_id=1, source_target_pairs={{0,1},{1,0},{2,3},{3,2},{4,5},{5,4},{6,7},{7,6},{8,9},{9,8},{10,11... | collective-permute-start | bytes 3145736 | tf_op jit(solution)/shard_map/ppermute | solution.py:450
  73.4 40.6 %collective-permute-start.8 = (bf16[256,2048]{1,0:T(8,128)(2,1)S(1)}, bf16[256,2048]{1,0:T(8,128)(2,1)}, u32[]{:S(2)}, u32[]{:S(2)}) collective-permute-start(bf16[256,2048]{1,0:T(8,128)(2,1)S(1)} %bitcast.141), channel_id=1, source_target_pairs={{0,16},{1,9},{2,18},{3,11},{4,20},{5,13},{6,22},{7,15},{8,24},{9,1... | collective-permute-start | bytes 3145736 | tf_op jit(solution)/shard_map/ppermute | solution.py:462
  75.0 39.1 %collective-permute-start.9 = (bf16[256,2048]{1,0:T(8,128)(2,1)}, bf16[256,2048]{1,0:T(8,128)(2,1)}, u32[]{:S(2)}, u32[]{:S(2)}) collective-permute-start(bf16[256,2048]{1,0:T(8,128)(2,1)} %collective-permute-done.7.refs_1_), channel_id=1, source_target_pairs={{0,16},{1,9},{2,18},{3,11},{4,20},{5,13},{6,22},{7,15},{8,24},{9,1... | collective-permute-start | bytes 3145736 | tf_op jit(solution)/shard_map/ppermute | solution.py:462
  121.8 280.0 %reduce-scatter.3.cloned.1.call-start = ((), (), s32[]{:S(2)}) async-start(), calls=%async_computation.7 | async-start | bytes 5242880 | tf_op jit(solution)/shard_map/reduce_scatter | solution.py:644
  181.2 34.2 %collective-permute-start.16 = (bf16[256,2048]{1,0:T(8,128)(2,1)}, bf16[256,2048]{1,0:T(8,128)(2,1)}, u32[]{:S(2)}, u32[]{:S(2)}) collective-permute-start(bf16[256,2048]{1,0:T(8,128)(2,1)} %get-tuple-element.122), channel_id=1, source_target_pairs={{6,4},{7,5},{14,12},{15,13},{22,20},{23,21},{30,28},{31,29}} | collective-permute-start | bytes 3145736 | tf_op jit(solution)/shard_map/ppermute | solution.py:600
  182.9 43.8 %collective-permute-start.14 = (bf16[256,2048]{1,0:T(8,128)(2,1)S(1)}, bf16[256,2048]{1,0:T(8,128)(2,1)}, u32[]{:S(2)}, u32[]{:S(2)}) collective-permute-start(bf16[256,2048]{1,0:T(8,128)(2,1)S(1)} %get-tuple-element.123), channel_id=1, source_target_pairs={{0,2},{1,3},{8,10},{9,11},{16,18},{17,19},{24,26},{25,27}} | collective-permute-start | bytes 3145736 | tf_op jit(solution)/shard_map/ppermute | solution.py:600
  215.3 288.7 %reduce-scatter.5.cloned.1.call-start = ((), (), s32[]{:S(2)}) async-start(), calls=%async_computation.8 | async-start | bytes 5242880 | tf_op jit(solution)/shard_map/reduce_scatter | solution.py:644
  231.1 68.2 %collective-permute-start.17 = (bf16[256,2048]{1,0:T(8,128)(2,1)}, bf16[256,2048]{1,0:T(8,128)(2,1)}, u32[]{:S(2)}, u32[]{:S(2)}) collective-permute-start(bf16[256,2048]{1,0:T(8,128)(2,1)} %get-tuple-element.120), channel_id=1, source_target_pairs={{6,4},{4,2},{7,5},{5,3},{14,12},{12,10},{15,13},{13,11},{22,20},{2... | collective-permute-start | bytes 3145736 | tf_op jit(solution)/shard_map/ppermute | solution.py:600
  232.8 66.6 %collective-permute-start.15 = (bf16[256,2048]{1,0:T(8,128)(2,1)}, bf16[256,2048]{1,0:T(8,128)(2,1)}, u32[]{:S(2)}, u32[]{:S(2)}) collective-permute-start(bf16[256,2048]{1,0:T(8,128)(2,1)} %get-tuple-element.121), channel_id=1, source_target_pairs={{0,2},{2,4},{1,3},{3,5},{8,10},{10,12},{9,11},{11,13},{16,18},{18,... | collective-permute-start | bytes 3145736 | tf_op jit(solution)/shard_map/ppermute | solution.py:600
  335.9 61.4 %collective-permute-start.23 = (bf16[256,2048]{1,0:T(8,128)(2,1)}, bf16[256,2048]{1,0:T(8,128)(2,1)S(1)}, u32[]{:S(2)}, u32[]{:S(2)}) collective-permute-start(bf16[256,2048]{1,0:T(8,128)(2,1)} %get-tuple-element.118), channel_id=1, source_target_pairs={{6,4},{4,2},{2,0},{7,5},{5,3},{3,1},{14,12},{12,10},{10,8},{15,13}... | collective-permute-start | bytes 3145736 | tf_op jit(solution)/shard_map/ppermute | solution.py:600
  337.1 61.1 %collective-permute-start.22 = (bf16[256,2048]{1,0:T(8,128)(2,1)}, bf16[256,2048]{1,0:T(8,128)(2,1)S(1)}, u32[]{:S(2)}, u32[]{:S(2)}) collective-permute-start(bf16[256,2048]{1,0:T(8,128)(2,1)} %get-tuple-element.119), channel_id=1, source_target_pairs={{0,2},{2,4},{4,6},{1,3},{3,5},{5,7},{8,10},{10,12},{12,14},{9,11},... | collective-permute-start | bytes 3145736 | tf_op jit(solution)/shard_map/ppermute | solution.py:600
  414.2 30.9 %collective-permute-start.20 = (bf16[256,2048]{1,0:T(8,128)(2,1)}, bf16[256,2048]{1,0:T(8,128)(2,1)S(1)}, u32[]{:S(2)}, u32[]{:S(2)}) collective-permute-start(bf16[256,2048]{1,0:T(8,128)(2,1)} %get-tuple-element.116), channel_id=1, source_target_pairs={{0,8},{1,17},{2,10},{3,19},{4,12},{5,21},{6,14},{7,23},{8,0},{9,25... | collective-permute-start | bytes 3145736 | tf_op jit(solution)/shard_map/ppermute | solution.py:462
  440.5 39.6 %collective-permute-start.40 = (bf16[256,2048]{1,0:T(8,128)(2,1)S(1)}, bf16[256,2048]{1,0:T(8,128)(2,1)}, u32[]{:S(2)}, u32[]{:S(2)}) collective-permute-start(bf16[256,2048]{1,0:T(8,128)(2,1)S(1)} %fusion.22.refs_0_), channel_id=1, source_target_pairs={{0,8},{1,17},{2,10},{3,19},{4,12},{5,21},{6,14},{7,23},{8,0},{9,25... | collective-permute-start | bytes 3145736 | tf_op jit(solution)/shard_map/ppermute | solution.py:462
  457.6 45.0 %collective-permute-start.37 = (bf16[2,256,1024]{2,1,0:T(8,128)(2,1)}, bf16[2,256,1024]{2,1,0:T(8,128)(2,1)}, u32[]{:S(2)}, u32[]{:S(2)}) collective-permute-start(bf16[2,256,1024]{2,1,0:T(8,128)(2,1)} %pad_maximum_fusion.2.refs_0_), channel_id=1, source_target_pairs={{0,8},{1,17},{2,10},{3,19},{4,12},{5,21},{6,14},{7,23},{8,0},{9,25... | collective-permute-start | bytes 3145736 | tf_op jit(solution)/shard_map/ppermute | solution.py:462
  459.0 66.0 %collective-permute-start.27 = (bf16[256,2048]{1,0:T(8,128)(2,1)}, bf16[256,2048]{1,0:T(8,128)(2,1)}, u32[]{:S(2)}, u32[]{:S(2)}) collective-permute-start(bf16[256,2048]{1,0:T(8,128)(2,1)} %get-tuple-element.112), channel_id=1, source_target_pairs={{0,8},{1,17},{2,10},{3,19},{4,12},{5,21},{6,14},{7,23},{8,0},{9,25... | collective-permute-start | bytes 3145736 | tf_op jit(solution)/shard_map/ppermute | solution.py:462
  462.8 63.7 %collective-permute-start.29 = (bf16[256,2048]{1,0:T(8,128)(2,1)}, bf16[256,2048]{1,0:T(8,128)(2,1)}, u32[]{:S(2)}, u32[]{:S(2)}) collective-permute-start(bf16[256,2048]{1,0:T(8,128)(2,1)} %add_convert_fusion.4), channel_id=1, source_target_pairs={{0,16},{1,9},{2,18},{3,11},{4,20},{5,13},{6,22},{7,15},{8,24},{9,1... | collective-permute-start | bytes 3145736 | tf_op jit(solution)/shard_map/ppermute | solution.py:462
  467.9 90.1 %collective-permute-start.41 = (bf16[256,2048]{1,0:T(8,128)(2,1)S(1)}, bf16[256,2048]{1,0:T(8,128)(2,1)}, u32[]{:S(2)}, u32[]{:S(2)}) collective-permute-start(bf16[256,2048]{1,0:T(8,128)(2,1)S(1)} %fusion.22.refs_0_), channel_id=1, source_target_pairs={{0,16},{1,9},{2,18},{3,11},{4,20},{5,13},{6,22},{7,15},{8,24},{9,1... | collective-permute-start | bytes 3145736 | tf_op jit(solution)/shard_map/ppermute | solution.py:462
  480.1 81.8 %collective-permute-start.42 = (bf16[256,2048]{1,0:T(8,128)(2,1)}, bf16[256,2048]{1,0:T(8,128)(2,1)}, u32[]{:S(2)}, u32[]{:S(2)}) collective-permute-start(bf16[256,2048]{1,0:T(8,128)(2,1)} %collective-permute-done.40.refs_1_), channel_id=1, source_target_pairs={{0,16},{1,9},{2,18},{3,11},{4,20},{5,13},{6,22},{7,15},{8,24},{9,1... | collective-permute-start | bytes 3145736 | tf_op jit(solution)/shard_map/ppermute | solution.py:462
  502.6 68.7 %collective-permute-start.38 = (bf16[2,256,1024]{2,1,0:T(8,128)(2,1)}, bf16[2,256,1024]{2,1,0:T(8,128)(2,1)}, u32[]{:S(2)}, u32[]{:S(2)}) collective-permute-start(bf16[2,256,1024]{2,1,0:T(8,128)(2,1)} %pad_maximum_fusion.2.refs_0_), channel_id=1, source_target_pairs={{0,16},{1,9},{2,18},{3,11},{4,20},{5,13},{6,22},{7,15},{8,24},{9,1... | collective-permute-start | bytes 3145736 | tf_op jit(solution)/shard_map/ppermute | solution.py:462
  525.0 38.3 %collective-permute-start.39 = (bf16[2,256,1024]{2,1,0:T(8,128)(2,1)}, bf16[2,256,1024]{2,1,0:T(8,128)(2,1)}, u32[]{:S(2)}, u32[]{:S(2)}) collective-permute-start(bf16[2,256,1024]{2,1,0:T(8,128)(2,1)} %collective-permute-done.37.refs_1_), channel_id=1, source_target_pairs={{0,16},{1,9},{2,18},{3,11},{4,20},{5,13},{6,22},{7,15},{8,24},{9,1... | collective-permute-start | bytes 3145736 | tf_op jit(solution)/shard_map/ppermute | solution.py:462
  557.9 33.7 %collective-permute-start.32 = (bf16[2,256,768]{2,1,0:T(8,128)(2,1)}, bf16[2,256,768]{2,1,0:T(8,128)(2,1)}, u32[]{:S(2)}, u32[]{:S(2)}) collective-permute-start(bf16[2,256,768]{2,1,0:T(8,128)(2,1)} %pad_maximum_fusion.3.refs_0_), channel_id=1, source_target_pairs={{0,16},{1,9},{2,18},{3,11},{4,20},{5,13},{6,22},{7,15},{8,24},{9,1... | collective-permute-start | bytes 2359304 | tf_op jit(solution)/shard_map/ppermute | solution.py:462
  (82 other events, 1162.1 us)
Sparse Core Ops, SparseCore 0:
  11.6 85.7 all-gather.3
  99.5 78.7 all-gather.5
  180.4 116.4 all-gather.7
  299.1 99.1 reduce-scatter.2
  402.0 76.5 reduce-scatter.4

commit v3 on v2

--- a/solution.py
+++ b/solution.py
@@ -228,8 +228,10 @@
             out_ref[...] = piece[...].astype(out_ref.dtype)
 
 
-def order_pieces(kernel, name, places, pieces, vectors=(), dtype=bf16):
+def order_pieces(kernel, name, places, pieces, vectors=(), dtype=bf16, size=None):
     local, d = pieces[0].shape
+    size = local if size is None else size
+    last = local // size - 1
     fixed = lambda i, places: (0, 0)
     return pl.pallas_call(
         kernel,
@@ -237,10 +239,10 @@
             num_scalar_prefetch=1,
             grid=(len(pieces),),
             in_specs=[pl.BlockSpec((1, d), fixed)] * len(vectors)
-            + [pl.BlockSpec((local, d), fixed)] * len(pieces),
-            out_specs=pl.BlockSpec((local, d), lambda i, places: (places[i], 0)),
+            + [pl.BlockSpec((size, d), lambda i, places: (last, 0))] * len(pieces),
+            out_specs=pl.BlockSpec((size, d), lambda i, places: (places[i], 0)),
         ),
-        out_shape=jax.ShapeDtypeStruct((len(pieces) * local, d), dtype),
+        out_shape=jax.ShapeDtypeStruct((len(pieces) * size, d), dtype),
         compiler_params=pltpu.CompilerParams(vmem_limit_bytes=48 * 1024 * 1024),
         name=name,
     )(places, *[v[None] for v in vectors], *pieces)
@@ -279,23 +281,24 @@
     *pieces, out_ref = refs
     ns = len(pieces)
     for i, piece in enumerate(pieces):
-        device = places_ref[i]
-        for q in range(nz):
-            for c in range(CORES):
-                to = pl.multiple_of(((q * CORES + c) * ns + device) * w, w)
-                out_ref[:, pl.ds(to, w)] = piece[c, :, q * w : (q + 1) * w].astype(f32)
-
-
-def place_units(places, pieces, nz, w):
-    cores, rows, width = pieces[0].shape
+        for c in range(CORES):
+            for q in range(nz):
+                core = c ^ places_ref[ns]
+                to = pl.multiple_of(((q * CORES + core) * ns + places_ref[i]) * w, w)
+                at = (c * nz + q) * w
+                out_ref[:, pl.ds(to, w)] = piece[:, at : at + w].astype(f32)
+
+
+def place_units(places, pieces, rows, nz, w):
+    width = pieces[0].shape[1]
     block = row_blocks(rows)
-    ff = width * cores * len(pieces)
+    ff = width * len(pieces)
     return pl.pallas_call(
         functools.partial(place_units_kernel, nz, w),
         grid_spec=pltpu.PrefetchScalarGridSpec(
             num_scalar_prefetch=1,
             grid=(rows // block,),
-            in_specs=[pl.BlockSpec((cores, block, width), lambda i, places: (0, i, 0)) for _ in pieces],
+            in_specs=[pl.BlockSpec((block, width), lambda i, places: (i, 0)) for _ in pieces],
             out_specs=pl.BlockSpec((block, ff), lambda i, places: (i, 0)),
         ),
         out_shape=jax.ShapeDtypeStruct((rows, ff), f32),
@@ -366,31 +369,61 @@
             for p in range(nz // 2):
                 at = (p * 3 + j) * PAIR
                 for c in range(CORES):
-                    loaded = [[pieces[i][c, :, at : at + PAIR].astype(f32) for i in pair] for pair in mates]
+                    own = slice(c * nz * 3 * HD + at, c * nz * 3 * HD + at + PAIR)
+                    loaded = [[pieces[i][:, own].astype(f32) for i in pair] for pair in mates]
+                    core = c ^ places_ref[ns]
                     one, two = loaded[0]
                     if ns == 4:
                         one = jnp.where(straight, one, loaded[1][0])
                         two = jnp.where(straight, two, loaded[1][1])
                     first, second = jnp.where(even, one, two), jnp.where(even, two, one)
                     for q, value in ((2 * p, lows(first, second)), (2 * p + 1, highs(first, second))):
-                        to = (((j * nz + q) * CORES + c) * tiles + tile) * PAIR
+                        to = (((j * nz + q) * CORES + core) * tiles + tile) * PAIR
                         out_ref[:, pl.ds(pl.multiple_of(to, PAIR), PAIR)] = value
 
 
 def place_heads(places, pieces, nz):
-    cores, rows, width = pieces[0].shape
+    rows = pieces[0].shape[0]
+    width = CORES * nz * 3 * HD
     block = row_blocks(rows)
-    whole = width * cores * len(pieces)
+    whole = width * len(pieces)
     return pl.pallas_call(
         functools.partial(place_heads_kernel, nz),
         grid_spec=pltpu.PrefetchScalarGridSpec(
             num_scalar_prefetch=1,
             grid=(rows // block,),
-            in_specs=[pl.BlockSpec((cores, block, width), lambda i, places: (0, i, 0)) for _ in pieces],
+            in_specs=[pl.BlockSpec((block, width), lambda i, places: (i, 0)) for _ in pieces],
             out_specs=pl.BlockSpec((block, whole), lambda i, places: (i, 0)),
         ),
         out_shape=jax.ShapeDtypeStruct((rows, whole), f32),
         name="place_heads",
+    )(places, *pieces)
+
+
+def place_out_kernel(places_ref, *refs):
+    *pieces, out_ref = refs
+    rows = out_ref.shape[0]
+    for i, piece in enumerate(pieces):
+
+        @pl.when(pl.program_id(0) == i)
+        def _(piece=piece):
+            wide = piece.shape[1]
+            for r in range(piece.shape[0] // rows):
+                out_ref[:, r * wide : (r + 1) * wide] = piece[r * rows : (r + 1) * rows, :].astype(f32)
+
+
+def place_out(places, pieces, wide, hw, d):
+    rows, width = pieces[0].shape
+    return pl.pallas_call(
+        place_out_kernel,
+        grid_spec=pltpu.PrefetchScalarGridSpec(
+            num_scalar_prefetch=1,
+            grid=(len(pieces),),
+            in_specs=[pl.BlockSpec((rows, wide), lambda i, places: (0, width // wide - 1)) for _ in pieces],
+            out_specs=pl.BlockSpec((hw, d), lambda i, places: (places[i], 0)),
+        ),
+        out_shape=jax.ShapeDtypeStruct((len(pieces) * hw, d), f32),
+        name="place_out",
     )(places, *pieces)
 
 
@@ -467,12 +500,30 @@
     places = jnp.stack([s ^ step for step in steps]).astype(jnp.int32)
     other_places = jnp.stack([s ^ step for step in other_steps]).astype(jnp.int32)
     both_places = jnp.concatenate([places, ns + other_places])
-
-    def plane_pieces(x, *passed):
-        if not two_steps:
-            return [x] + [plane_send(x, d) for d in range(1, ns)]
-        near, far = plane_hop(x, 0), plane_hop(x, 1)
-        return [x, near, far, plane_hop(after(near, *passed), 1)]
+    places = jnp.concatenate([places, k[None].astype(jnp.int32)])
+
+    class Pieces:
+        def __init__(self, x):
+            self.pieces = [x]
+            if two_steps:
+                self.pieces += [plane_hop(x, 0), plane_hop(x, 1)]
+            else:
+                self.pieces += [plane_send(x, d) for d in range(1, ns)]
+
+        def middle(self, *passed):
+            if two_steps:
+                near = after(self.pieces[1], self.pieces[2], *passed)
+                self.pieces.append(plane_hop(near, 1))
+                return [near]
+            return self.pieces[1:]
+
+        def all(self, *passed):
+            return self.pieces[:1] + [after(piece, *passed) for piece in self.pieces[1:]]
+
+    def plane_pieces(x):
+        pieces = Pieces(x)
+        pieces.middle()
+        return pieces.pieces
 
     def arrange(pieces, dtype):
         size = pieces[0].shape[0]
@@ -517,35 +568,37 @@
     upb_mine = pick(units_of(upb[None])[0], k, 0)
     tables = rotary_lanes(length)
 
-    up_both = units_of(up_weight) if not tiled else unit_columns(up_weight, place, nz, ns, w)
-    up_both = lax.all_gather(up_both.reshape(rows, -1), "fsdp", axis=0, tiled=True)
-    up_mine = core_half(up_both)
+    up_part = units_of(up_weight) if not tiled else unit_columns(up_weight, place, nz, ns, w)
+    up_part = up_part.reshape(rows, -1)
+    down_part = lax.dynamic_slice_in_dim(down_weight, s * w, w, 0)
+    merged = up_part.shape[1] == d
+    if merged:
+        ff_both = lax.all_gather(jnp.concatenate([up_part, down_part]), "fsdp", axis=0, tiled=True)
+    else:
+        up_both = lax.all_gather(up_part, "fsdp", axis=0, tiled=True)
+        down_mine = lax.all_gather(down_part, "fsdp", axis=0, tiled=True, axis_index_groups=lines)
 
     qkv_part = heads_of(qkv_weight) if not one_each else head_columns(qkv_weight, place, nz, ns)
     qkv_part = qkv_part.reshape(rows, CORES, -1)
-    down_part = lax.dynamic_slice_in_dim(down_weight, s * w, w, 0)
     out_part = lax.dynamic_slice_in_dim(out_weight, s * hw, hw, 0)
 
     x_pieces = plane_pieces(tokens[0])
-    ready = (gain, nbias, qkvb_mine, upb_mine, qkv_part, down_part, out_part) + tuple(tables)
+    ready = (gain, nbias, qkvb_mine, upb_mine, qkv_part, out_part) + tuple(tables)
     x_pieces = x_pieces[:1] + [after(piece, *ready) for piece in x_pieces[1:]]
     c_pieces = plane_pieces(after(cotangent[0], *x_pieces[1:]))
     x_pieces = x_pieces + [other_core(piece) for piece in x_pieces]
 
     normed = order_pieces(norm_kernel, "norm_both", both_places, x_pieces, (gain, nbias))
 
+    normed = order_pieces(norm_kernel, "norm_both", both_places, x_pieces, (gain, nbias))
+
     down_part = after(down_part, x_pieces[ns - 1])
-    down_mine = lax.all_gather(down_part, "fsdp", axis=0, tiled=True, axis_index_groups=lines)
-
-    qkv_part = after(qkv_part, normed)
+
     if one_each:
-        keep = pick(qkv_part, k, 1)
-        got = other_core(pick(qkv_part, 1 - k, 1))
-        both = jnp.concatenate([jnp.where(k == 0, keep, got), jnp.where(k == 0, got, keep)])
-        wide = hw * d // (CORES * rows)
-        beside = out_part.reshape(hw, -1, wide).transpose(1, 0, 2).reshape(CORES * rows, wide)
-        both = jnp.concatenate([both, beside], axis=1)
-        both = lax.all_gather(both, "fsdp", axis=0, tiled=True, axis_index_groups=lines)
+        out_wide = d * hw // rows
+        beside = out_part.reshape(hw, -1, out_wide).transpose(1, 0, 2).reshape(rows, out_wide)
+        both = jnp.concatenate([qkv_part.reshape(rows, -1), beside], axis=1)
+        both = lax.all_gather(after(both, normed), "fsdp", axis=0, tiled=True)
     else:
         qkv_both = lax.all_gather(qkv_part.reshape(rows, -1), "fsdp", axis=0, tiled=True)
         qkv_mine = core_half(qkv_both)
@@ -599,10 +652,14 @@
                 hops_.append((CORES * at + c, CORES * to + c))
         return lax.ppermute(part, "fsdp", hops_)
 
-    def both_cores(x):
-        keep = lax.dynamic_slice_in_dim(x, k * rows, rows, 0)
-        got = other_core(lax.dynamic_slice_in_dim(x, (1 - k) * rows, rows, 0))
-        return jnp.stack([jnp.where(k == 0, keep, got), jnp.where(k == 0, got, keep)])
+    def pair_cores(x):
+        by_core = x.reshape(nz, CORES, rows, -1)
+        keep, got = pick(by_core, k, 1), other_core(pick(by_core, 1 - k, 1))
+        return jnp.concatenate([keep, got], axis=2).reshape(nz * rows, -1)
+
+    def both_in_order(pieces):
+        every = arrange([piece[None] for piece in pieces], bf16).reshape(ns, rows, CORES, -1)
+        return jnp.where(k == 0, every, every[:, :, ::-1])
 
     def halves(left, right, dot, more=None):
         far = dot(left[length:], right)
@@ -619,87 +676,97 @@
             parts.append(part + lax.dynamic_slice_in_dim(got, at, local, 0).astype(f32))
         return parts[:1] + [part.astype(bf16) for part in parts[1:]]
 
-    def rank_sum(parts, *passed):
-        if not two_steps:
-            total = parts[0]
-            for d in range(1, ns):
-                total = total + plane_send(parts[d], d).astype(f32)
+    class RankSum:
+        def __init__(self, parts):
+            self.parts = parts
+            if two_steps:
+                self.across, self.beside = plane_hop(parts[3], 0), plane_hop(parts[1], 0)
+            else:
+                self.others = [plane_send(parts[d], d) for d in range(1, ns)]
+
+        def middle(self, *passed):
+            if not two_steps:
+                return list(passed)
+            across = after(self.across, self.beside, *passed)
+            self.rest = (self.parts[2].astype(f32) + across.astype(f32)).astype(bf16)
+            return [self.rest]
+
+        def total(self, *passed):
+            others = [self.beside, plane_hop(self.rest, 1)] if two_steps else self.others
+            total = self.parts[0]
+            for other in others:
+                total = total + after(other, *passed).astype(f32)
             return total
-        across = plane_hop(parts[3], 0)
-        beside = plane_hop(parts[1], 0)
-        across = after(across, *passed)
-        rest = plane_hop((parts[2].astype(f32) + across.astype(f32)).astype(bf16), 1)
-        return parts[0] + beside.astype(f32) + rest.astype(f32)
-
-    hidden = plain_dot(normed, up_mine) + upb_mine
-    activated, slope = gelu_and_slope(hidden)
-    activated = activated.astype(bf16)
-    c_pieces = c_pieces[:1] + [after(piece, activated) for piece in c_pieces[1:]]
-    c2 = order_pieces(order_kernel, "order_both", both_places, c_pieces + [other_core(piece) for piece in c_pieces])
-    down_local = first_first(activated, c2).astype(bf16)
-    down_walk = Walk(down_local)
-    down_walk.step()
 
     def line_sum(x):
         return lax.psum_scatter(
             x, "fsdp", scatter_dimension=0, tiled=True, axis_index_groups=lines
         )
 
-    c2, down_mine = after(c2, down_local), after(down_mine, down_local)
+    c_pieces = c_pieces[:1] + [after(piece, normed) for piece in c_pieces[1:]]
+    c2 = order_pieces(order_kernel, "order_both", both_places, c_pieces + [other_core(piece) for piece in c_pieces])
+    if merged:
+        ff_both = after(ff_both, c2).reshape(nz, CORES, rows + w, d)
+        up_mine = core_half(ff_both[:, :, :rows].reshape(d, d))
+        down_mine = pick(ff_both[:, :, rows:], k, 1).reshape(nz * w, d)
+    else:
+        up_mine = core_half(up_both)
+    hidden = plain_dot(normed, up_mine) + upb_mine
+    activated, slope = gelu_and_slope(hidden)
+    activated = activated.astype(bf16)
+    down_local = first_first(activated, c2).astype(bf16)
+    c2 = after(c2, down_local)
     hidden_grad = (last_last(c2, down_mine) * slope).astype(bf16)
-    up_local = first_first(normed, hidden_grad).astype(bf16)
-    up_own = line_sum(up_local)
-    activated = after(activated, up_local, *down_walk.step(after=up_local))
-    branch_more = halves(activated, down_mine, plain_dot)
-    hidden_grad = after(hidden_grad, *branch_more)
-    back_more = halves(hidden_grad, up_mine, last_last)
+    up_local = pair_cores(first_first(normed, hidden_grad).astype(bf16))
+    if merged:
+        ff_local = [x.reshape(nz, -1, d) for x in (up_local, down_local)]
+        ff_local = [jnp.concatenate(ff_local, axis=1).reshape(-1, d)]
+    else:
+        ff_local = [up_local, down_local]
+    ff_own = [line_sum(x) for x in ff_local]
 
     if one_each:
-        both = after(both, *back_more)
-        qkv_mine = both[:, : 3 * rank_cols]
-        out_mine = both[:, 3 * rank_cols :].reshape(nz, -1, hw, wide).transpose(0, 2, 1, 3)
-        out_mine = out_mine.reshape(rank_cols, d)
-    normed = after(normed, *down_walk.rest(after=back_more[0]))
+        both = after(both, *ff_local)
+        qkv_mine = lax.dynamic_slice_in_dim(both, k * 3 * rank_cols, 3 * rank_cols, 1)
+        out_mine = pick(both.reshape(nz, CORES, rows, -1), k, 1)[:, :, CORES * 3 * rank_cols :]
+        out_mine = out_mine.reshape(nz, -1, hw, out_wide).transpose(0, 2, 1, 3).reshape(rank_cols, d)
+    normed = after(normed, *ff_local)
     mixed = plain_dot(normed, qkv_mine) + qkvb_mine
     heads, attended, logsums = attend(mixed, tables, length)
     c2 = after(c2, attended)
     attended_grad = last_last(c2, out_mine).astype(bf16)
     attended = after(attended, attended_grad)
-    branch_far, branch_near = halves(attended, out_mine, plain_dot, branch_more)
-    branch_got = other_core(branch_far)
-    attended = after(attended, branch_near)
     out_local = first_first(attended, c2).astype(bf16)
-    branch_parts = rank_parts(branch_near, after(branch_got, out_local))
+    beside = []
+    if one_each:
+        beside = out_local.reshape(nz, hw, -1, out_wide).transpose(0, 2, 1, 3)
+        beside = [beside.reshape(nz * rows, out_wide)]
+    activated, attended = after(activated, out_local), after(attended, out_local)
+    branch_far, branch_near = halves(activated, down_mine, plain_dot, halves(attended, out_mine, plain_dot))
+    branch_got = after(other_core(branch_far), branch_near, *beside)
+    branch_parts = rank_parts(branch_near, branch_got)
+    branch_sum = RankSum(branch_parts)
     attended_grad = after(attended_grad, *branch_parts)
     mixed_grad = attend_back(heads, attended_grad, logsums, tables, length)
     normed = after(normed, mixed_grad)
     qkv_local = first_first(normed, mixed_grad).astype(bf16)
-    if one_each:
-        beside = out_local.reshape(nz, hw, -1, wide).transpose(0, 2, 1, 3).reshape(d, wide)
-        beside = jnp.concatenate([qkv_local, beside], axis=1)
-        own = line_sum(after(beside, up_own))
-        qkv_own = own[:, : 3 * rank_cols]
-        out_own = own[:, 3 * rank_cols :].reshape(-1, hw, wide).transpose(1, 0, 2).reshape(hw, d)
-    else:
-        qkv_own = line_sum(qkv_local)
-        out_own = line_sum(out_local) if spread else None
-    down_walk.got = [after(g, qkv_local) for g in down_walk.got]
-    down_own = down_walk.own()
-    branches = rank_sum(branch_parts, down_own)
-    mixed_grad = after(mixed_grad, down_own)
-    far, near = halves(mixed_grad, qkv_mine, last_last, back_more)
+    passed = branch_sum.middle(qkv_local)
+    hidden_grad, mixed_grad = after(hidden_grad, *passed), after(mixed_grad, *passed)
+    far, near = halves(hidden_grad, up_mine, last_last, halves(mixed_grad, qkv_mine, last_last))
     got = other_core(far)
-    down_pieces = plane_pieces(down_own, near)
-    up_both = both_cores(after(up_own, near))
-    grad_parts = rank_parts(near, after(got, up_both))
-    branches = after(branches, *grad_parts)
-    up_pieces = plane_pieces(up_both, *grad_parts)
-    normed_grad = rank_sum(grad_parts, branches)
-    up_pieces = [up_both] + [after(piece, normed_grad) for piece in up_pieces[1:]]
-    down_pieces = down_pieces[:1] + [after(piece, *grad_parts) for piece in down_pieces[1:]]
-    qkv_both = both_cores(qkv_own)
-    qkv_pieces = plane_pieces(qkv_both)
-    out_pieces = plane_pieces(after(out_own, qkv_both)) if spread else None
+    branches = branch_sum.total(near)
+    attn_local = pair_cores(after(qkv_local, near, branches))
+    attn_local = jnp.concatenate([attn_local] + beside, axis=1)
+    grad_parts = rank_parts(near, after(got, attn_local))
+    grad_sum = RankSum(grad_parts)
+    ff_own = [after(x, *grad_parts) for x in ff_own]
+    attn_own = line_sum(after(attn_local, *ff_own))
+    out_own = line_sum(out_local) if spread and not one_each else None
+    ff_pieces = [Pieces(x) for x in ff_own]
+    passed = grad_sum.middle(*ff_own)
+    normed_grad = grad_sum.total(*passed)
+    passed = [normed_grad] + [x for pieces in ff_pieces for x in pieces.middle(*passed)]
+    attn_pieces = Pieces(after(attn_own, *passed))
 
     token_rows = tokens[0].astype(f32)
     block_out = (token_rows + branches + outb + downb).astype(bf16)[None]
@@ -715,34 +782,19 @@
     upstream = cotangent[0].astype(f32)
     tokens_grad = (upstream + rows_grad).astype(bf16)[None]
 
-    if spread and one_each:
-        qkv_wgrad = place_heads(places, qkv_pieces, nz)
-    elif spread:
-        qkv_all = arrange([piece[None] for piece in qkv_pieces], bf16)
-        qkv_all = qkv_all.reshape(ns, CORES, rows, pairs, 3, PAIR).transpose(0, 1, 2, 4, 3, 5)
-        qkv_all = qkv_all.reshape(ns, CORES, rows, 3, nz, hw)
-        qkv_wgrad = qkv_all.transpose(2, 3, 4, 1, 0, 5).reshape(rows, 3 * d).astype(f32)
-    else:
-        qkv_all = arrange([piece[None] for piece in qkv_pieces], bf16)
-        qkv_all = qkv_all.reshape(ns, CORES, rows, pairs, 3, PAIR)
-        qkv_wgrad = qkv_all.transpose(2, 4, 0, 1, 3, 5).reshape(rows, 3 * d).astype(f32)
-    if spread:
-        out_wgrad = order_pieces(order_kernel, "place_out", places, out_pieces, dtype=f32)
-    else:
-        rank = CORES * s + k
-        out_padded = lax.dynamic_update_slice_in_dim(
-            jnp.zeros((d, d), bf16), out_local, rank * rank_cols, 0
-        )
-        out_shard = lax.psum_scatter(out_padded, "fsdp", scatter_dimension=0, tiled=True)
-        out_wgrad = lax.psum(out_shard.astype(f32), "seq")
-    if tiled:
-        up_wgrad = place_units(places, up_pieces, nz, w)
-    else:
-        up_all = arrange([piece[None] for piece in up_pieces], bf16)
-        up_all = up_all.reshape(ns, CORES, rows, nz, w)
-        up_wgrad = up_all.transpose(2, 3, 1, 0, 4).reshape(rows, ff).astype(f32)
-    down_wgrad = order_pieces(order_kernel, "place_down", places, down_pieces, dtype=f32)
-
+    def everyone_sum(sums):
+        flat = jnp.concatenate([v.reshape(nf, -1) for v in sums], axis=1)
+        flat = jnp.broadcast_to(flat[None], (ns,) + flat.shape).reshape(ns * nf, -1)
+        flat = lax.all_to_all(flat, everyone, split_axis=0, concat_axis=0, tiled=True)
+        flat = jnp.sum(flat, axis=0)
+        shards, at = [], 0
+        for v in sums:
+            size = v.shape[0] // nf
+            shards.append(flat[at : at + size])
+            at += size
+        return shards
+
+    mixed_grad, hidden_grad = after(mixed_grad, normed_grad), after(hidden_grad, normed_grad)
     mixed_sum = jnp.sum(mixed_grad.astype(f32), axis=0).reshape(pairs, 3, PAIR).transpose(1, 0, 2)
     if spread:
         mixed_sum = mixed_sum.reshape(3, nz, 1, 1, hw)
@@ -757,28 +809,47 @@
     hidden_full = lax.dynamic_update_slice(
         jnp.zeros((nz, CORES, ns, w), f32), hidden_sum, (0, k, s, 0)
     )
-    gain_local = jnp.sum(xhat * normed_grad, axis=0)
-    nbias_local = jnp.sum(normed_grad, axis=0)
-    c_local = jnp.sum(upstream, axis=0)
+    c_local = jnp.sum(after(cotangent[0], normed_grad).astype(f32), axis=0)
     sums = (
         mixed_full.reshape(-1)[: 2 * d],
         mixed_full.reshape(-1)[2 * d :],
         hidden_full.reshape(-1),
-        gain_local,
-        nbias_local,
         c_local,
+        jnp.sum(xhat * normed_grad, axis=0),
+        jnp.sum(normed_grad, axis=0),
     )
-    flat = jnp.concatenate([v.reshape(nf, -1) for v in sums], axis=1)
-    flat = jnp.broadcast_to(flat[None], (ns,) + flat.shape).reshape(ns * nf, -1)
-    flat = lax.all_to_all(flat, everyone, split_axis=0, concat_axis=0, tiled=True)
-    flat = jnp.sum(flat, axis=0)
-    shards, at = [], 0
-    for v in sums:
-        size = v.shape[0] // nf
-        shards.append(flat[at : at + size])
-        at += size
-    qkv_bgrad, value_bgrad, up_bgrad, gain_grad, norm_bgrad, out_bgrad = shards
-
+    bias_grads = everyone_sum(sums)
+    qkv_bgrad, value_bgrad, up_bgrad, out_bgrad, gain_grad, norm_bgrad = bias_grads
+
+    passed = attn_pieces.middle(tokens_grad, *bias_grads)
+    ff_pieces = [pieces.all(*passed) for pieces in ff_pieces]
+    up_pieces, down_pieces = ff_pieces[0], ff_pieces[-1]
+    if tiled:
+        up_wgrad = place_units(places, up_pieces, rows, nz, w)
+    else:
+        up_all = both_in_order(up_pieces).reshape(ns, rows, CORES, nz, w)
+        up_wgrad = up_all.transpose(1, 3, 2, 0, 4).reshape(rows, ff).astype(f32)
+    down_wgrad = order_pieces(order_kernel, "place_down", places, down_pieces, dtype=f32, size=w)
+
+    attn_pieces = attn_pieces.all(up_wgrad, down_wgrad)
+    out_pieces = plane_pieces(out_own) if spread and not one_each else None
+    if one_each:
+        qkv_wgrad = place_heads(places, attn_pieces, nz)
+        out_wgrad = place_out(places, attn_pieces, out_wide, hw, d)
+    elif spread:
+        qkv_all = both_in_order(attn_pieces).reshape(ns, rows, CORES, pairs, 3, PAIR)
+        qkv_all = qkv_all.transpose(0, 2, 1, 4, 3, 5).reshape(ns, CORES, rows, 3, nz, hw)
+        qkv_wgrad = qkv_all.transpose(2, 3, 4, 1, 0, 5).reshape(rows, 3 * d).astype(f32)
+        out_wgrad = order_pieces(order_kernel, "place_out", places, out_pieces, dtype=f32)
+    else:
+        qkv_all = both_in_order(attn_pieces).reshape(ns, rows, CORES, pairs, 3, PAIR)
+        qkv_wgrad = qkv_all.transpose(1, 4, 0, 2, 3, 5).reshape(rows, 3 * d).astype(f32)
+        rank = CORES * s + k
+        out_padded = lax.dynamic_update_slice_in_dim(
+            jnp.zeros((d, d), bf16), out_local, rank * rank_cols, 0
+        )
+        out_shard = lax.psum_scatter(out_padded, "fsdp", scatter_dimension=0, tiled=True)
+        out_wgrad = lax.psum(out_shard.astype(f32), "seq")
     return (
         block_out,
         tokens_grad,

time: 611 us -> 582 us (0.953)
  starting transfers between devices: 60.2 us -> 35.1 us
  Pallas kernels: 97.9 us -> 86 us
  local copies, waits for them, and re-layouts: 28.8 us -> 40 us
    all_to_all x1, waiting for transfers between devices: 0.01 us -> 39.9 us  [everyone_sum(): lax.all_to_all(flat, everyone, split_axis=0, concat_axis=0, tiled=True)]
    ppermute x6 -> x0, waiting for transfers between devices: 22.2 us -> none  [step_line(): return lax.ppermute(part, 'fsdp', hops_)]
    ppermute x6 -> x0, starting transfers between devices: 17.7 us -> none  [step_line(): return lax.ppermute(part, 'fsdp', hops_)]
    ppermute x24 -> x18, waiting for transfers between devices: 129 us -> 112 us  [plane_hop(): return lax.ppermute(x, everyone, hops)]
    pallas_call x4 -> x3, Pallas kernels: 40.9 us -> 25.3 us  [order_pieces(): pl.pallas_call(kernel, grid_spec=pltpu.PrefetchScalarGridSpec(num_scalar_...]
    all_gather x3 -> x2, waiting for transfers between devices: 64.9 us -> 52.2 us  [the longest x1 52.1 us: on_device(): lax.all_gather(jnp.concatenate([up_part, down_part]), 'fsdp', axis=0, til...]
    convert_element_type x5 -> x2, other arithmetic: 14.2 us -> 1.99 us  [middle(): self.rest = (self.parts[2].astype(f32) + across.astype(f32)).astype(bf16)]
    concatenate x2 -> x4, other arithmetic: 3.72 us -> 14.5 us  [the longest x1 7.15 us: on_device(): ff_local = [jnp.concatenate(ff_local, axis=1).reshape(-1, d)]]
  transfers between devices with their start and end apart: 50 -> 36, of which waited for: 20 -> 15; matrix products, arithmetic and copies ran while one was open for 34% -> 36% of each run, Pallas kernels for 14% -> 13%
where the time goes in v3:
time: 582 us; the launch traced here: 573 us
  waiting for transfers between devices  218 us (37%)
  matrix products  130 us (22%)
  Pallas kernels  86 us (15%)
  other arithmetic  48.9 us (8%)
  local copies, waits for them, and re-layouts  40 us (7%)
  starting transfers between devices  35.1 us (6%)
  between operations  15 us (3%)
    ppermute x18, waiting for transfers between devices, plane_hop(): return lax.ppermute(x, everyone, hops)  112 us
    all_gather x1, waiting for transfers between devices, on_device(): lax.all_gather(jnp.concatenate([up_part, down_part]), 'fsdp', axis=0, til...  52.1 us
    dot_general x6, matrix products, last_last(): lax.dot_general(left, right, (((1,), (1,)), ((), ())), preferred_element_...  50.7 us
    dot_general x6, matrix products, plain_dot(): return jnp.dot(left, right, preferred_element_type=f32)  44.1 us
    all_to_all x1, waiting for transfers between devices, everyone_sum(): lax.all_to_all(flat, everyone, split_axis=0, concat_axis=0, tiled=True)  39.9 us
    dot_general x4, matrix products, first_first(): lax.dot_general(left, right, (((0,), (0,)), ((), ())), preferred_element_...  35.7 us
    pallas_call x3, Pallas kernels, order_pieces(): pl.pallas_call(kernel, grid_spec=pltpu.PrefetchScalarGridSpec(num_scalar_...  25.3 us
    ppermute x18, starting transfers between devices, plane_hop(): return lax.ppermute(x, everyone, hops)  24.6 us
  transfers between devices with their start and end apart: 36, of which 15 were waited for; matrix products, arithmetic and copies ran while one was open for 36% of the time, Pallas kernels for 13%

profile of v3, /device:TPU:0, one launch (start us, length us, event | category | flops | bytes accessed | tf_op | source)
XLA Modules:
  0.0 573.1 jit_solution(16663077480655549702)
XLA Ops:
  31.7 10.5 %collective-permute-done.1.refs_2_ = bf16[256,2048]{1,0:T(8,128)(2,1)} collective-permute-done((bf16[256,2048]{1,0:T(8,128)(2,1)S(1)}, bf16[256,2048]{1,0:T(8,128)(2,1)}, u32[]{:S(2)}, u32[]{:S(2)}) %collective-permute-start.1) | collective-permute-done | bytes 1048608 | tf_op jit(solution)/shard_map/ppermute | solution.py:495
  50.5 7.3 %collective-permute-done.2.refs_3_ = bf16[256,2048]{1,0:T(8,128)(2,1)} collective-permute-done((bf16[256,2048]{1,0:T(8,128)(2,1)}, bf16[256,2048]{1,0:T(8,128)(2,1)}, u32[]{:S(2)}, u32[]{:S(2)}) %collective-permute-start.2) | collective-permute-done | bytes 1048608 | tf_op jit(solution)/shard_map/ppermute | solution.py:495
  61.1 21.4 %collective-permute-done.8.refs_2_ = bf16[256,2048]{1,0:T(8,128)(2,1)S(1)} collective-permute-done((bf16[256,2048]{1,0:T(8,128)(2,1)S(1)}, bf16[256,2048]{1,0:T(8,128)(2,1)S(1)}, u32[]{:S(2)}, u32[]{:S(2)}) %collective-permute-start.8) | collective-permute-done | bytes 1048608 | tf_op jit(solution)/shard_map/ppermute | solution.py:495
  88.7 11.5 %norm_both.1 = bf16[2048,2048]{1,0:T(8,128)(2,1)} custom-call(s32[8]{0:T(128)S(1)} %concatenate.36.places_ref, f32[1,2048]{1,0:T(1,128)S(1)} %bitcast.121, f32[1,2048]{1,0:T(1,128)S(1)} %bitcast.120, bf16[256,2048]{1,0:T(8,128)(2,1)S(1)} %bitcast.114, bf16[256,2048]{1,0:T(8,128)(2,1)} %collective-permute-done.refs_1_, ...), custom_call_target="tpu_custom_call" | custom-call | tf_op jit(solution)/shard_map/norm_both/pallas_call | solution.py:236
  110.6 7.8 %order_both.1 = bf16[2048,2048]{1,0:T(8,128)(2,1)} custom-call(s32[8]{0:T(128)S(1)} %concatenate.36.places_ref, bf16[256,2048]{1,0:T(8,128)(2,1)S(1)} %bitcast.118, bf16[256,2048]{1,0:T(8,128)(2,1)} %collective-permute-done.7.refs_1_, bf16[256,2048]{1,0:T(8,128)(2,1)S(1)} %copy-done.8, bf16[256,2048]{1,0:T(8,128)(2,1)} %collective-permute-done.9.refs_3_, ...), custom_call_target="tpu_custom_call" | custom-call | tf_op jit(solution)/shard_map/order_both/pallas_call | solution.py:236
  118.4 52.1 %all-gather.3.cloned.1.call-done = bf16[4096,2048]{1,0:T(8,128)(2,1)} async-done(((bf16[512,2048]{1,0:T(8,128)(2,1)}), bf16[4096,2048]{1,0:T(8,128)(2,1)}) %all-gather.3.cloned.1.call-update) | async-done | bytes 16777232 | tf_op jit(solution)/shard_map/all_gather | solution.py:576
  170.5 10.1 %fusion.53 = (bf16[4,2,256,2048]{3,2,1,0:T(8,128)(2,1)S(1)}, bf16[4,2,256,2048]{3,2,1,0:T(8,128)(2,1)}) fusion(bf16[4,2,512,2048]{3,2,1,0:T(8,128)(2,1)} %bitcast.127), kind=kLoop, calls=%fused_computation.133 | loop fusion | bytes 33554432 | tf_op jit(solution)/shard_map/slice | solution.py:711
  180.6 16.1 %multiply_convert_fusion.1 = (bf16[2048,1024]{1,0:T(8,128)(2,1)S(1)}, f32[2048,1024]{1,0:T(8,128)}) fusion(f32[1024]{0:T(1024)S(1)} %bitcast.168, bf16[2048,2048]{1,0:T(8,128)(2,1)} %norm_both.1, bf16[2048,2048]{1,0:T(8,128)(2,1)} %bitcast.133, s32[]{:T(128)S(6)} %select_n.186), kind=kOutput, calls=%fused_computation.7 | convolution fusion | flops 8610906112 | bytes 25169924 | tf_op jit(solution)/shard_map/dot_general | solution.py:50
  196.7 10.7 %convolution_convert_fusion = bf16[1024,2048]{1,0:T(8,128)(2,1)} fusion(bf16[2048,1024]{1,0:T(8,128)(2,1)S(1)} %get-tuple-element.78, bf16[2048,2048]{1,0:T(8,128)(2,1)S(1)} %bitcast.123), kind=kOutput, calls=%fused_computation.12 | convolution fusion | flops 8592031744 | bytes 16777216 | tf_op jit(solution)/shard_map/dot_general | solution.py:612
  209.8 17.2 %multiply_convert_fusion = bf16[2048,1024]{1,0:T(8,128)(2,1)S(1)} fusion(f32[2048,1024]{1,0:T(8,128)} %get-tuple-element.145, bf16[2048,2048]{1,0:T(8,128)(2,1)S(1)} %bitcast.123, bf16[1024,2048]{1,0:T(8,128)(2,1)} %bitcast.139, f32[1024]{0:T(1024)S(1)} %bitcast.169), kind=kOutput, calls=%fused_computation.6 | convolution fusion | flops 8629780480 | bytes 25169920 | tf_op jit(solution)/shard_map/dot_general | solution.py:46
  227.1 13.1 %convolution_convert_fusion.1 = bf16[2048,1024]{1,0:T(8,128)(2,1)S(1)} fusion(bf16[2048,2048]{1,0:T(8,128)(2,1)} %norm_both.1, bf16[2048,1024]{1,0:T(8,128)(2,1)S(1)} %multiply_convert_fusion), kind=kOutput, calls=%fused_computation.13 | convolution fusion | flops 8592031744 | bytes 16777216 | tf_op jit(solution)/shard_map/dot_general | solution.py:612
  258.4 11.4 %broadcast_add_fusion.mixed_ref = f32[2048,768]{1,0:T(8,128)S(1)} fusion(f32[768]{0:T(1024)S(1)} %fusion.46, bf16[2048,2048]{1,0:T(8,128)(2,1)} %norm_both.1, bf16[2048,2048]{1,0:T(8,128)(2,1)} %all-gather.5.cloned.1.call-done, s32[]{:T(128)S(6)} %select_n.188), kind=kOutput, calls=%fused_computation.19 | convolution fusion | flops 6444023808 | bytes 17828868 | tf_op jit(solution)/shard_map/dot_general | solution.py:50
  269.8 15.3 %attend.1 = (bf16[2048,768]{1,0:T(8,128)(2,1)S(1)}, bf16[2048,256]{1,0:T(8,128)(2,1)S(1)}, f32[2,2,2,1024]{3,2,1,0:T(2,128)S(1)}) custom-call(f32[2048,768]{1,0:T(8,128)S(1)} %broadcast_add_fusion.mixed_ref, f32[1024,128]{1,0:T(8,128)S(1)} %copy-done.15, f32[1024,128]{1,0:T(8,128)S(1)} %copy-done.13, f32[1024,128]{1,0:T(8,128)S(1)} %copy-done.11), custom_call_target="tpu_custom_call" | custom-call | flops 2147483648 | bytes 12582912 | tf_op jit(solution)/shard_map/attend/pallas_call | solution.py:150
  293.9 7.9 %add_convert_fusion.2 = bf16[1024,2048]{1,0:T(8,128)(2,1)} fusion(bf16[1024,2048]{1,0:T(8,128)(2,1)S(1)} %fusion.36, bf16[1024,2048]{1,0:T(8,128)(2,1)S(1)} %bitcast.140, bf16[2048,1024]{1,0:T(8,128)(2,1)} %copy-done.41), kind=kOutput, calls=%fused_computation.4 | convolution fusion | flops 4301258752 | bytes 14680064 | tf_op jit(solution)/shard_map/dot_general | solution.py:50
  321.7 20.4 %attend_back.1 = bf16[2048,768]{1,0:T(8,128)(2,1)S(1)} custom-call(bf16[2048,768]{1,0:T(8,128)(2,1)S(1)} %copy-done.19, bf16[2048,256]{1,0:T(8,128)(2,1)S(1)} %copy-done.20, f32[2,2,2,1024]{3,2,1,0:T(2,128)S(1)} %get-tuple-element.83.logsum_ref, f32[1024,128]{1,0:T(8,128)S(1)} %copy-done.16, f32[1024,128]{1,0:T(8,128)S(1)} %copy-done.14, ...), custom_call_target="tpu_custom_call" | custom-call | flops 5368709120 | bytes 9437184 | tf_op jit(solution)/shard_map/attend_back/pallas_call | solution.py:180
  342.1 8.5 %convolution_convert_fusion.2 = bf16[2048,768]{1,0:T(8,128)(2,1)} fusion(bf16[2048,2048]{1,0:T(8,128)(2,1)S(1)} %bitcast.132, bf16[2048,768]{1,0:T(8,128)(2,1)S(1)} %attend_back.1), kind=kOutput, calls=%fused_computation.14 | convolution fusion | flops 6444023808 | bytes 14680064 | tf_op jit(solution)/shard_map/dot_general | solution.py:612
  358.1 8.5 %add_convert_fusion = bf16[1024,2048]{1,0:T(8,128)(2,1)} fusion(bf16[1024,2048]{1,0:T(8,128)(2,1)S(1)} %fusion.9, bf16[2048,2048]{1,0:T(8,128)(2,1)} %bitcast.134, s32[]{:T(128)S(6)} %select_n.186, bf16[2048,1024]{1,0:T(8,128)(2,1)S(1)} %copy-done.24), kind=kOutput, calls=%fused_computation.2 | convolution fusion | flops 4301258752 | bytes 14680068 | tf_op jit(solution)/shard_map/dot_general | solution.py:46
  367.8 7.5 %fusion.11 = bf16[1024,2048]{1,0:T(8,128)(2,1)} fusion(bf16[2048,2048]{1,0:T(8,128)(2,1)} %all-gather.5.cloned.1.call-done, s32[]{:T(128)S(6)} %select_n.188, bf16[2048,768]{1,0:T(8,128)(2,1)S(1)} %attend_back.1), kind=kOutput, calls=%fused_computation.32 | convolution fusion | flops 3221225472 | bytes 8912900 | tf_op jit(solution)/shard_map/dot_general | solution.py:46
  375.3 8.4 %add_convert_fusion.1 = bf16[1024,2048]{1,0:T(8,128)(2,1)} fusion(bf16[1024,2048]{1,0:T(8,128)(2,1)} %fusion.11, bf16[2048,2048]{1,0:T(8,128)(2,1)S(1)} %bitcast.137, s32[]{:T(128)S(6)} %select_n.186, bf16[2048,1024]{1,0:T(8,128)(2,1)} %copy-done.23), kind=kOutput, calls=%fused_computation.3 | convolution fusion | flops 4301258752 | bytes 14680068 | tf_op jit(solution)/shard_map/dot_general | solution.py:46
  402.2 13.0 %collective-permute-done.22 = bf16[256,2048]{1,0:T(8,128)(2,1)S(1)} collective-permute-done((bf16[256,2048]{1,0:T(8,128)(2,1)}, bf16[256,2048]{1,0:T(8,128)(2,1)S(1)}, u32[]{:S(2)}, u32[]{:S(2)}) %collective-permute-start.22) | collective-permute-done | bytes 1048608 | tf_op jit(solution)/shard_map/ppermute | solution.py:495
  415.2 11.2 %collective-permute-done.21 = bf16[256,2048]{1,0:T(8,128)(2,1)S(1)} collective-permute-done((bf16[256,2048]{1,0:T(8,128)(2,1)}, bf16[256,2048]{1,0:T(8,128)(2,1)S(1)}, u32[]{:S(2)}, u32[]{:S(2)}) %collective-permute-start.21) | collective-permute-done | bytes 1048608 | tf_op jit(solution)/shard_map/ppermute | solution.py:495
  430.2 22.7 %collective-permute-done.23 = bf16[256,2048]{1,0:T(8,128)(2,1)S(1)} collective-permute-done((bf16[256,2048]{1,0:T(8,128)(2,1)S(1)}, bf16[256,2048]{1,0:T(8,128)(2,1)S(1)}, u32[]{:S(2)}, u32[]{:S(2)}) %collective-permute-start.23) | collective-permute-done | bytes 1048608 | tf_op jit(solution)/shard_map/ppermute | solution.py:495
  460.6 26.2 %collective-permute-done.25.refs_2_ = bf16[512,2048]{1,0:T(8,128)(2,1)} collective-permute-done((bf16[512,2048]{1,0:T(8,128)(2,1)}, bf16[512,2048]{1,0:T(8,128)(2,1)}, u32[]{:S(2)}, u32[]{:S(2)}) %collective-permute-start.25) | collective-permute-done | bytes 2097184 | tf_op jit(solution)/shard_map/ppermute | solution.py:495
  498.1 39.9 %all-to-all-done.1 = f32[32,1,2560]{2,1,0:T(1,128)S(1)} async-done(((f32[32,1,2560]{2,1,0:T(1,128)}), f32[32,1,2560]{2,1,0:T(1,128)S(1)}, u32[]{:S(2)}, u32[]{:S(2)}) %all-to-all-start.1) | async-done | bytes 327712 | tf_op jit(solution)/shard_map/all_to_all | solution.py:788
  (286 shorter events, 179.3 us)
Async XLA Ops:
  7.2 163.3 %all-gather.3.cloned.1.call-start = ((), (), s32[]{:S(2)}) async-start(), calls=%async_computation.4 | async-start | bytes 18874368 | tf_op jit(solution)/shard_map/all_gather | solution.py:576
  15.6 26.6 %collective-permute-start.1 = (bf16[256,2048]{1,0:T(8,128)(2,1)S(1)}, bf16[256,2048]{1,0:T(8,128)(2,1)}, u32[]{:S(2)}, u32[]{:S(2)}) collective-permute-start(bf16[256,2048]{1,0:T(8,128)(2,1)S(1)} %bitcast.111), channel_id=1, source_target_pairs={{0,16},{1,9},{2,18},{3,11},{4,20},{5,13},{6,22},{7,15},{8,24},{9,1... | collective-permute-start | bytes 3145736 | tf_op jit(solution)/shard_map/ppermute | solution.py:495
  18.7 23.6 %collective-permute-start = (bf16[256,2048]{1,0:T(8,128)(2,1)S(1)}, bf16[256,2048]{1,0:T(8,128)(2,1)}, u32[]{:S(2)}, u32[]{:S(2)}) collective-permute-start(bf16[256,2048]{1,0:T(8,128)(2,1)S(1)} %bitcast.112), channel_id=1, source_target_pairs={{0,8},{1,17},{2,10},{3,19},{4,12},{5,21},{6,14},{7,23},{8,0},{9,25... | collective-permute-start | bytes 3145736 | tf_op jit(solution)/shard_map/ppermute | solution.py:495
  23.5 25.3 %all-to-all-start = ((bf16[8,2,1408]{2,1,0:T(2,128)(2,1)}), bf16[8,2,1408]{2,1,0:T(2,128)(2,1)S(1)}, u32[]{:S(2)}, u32[]{:S(2)}) async-start(bf16[8,2,1408]{2,1,0:T(2,128)(2,1)} %reshape.275), calls=%async_computation | async-start | bytes 90112 | tf_op jit(solution)/shard_map/all_to_all | solution.py:542
  28.4 226.2 %all-gather.5.cloned.1.call-start = ((), (), s32[]{:S(2)}) async-start(), calls=%async_computation.5 | async-start | bytes 9437184 | tf_op jit(solution)/shard_map/all_gather | solution.py:601
  57.8 24.7 %collective-permute-start.8 = (bf16[256,2048]{1,0:T(8,128)(2,1)S(1)}, bf16[256,2048]{1,0:T(8,128)(2,1)S(1)}, u32[]{:S(2)}, u32[]{:S(2)}) collective-permute-start(bf16[256,2048]{1,0:T(8,128)(2,1)S(1)} %bitcast.115), channel_id=1, source_target_pairs={{0,16},{1,9},{2,18},{3,11},{4,20},{5,13},{6,22},{7,15},{8,24},{9,1... | collective-permute-start | bytes 3145736 | tf_op jit(solution)/shard_map/ppermute | solution.py:495
  59.9 22.7 %collective-permute-start.7 = (bf16[256,2048]{1,0:T(8,128)(2,1)S(1)}, bf16[256,2048]{1,0:T(8,128)(2,1)}, u32[]{:S(2)}, u32[]{:S(2)}) collective-permute-start(bf16[256,2048]{1,0:T(8,128)(2,1)S(1)} %bitcast.116), channel_id=1, source_target_pairs={{0,8},{1,17},{2,10},{3,19},{4,12},{5,21},{6,14},{7,23},{8,0},{9,25... | collective-permute-start | bytes 3145736 | tf_op jit(solution)/shard_map/ppermute | solution.py:495
  60.6 28.1 %collective-permute-start.3 = (bf16[256,2048]{1,0:T(8,128)(2,1)S(1)}, bf16[256,2048]{1,0:T(8,128)(2,1)}, u32[]{:S(2)}, u32[]{:S(2)}) collective-permute-start(bf16[256,2048]{1,0:T(8,128)(2,1)S(1)} %bitcast.113), channel_id=1, source_target_pairs={{0,1},{1,0},{2,3},{3,2},{4,5},{5,4},{6,7},{7,6},{8,9},{9,8},{10,11... | collective-permute-start | bytes 3145736 | tf_op jit(solution)/shard_map/ppermute | solution.py:483
  60.6 28.1 %collective-permute-start.4 = (bf16[256,2048]{1,0:T(8,128)(2,1)}, bf16[256,2048]{1,0:T(8,128)(2,1)}, u32[]{:S(2)}, u32[]{:S(2)}) collective-permute-start(bf16[256,2048]{1,0:T(8,128)(2,1)} %collective-permute-done.refs_1_), channel_id=1, source_target_pairs={{0,1},{1,0},{2,3},{3,2},{4,5},{5,4},{6,7},{7,6},{8,9},{9,8},{10,11... | collective-permute-start | bytes 3145736 | tf_op jit(solution)/shard_map/ppermute | solution.py:483
  61.1 27.6 %collective-permute-start.5 = (bf16[256,2048]{1,0:T(8,128)(2,1)}, bf16[256,2048]{1,0:T(8,128)(2,1)}, u32[]{:S(2)}, u32[]{:S(2)}) collective-permute-start(bf16[256,2048]{1,0:T(8,128)(2,1)} %collective-permute-done.1.refs_2_), channel_id=1, source_target_pairs={{0,1},{1,0},{2,3},{3,2},{4,5},{5,4},{6,7},{7,6},{8,9},{9,8},{10,11... | collective-permute-start | bytes 3145736 | tf_op jit(solution)/shard_map/ppermute | solution.py:483
  82.5 18.7 %collective-permute-start.9 = (bf16[256,2048]{1,0:T(8,128)(2,1)}, bf16[256,2048]{1,0:T(8,128)(2,1)}, u32[]{:S(2)}, u32[]{:S(2)}) collective-permute-start(bf16[256,2048]{1,0:T(8,128)(2,1)} %collective-permute-done.7.refs_1_), channel_id=1, source_target_pairs={{0,16},{1,9},{2,18},{3,11},{4,20},{5,13},{6,22},{7,15},{8,24},{9,1... | collective-permute-start | bytes 3145736 | tf_op jit(solution)/shard_map/ppermute | solution.py:495
  100.3 299.8 %reduce-scatter.3.cloned.1.call-start = ((), (), s32[]{:S(2)}) async-start(), calls=%async_computation.6 | async-start | bytes 10485760 | tf_op jit(solution)/shard_map/reduce_scatter | solution.py:702
  254.3 233.4 %reduce-scatter.5.cloned.1.call-start = ((), (), s32[]{:S(2)}) async-start(), calls=%async_computation.7 | async-start | bytes 5242880 | tf_op jit(solution)/shard_map/reduce_scatter | solution.py:702
  319.6 31.1 %collective-permute-start.17 = (bf16[256,2048]{1,0:T(8,128)(2,1)}, bf16[256,2048]{1,0:T(8,128)(2,1)}, u32[]{:S(2)}, u32[]{:S(2)}) collective-permute-start(bf16[256,2048]{1,0:T(8,128)(2,1)} %get-tuple-element.123), channel_id=1, source_target_pairs={{0,8},{1,17},{2,10},{3,19},{4,12},{5,21},{6,14},{7,23},{8,0},{9,25... | collective-permute-start | bytes 3145736 | tf_op jit(solution)/shard_map/ppermute | solution.py:495
  320.7 30.0 %collective-permute-start.16 = (bf16[256,2048]{1,0:T(8,128)(2,1)}, bf16[256,2048]{1,0:T(8,128)(2,1)}, u32[]{:S(2)}, u32[]{:S(2)}) collective-permute-start(bf16[256,2048]{1,0:T(8,128)(2,1)} %get-tuple-element.124), channel_id=1, source_target_pairs={{0,8},{1,17},{2,10},{3,19},{4,12},{5,21},{6,14},{7,23},{8,0},{9,25... | collective-permute-start | bytes 3145736 | tf_op jit(solution)/shard_map/ppermute | solution.py:495
  366.5 26.6 %collective-permute-start.19 = (bf16[1024,2048]{1,0:T(8,128)(2,1)}, bf16[1024,2048]{1,0:T(8,128)(2,1)}, u32[]{:S(2)}, u32[]{:S(2)}) collective-permute-start(bf16[1024,2048]{1,0:T(8,128)(2,1)} %add_convert_fusion), channel_id=1, source_target_pairs={{0,1},{1,0},{2,3},{3,2},{4,5},{5,4},{6,7},{7,6},{8,9},{9,8},{10,11... | collective-permute-start | bytes 12582920 | tf_op jit(solution)/shard_map/ppermute | solution.py:483
  401.4 25.0 %collective-permute-start.21 = (bf16[256,2048]{1,0:T(8,128)(2,1)}, bf16[256,2048]{1,0:T(8,128)(2,1)S(1)}, u32[]{:S(2)}, u32[]{:S(2)}) collective-permute-start(bf16[256,2048]{1,0:T(8,128)(2,1)} %get-tuple-element.120), channel_id=1, source_target_pairs={{0,8},{1,17},{2,10},{3,19},{4,12},{5,21},{6,14},{7,23},{8,0},{9,25... | collective-permute-start | bytes 3145736 | tf_op jit(solution)/shard_map/ppermute | solution.py:495
  426.9 26.0 %collective-permute-start.23 = (bf16[256,2048]{1,0:T(8,128)(2,1)S(1)}, bf16[256,2048]{1,0:T(8,128)(2,1)S(1)}, u32[]{:S(2)}, u32[]{:S(2)}) collective-permute-start(bf16[256,2048]{1,0:T(8,128)(2,1)S(1)} %add_convert_fusion.4), channel_id=1, source_target_pairs={{0,16},{1,9},{2,18},{3,11},{4,20},{5,13},{6,22},{7,15},{8,24},{9,1... | collective-permute-start | bytes 3145736 | tf_op jit(solution)/shard_map/ppermute | solution.py:495
  427.9 58.9 %collective-permute-start.25 = (bf16[512,2048]{1,0:T(8,128)(2,1)}, bf16[512,2048]{1,0:T(8,128)(2,1)}, u32[]{:S(2)}, u32[]{:S(2)}) collective-permute-start(bf16[512,2048]{1,0:T(8,128)(2,1)} %reduce-scatter.3.cloned.1.call-done.refs_0_), channel_id=1, source_target_pairs={{0,16},{1,9},{2,18},{3,11},{4,20},{5,13},{6,22},{7,15},{8,24},{9,1... | collective-permute-start | bytes 6291464 | tf_op jit(solution)/shard_map/ppermute | solution.py:495
  428.9 57.8 %collective-permute-start.24 = (bf16[512,2048]{1,0:T(8,128)(2,1)}, bf16[512,2048]{1,0:T(8,128)(2,1)}, u32[]{:S(2)}, u32[]{:S(2)}) collective-permute-start(bf16[512,2048]{1,0:T(8,128)(2,1)} %reduce-scatter.3.cloned.1.call-done.refs_0_), channel_id=1, source_target_pairs={{0,8},{1,17},{2,10},{3,19},{4,12},{5,21},{6,14},{7,23},{8,0},{9,25... | collective-permute-start | bytes 6291464 | tf_op jit(solution)/shard_map/ppermute | solution.py:495
  486.8 54.5 %collective-permute-start.28 = (bf16[512,2048]{1,0:T(8,128)(2,1)}, bf16[512,2048]{1,0:T(8,128)(2,1)}, u32[]{:S(2)}, u32[]{:S(2)}) collective-permute-start(bf16[512,2048]{1,0:T(8,128)(2,1)} %collective-permute-done.24.refs_1_), channel_id=1, source_target_pairs={{0,16},{1,9},{2,18},{3,11},{4,20},{5,13},{6,22},{7,15},{8,24},{9,1... | collective-permute-start | bytes 6291464 | tf_op jit(solution)/shard_map/ppermute | solution.py:495
  487.7 52.3 %collective-permute-start.27 = (bf16[256,2048]{1,0:T(8,128)(2,1)}, bf16[256,2048]{1,0:T(8,128)(2,1)S(1)}, u32[]{:S(2)}, u32[]{:S(2)}) collective-permute-start(bf16[256,2048]{1,0:T(8,128)(2,1)} %reduce-scatter.5.cloned.1.call-done.refs_0_), channel_id=1, source_target_pairs={{0,16},{1,9},{2,18},{3,11},{4,20},{5,13},{6,22},{7,15},{8,24},{9,1... | collective-permute-start | bytes 3145736 | tf_op jit(solution)/shard_map/ppermute | solution.py:495
  488.8 51.2 %collective-permute-start.26 = (bf16[256,2048]{1,0:T(8,128)(2,1)}, bf16[256,2048]{1,0:T(8,128)(2,1)}, u32[]{:S(2)}, u32[]{:S(2)}) collective-permute-start(bf16[256,2048]{1,0:T(8,128)(2,1)} %reduce-scatter.5.cloned.1.call-done.refs_0_), channel_id=1, source_target_pairs={{0,8},{1,17},{2,10},{3,19},{4,12},{5,21},{6,14},{7,23},{8,0},{9,25... | collective-permute-start | bytes 3145736 | tf_op jit(solution)/shard_map/ppermute | solution.py:495
  491.1 46.9 %all-to-all-start.1 = ((f32[32,1,2560]{2,1,0:T(1,128)}), f32[32,1,2560]{2,1,0:T(1,128)S(1)}, u32[]{:S(2)}, u32[]{:S(2)}) async-start(f32[32,1,2560]{2,1,0:T(1,128)} %all_to_all.14), calls=%async_computation.3 | async-start | bytes 655360 | tf_op jit(solution)/shard_map/all_to_all | solution.py:788
  (63 other events, 909.7 us)
Sparse Core Ops, SparseCore 0:
  15.7 154.7 all-gather.2
  172.7 79.3 all-gather.4
  254.5 142.9 reduce-scatter.2
  400.2 77.4 reduce-scatter.4

commit v4 on v3

--- a/solution.py
+++ b/solution.py
@@ -205,8 +205,9 @@
     )(heads, grad, logsums, *tables)
 
 
-def norm_kernel(places_ref, gain_ref, bias_ref, *refs):
-    *pieces, out_ref = refs
+def norm_kernel(rows, places_ref, gain_ref, bias_ref, *refs):
+    *pieces, out_ref, near_ref, far_ref = refs
+    core = places_ref[len(pieces)]
     for i, piece in enumerate(pieces):
 
         @pl.when(pl.program_id(0) == i)
@@ -217,6 +218,38 @@
             out_ref[...] = (
                 centred * lax.rsqrt(variance + epsilon) * gain_ref[...] + bias_ref[...]
             ).astype(bf16)
+
+    for q in range(near_ref.shape[1] // rows):
+        for side, half_ref in ((core, near_ref), (1 - core, far_ref)):
+            at = pl.multiple_of((q * CORES + side) * rows, rows)
+            half_ref[:, q * rows : (q + 1) * rows] = out_ref[:, pl.ds(at, rows)]
+
+
+def norm_pieces(places, pieces, gain, bias, rows):
+    local, d = pieces[0].shape
+    fixed = lambda i, places: (0, 0)
+    there = lambda i, places: (places[i], 0)
+    count = len(pieces) * local
+    return pl.pallas_call(
+        functools.partial(norm_kernel, rows),
+        grid_spec=pltpu.PrefetchScalarGridSpec(
+            num_scalar_prefetch=1,
+            grid=(len(pieces),),
+            in_specs=[pl.BlockSpec((1, d), fixed)] * 2 + [pl.BlockSpec((local, d), fixed)] * len(pieces),
+            out_specs=[
+                pl.BlockSpec((local, d), there),
+                pl.BlockSpec((local, d // CORES), there),
+                pl.BlockSpec((local, d // CORES), there),
+            ],
+        ),
+        out_shape=[
+            jax.ShapeDtypeStruct((count, d), bf16),
+            jax.ShapeDtypeStruct((count, d // CORES), bf16),
+            jax.ShapeDtypeStruct((count, d // CORES), bf16),
+        ],
+        compiler_params=pltpu.CompilerParams(vmem_limit_bytes=48 * 1024 * 1024),
+        name="norm_pieces",
+    )(places, gain[None], bias[None], *pieces)
 
 
 def order_kernel(places_ref, *refs):
@@ -425,6 +458,80 @@
         out_shape=jax.ShapeDtypeStruct((len(pieces) * hw, d), f32),
         name="place_out",
     )(places, *pieces)
+
+
+def pack_kernel(near_ref, got_ref, out_ref, packed_ref):
+    width = near_ref.shape[1]
+    hw = out_ref.shape[0]
+    wide = packed_ref.shape[1] - 2 * width
+    packed_ref[:, :width] = near_ref[...]
+    packed_ref[:, width : 2 * width] = got_ref[...]
+    for i in range(out_ref.shape[1] // wide):
+        packed_ref[i * hw : (i + 1) * hw, 2 * width :] = out_ref[:, i * wide : (i + 1) * wide]
+
+
+def pack(near, got, out_local, rows, hw):
+    count, width = near.shape
+    d = out_local.shape[1]
+    whole = 2 * width + d * hw // rows
+    half = pl.BlockSpec((rows, width), lambda i: (i, 0))
+    return pl.pallas_call(
+        pack_kernel,
+        grid=(count // rows,),
+        in_specs=[half, half, pl.BlockSpec((hw, d), lambda i: (i, 0))],
+        out_specs=pl.BlockSpec((rows, whole), lambda i: (i, 0)),
+        out_shape=jax.ShapeDtypeStruct((count, whole), bf16),
+        name="pack",
+    )(near, got, out_local)
+
+
+def two_products_kernel(first_ref, first_right_ref, second_ref, second_right_ref, far_ref, near_ref):
+    def products(out_ref):
+        width = out_ref.shape[1]
+        step = min(512, width)
+        for at in range(0, width, step):
+            columns = slice(at, at + step)
+            out_ref[:, columns] = (
+                last_last(first_ref[...], first_right_ref[columns, :])
+                + last_last(second_ref[...], second_right_ref[columns, :])
+            ).astype(bf16)
+
+    half = pl.num_programs(0) // 2
+    pl.when(pl.program_id(0) < half)(lambda: products(far_ref))
+    pl.when(pl.program_id(0) >= half)(lambda: products(near_ref))
+
+
+def two_products(first, first_right, second, second_right):
+    rows = first.shape[0] // 2
+    block = min(512, rows)
+    half = rows // block
+    width = first_right.shape[0]
+
+    def left(x):
+        return pl.BlockSpec((block, x.shape[1]), lambda i: (lax.rem(i + half, 2 * half), 0))
+
+    def right(x):
+        return pl.BlockSpec(x.shape, lambda i: (0, 0))
+
+    depth = first.shape[1] + second.shape[1]
+    out = jax.ShapeDtypeStruct((rows, width), bf16)
+    return pl.pallas_call(
+        two_products_kernel,
+        grid=(2 * half,),
+        in_specs=[left(first), right(first_right), left(second), right(second_right)],
+        out_specs=[
+            pl.BlockSpec((block, width), lambda i: (jnp.minimum(i, half - 1), 0)),
+            pl.BlockSpec((block, width), lambda i: (jnp.maximum(i - half, 0), 0)),
+        ],
+        out_shape=[out, out],
+        compiler_params=pltpu.CompilerParams(vmem_limit_bytes=48 * 1024 * 1024),
+        cost_estimate=pl.CostEstimate(
+            flops=4 * rows * width * depth,
+            bytes_accessed=2 * (2 * rows + width) * depth + 4 * rows * width,
+            transcendentals=0,
+        ),
+        name="two_products",
+    )(first, first_right, second, second_right)
 
 
 def gelu_and_slope(u):
@@ -588,11 +695,8 @@
     c_pieces = plane_pieces(after(cotangent[0], *x_pieces[1:]))
     x_pieces = x_pieces + [other_core(piece) for piece in x_pieces]
 
-    normed = order_pieces(norm_kernel, "norm_both", both_places, x_pieces, (gain, nbias))
-
-    normed = order_pieces(norm_kernel, "norm_both", both_places, x_pieces, (gain, nbias))
-
-    down_part = after(down_part, x_pieces[ns - 1])
+    norm_places = jnp.concatenate([both_places, k[None].astype(jnp.int32)])
+    normed, normed_near, normed_far = norm_pieces(norm_places, x_pieces, gain, nbias, rows)
 
     if one_each:
         out_wide = d * hw // rows
@@ -611,47 +715,6 @@
     def first_first(left, right):
         return lax.dot_general(left, right, (((0,), (0,)), ((), ())), preferred_element_type=f32)
 
-    pinned = after
-
-    class Walk:
-        def __init__(self, x):
-            self.blocks = x.reshape((nz, -1) + x.shape[1:])
-            self.hop = 0
-            self.got = None
-
-        def parts(self):
-            hop = self.hop + 1
-            ends = (jnp.minimum(nz - hop + z, nz - 1), jnp.maximum(hop + z - nz, 0))
-            parts = [pick(self.blocks, end, 0) for end in ends]
-            if self.got is not None:
-                parts = [(p.astype(f32) + g.astype(f32)).astype(bf16) for p, g in zip(parts, self.got)]
-            return parts
-
-        def step(self, hops=1, after=None):
-            parts = []
-            for _ in range(hops):
-                if after is not None:
-                    self.got = [pinned(g, after) for g in self.got]
-                parts = self.parts()
-                self.hop += 1
-                self.got = [step_line(p, self.hop, way) for p, way in zip(parts, (True, False))]
-            return parts
-
-        def rest(self, after=None):
-            return self.step(nz - 1 - self.hop, after)
-
-        def own(self):
-            own = pick(self.blocks, z, 0).astype(f32)
-            return (own + self.got[0].astype(f32) + self.got[1].astype(f32)).astype(bf16)
-
-    def step_line(part, hops, forward):
-        hops_ = []
-        for c in range(CORES):
-            for q in range(hops):
-                at, to = (q, q + 1) if forward else (nz - 1 - q, nz - 2 - q)
-                hops_.append((CORES * at + c, CORES * to + c))
-        return lax.ppermute(part, "fsdp", hops_)
-
     def pair_cores(x):
         by_core = x.reshape(nz, CORES, rows, -1)
         keep, got = pick(by_core, k, 1), other_core(pick(by_core, 1 - k, 1))
@@ -683,6 +746,9 @@
                 self.across, self.beside = plane_hop(parts[3], 0), plane_hop(parts[1], 0)
             else:
                 self.others = [plane_send(parts[d], d) for d in range(1, ns)]
+
+        def first(self):
+            return [self.across, self.beside] if two_steps else self.others
 
         def middle(self, *passed):
             if not two_steps:
@@ -737,64 +803,30 @@
     attended_grad = last_last(c2, out_mine).astype(bf16)
     attended = after(attended, attended_grad)
     out_local = first_first(attended, c2).astype(bf16)
-    beside = []
-    if one_each:
-        beside = out_local.reshape(nz, hw, -1, out_wide).transpose(0, 2, 1, 3)
-        beside = [beside.reshape(nz * rows, out_wide)]
     activated, attended = after(activated, out_local), after(attended, out_local)
     branch_far, branch_near = halves(activated, down_mine, plain_dot, halves(attended, out_mine, plain_dot))
-    branch_got = after(other_core(branch_far), branch_near, *beside)
+    branch_got = after(other_core(branch_far), branch_near)
     branch_parts = rank_parts(branch_near, branch_got)
     branch_sum = RankSum(branch_parts)
     attended_grad = after(attended_grad, *branch_parts)
     mixed_grad = attend_back(heads, attended_grad, logsums, tables, length)
-    normed = after(normed, mixed_grad)
-    qkv_local = first_first(normed, mixed_grad).astype(bf16)
-    passed = branch_sum.middle(qkv_local)
-    hidden_grad, mixed_grad = after(hidden_grad, *passed), after(mixed_grad, *passed)
-    far, near = halves(hidden_grad, up_mine, last_last, halves(mixed_grad, qkv_mine, last_last))
+    normed_far = after(normed_far, mixed_grad)
+    qkv_far = first_first(normed_far, mixed_grad).astype(bf16)
+    qkv_got = other_core(qkv_far)
+    normed_near = after(normed_near, qkv_far)
+    qkv_near = first_first(normed_near, mixed_grad).astype(bf16)
+    passed = branch_sum.middle(qkv_near)
+    hidden_grad, mixed_grad = after(hidden_grad, *passed), after(mixed_grad, qkv_got)
+    far, near = two_products(hidden_grad, up_mine, mixed_grad, qkv_mine)
     got = other_core(far)
-    branches = branch_sum.total(near)
-    attn_local = pair_cores(after(qkv_local, near, branches))
-    attn_local = jnp.concatenate([attn_local] + beside, axis=1)
+    if one_each:
+        attn_local = pack(qkv_near, after(qkv_got, near), out_local, rows, hw)
+    else:
+        attn_local = jnp.concatenate([qkv_near, qkv_got], axis=1)
     grad_parts = rank_parts(near, after(got, attn_local))
     grad_sum = RankSum(grad_parts)
-    ff_own = [after(x, *grad_parts) for x in ff_own]
-    attn_own = line_sum(after(attn_local, *ff_own))
-    out_own = line_sum(out_local) if spread and not one_each else None
-    ff_pieces = [Pieces(x) for x in ff_own]
-    passed = grad_sum.middle(*ff_own)
-    normed_grad = grad_sum.total(*passed)
-    passed = [normed_grad] + [x for pieces in ff_pieces for x in pieces.middle(*passed)]
-    attn_pieces = Pieces(after(attn_own, *passed))
-
-    token_rows = tokens[0].astype(f32)
-    block_out = (token_rows + branches + outb + downb).astype(bf16)[None]
-
-    centred_own = token_rows - jnp.mean(token_rows, axis=-1, keepdims=True)
-    variance_own = jnp.mean(centred_own * centred_own, axis=-1, keepdims=True)
-    inverse = lax.rsqrt(variance_own + epsilon)
-    xhat = centred_own * inverse
-    g = normed_grad * gain
-    rows_grad = inverse * (
-        g - jnp.mean(g, axis=-1, keepdims=True) - xhat * jnp.mean(g * xhat, axis=-1, keepdims=True)
-    )
-    upstream = cotangent[0].astype(f32)
-    tokens_grad = (upstream + rows_grad).astype(bf16)[None]
-
-    def everyone_sum(sums):
-        flat = jnp.concatenate([v.reshape(nf, -1) for v in sums], axis=1)
-        flat = jnp.broadcast_to(flat[None], (ns,) + flat.shape).reshape(ns * nf, -1)
-        flat = lax.all_to_all(flat, everyone, split_axis=0, concat_axis=0, tiled=True)
-        flat = jnp.sum(flat, axis=0)
-        shards, at = [], 0
-        for v in sums:
-            size = v.shape[0] // nf
-            shards.append(flat[at : at + size])
-            at += size
-        return shards
-
-    mixed_grad, hidden_grad = after(mixed_grad, normed_grad), after(hidden_grad, normed_grad)
+    branches = branch_sum.total(*grad_parts)
+    mixed_grad, hidden_grad = after(mixed_grad, branches), after(hidden_grad, branches)
     mixed_sum = jnp.sum(mixed_grad.astype(f32), axis=0).reshape(pairs, 3, PAIR).transpose(1, 0, 2)
     if spread:
         mixed_sum = mixed_sum.reshape(3, nz, 1, 1, hw)
@@ -809,7 +841,54 @@
     hidden_full = lax.dynamic_update_slice(
         jnp.zeros((nz, CORES, ns, w), f32), hidden_sum, (0, k, s, 0)
     )
-    c_local = jnp.sum(after(cotangent[0], normed_grad).astype(f32), axis=0)
+    c_local = jnp.sum(after(cotangent[0], branches).astype(f32), axis=0)
+    passed = (branches, mixed_full, hidden_full, c_local)
+    ff_own = [after(x, *passed, *grad_sum.first()) for x in ff_own]
+    attn_own = line_sum(after(attn_local, *ff_own))
+    out_own = line_sum(out_local) if spread and not one_each else None
+    ff_pieces = [Pieces(x) for x in ff_own]
+    passed = grad_sum.middle(*ff_own)
+    normed_grad = grad_sum.total(*passed)
+
+    token_rows = tokens[0].astype(f32)
+    block_out = (token_rows + branches + outb + downb).astype(bf16)[None]
+
+    centred_own = token_rows - jnp.mean(token_rows, axis=-1, keepdims=True)
+    variance_own = jnp.mean(centred_own * centred_own, axis=-1, keepdims=True)
+    inverse = lax.rsqrt(variance_own + epsilon)
+    xhat = centred_own * inverse
+    g = normed_grad * gain
+    rows_grad = inverse * (
+        g - jnp.mean(g, axis=-1, keepdims=True) - xhat * jnp.mean(g * xhat, axis=-1, keepdims=True)
+    )
+    upstream = cotangent[0].astype(f32)
+    tokens_grad = (upstream + rows_grad).astype(bf16)[None]
+
+    passed = [x for pieces in ff_pieces for x in pieces.middle(tokens_grad)]
+    attn_pieces = Pieces(after(attn_own, *passed))
+    ff_pieces = [pieces.all(attn_pieces.pieces[0]) for pieces in ff_pieces]
+    up_pieces, down_pieces = ff_pieces[0], ff_pieces[-1]
+    if tiled:
+        up_wgrad = place_units(places, up_pieces, rows, nz, w)
+    else:
+        up_all = both_in_order(up_pieces).reshape(ns, rows, CORES, nz, w)
+        up_wgrad = up_all.transpose(1, 3, 2, 0, 4).reshape(rows, ff).astype(f32)
+    passed = attn_pieces.middle(up_wgrad)
+    down_pieces = down_pieces[:1] + [after(piece, *passed) for piece in down_pieces[1:]]
+    down_wgrad = order_pieces(order_kernel, "place_down", places, down_pieces, dtype=f32, size=w)
+
+    def everyone_sum(sums):
+        flat = jnp.concatenate([v.reshape(nf, -1) for v in sums], axis=1)
+        flat = jnp.broadcast_to(flat[None], (ns,) + flat.shape).reshape(ns * nf, -1)
+        flat = lax.all_to_all(after(flat, *passed), everyone, split_axis=0, concat_axis=0, tiled=True)
+        flat = jnp.sum(flat, axis=0)
+        shards, at = [], 0
+        for v in sums:
+            size = v.shape[0] // nf
+            shards.append(flat[at : at + size])
+            at += size
+        return shards
+
     sums = (
         mixed_full.reshape(-1)[: 2 * d],
         mixed_full.reshape(-1)[2 * d :],
@@ -821,17 +900,7 @@
     bias_grads = everyone_sum(sums)
     qkv_bgrad, value_bgrad, up_bgrad, out_bgrad, gain_grad, norm_bgrad = bias_grads
 
-    passed = attn_pieces.middle(tokens_grad, *bias_grads)
-    ff_pieces = [pieces.all(*passed) for pieces in ff_pieces]
-    up_pieces, down_pieces = ff_pieces[0], ff_pieces[-1]
-    if tiled:
-        up_wgrad = place_units(places, up_pieces, rows, nz, w)
-    else:
-        up_all = both_in_order(up_pieces).reshape(ns, rows, CORES, nz, w)
-        up_wgrad = up_all.transpose(1, 3, 2, 0, 4).reshape(rows, ff).astype(f32)
-    down_wgrad = order_pieces(order_kernel, "place_down", places, down_pieces, dtype=f32, size=w)
-
-    attn_pieces = attn_pieces.all(up_wgrad, down_wgrad)
+    attn_pieces = attn_pieces.all()
     out_pieces = plane_pieces(out_own) if spread and not one_each else None
     if one_each:
         qkv_wgrad = place_heads(places, attn_pieces, nz)

time: 582 us -> 567 us (0.974)
  matrix products: 130 us -> 100 us
  Pallas kernels: 86 us -> 116 us
    pallas_call x0 -> x3, Pallas kernels: none -> 40.3 us  [the longest x1 22.1 us: two_products(): pl.pallas_call(two_products_kernel, grid=(2 * half,), in_specs=[left(firs...]
    all_to_all x1, waiting for transfers between devices: 39.9 us -> 6.37 us  [everyone_sum(): lax.all_to_all(after(flat, *passed), everyone, split_axis=0, concat_axis=...]
    dot_general x6 -> x2, matrix products: 50.7 us -> 20.6 us  [last_last(): lax.dot_general(left, right, (((1,), (1,)), ((), ())), preferred_element_...]
    ppermute x18, waiting for transfers between devices: 112 us -> 132 us  [plane_hop(): return lax.ppermute(x, everyone, hops)]
    reduce_scatter x2, waiting for transfers between devices: 0.01 us -> 12.6 us  [line_sum(): lax.psum_scatter(x, 'fsdp', scatter_dimension=0, tiled=True, axis_index_g...]
    pallas_call x3 -> x2, Pallas kernels: 25.3 us -> 14.8 us  [order_pieces(): pl.pallas_call(kernel, grid_spec=pltpu.PrefetchScalarGridSpec(num_scalar_...]
    dynamic_slice x0 -> x2, local copies, waits for them, and re-layouts: none -> 5.91 us  [the longest x1 3.22 us: on_device(): lax.dynamic_slice_in_dim(both, k * 3 * rank_cols, 3 * rank_cols, 1)]
    ppermute x12, waiting for transfers between devices: 13.1 us -> 7.24 us  [other_core(): return lax.ppermute(x, 'fsdp', swap)]
  transfers between devices with their start and end apart: 36 -> 36, of which waited for: 15 -> 17; matrix products, arithmetic and copies ran while one was open for 36% -> 30% of each run, Pallas kernels for 13% -> 18%
where the time goes in v4:
time: 567 us; the launch traced here: 563 us
  waiting for transfers between devices  214 us (38%)
  Pallas kernels  116 us (20%)
  matrix products  100 us (18%)
  other arithmetic  45 us (8%)
  local copies, waits for them, and re-layouts  38.4 us (7%)
  starting transfers between devices  35.3 us (6%)
  between operations  14.9 us (3%)
    ppermute x18, waiting for transfers between devices, plane_hop(): return lax.ppermute(x, everyone, hops)  132 us
    all_gather x1, waiting for transfers between devices, on_device(): lax.all_gather(jnp.concatenate([up_part, down_part]), 'fsdp', axis=0, til...  55.5 us
    dot_general x6, matrix products, plain_dot(): return jnp.dot(left, right, preferred_element_type=f32)  43.7 us
    dot_general x5, matrix products, first_first(): lax.dot_general(left, right, (((0,), (0,)), ((), ())), preferred_element_...  35.7 us
    ppermute x18, starting transfers between devices, plane_hop(): return lax.ppermute(x, everyone, hops)  24.3 us
    pallas_call x1, Pallas kernels, two_products(): pl.pallas_call(two_products_kernel, grid=(2 * half,), in_specs=[left(firs...  22.1 us
    dot_general x2, matrix products, last_last(): lax.dot_general(left, right, (((1,), (1,)), ((), ())), preferred_element_...  20.6 us
    pallas_call x1, Pallas kernels, attend_back(): pl.pallas_call(attend_back_kernel, grid=(count, pairs), in_specs=[wide, p...  20.4 us
  transfers between devices with their start and end apart: 36, of which 17 were waited for; matrix products, arithmetic and copies ran while one was open for 30% of the time, Pallas kernels for 18%

profile of v4, /device:TPU:0, one launch (start us, length us, event | category | flops | bytes accessed | tf_op | source)
XLA Modules:
  0.0 563.2 jit_solution(9974241196916833673)
XLA Ops:
  31.9 10.3 %collective-permute-done.refs_1_ = bf16[256,2048]{1,0:T(8,128)(2,1)} collective-permute-done((bf16[256,2048]{1,0:T(8,128)(2,1)S(1)}, bf16[256,2048]{1,0:T(8,128)(2,1)}, u32[]{:S(2)}, u32[]{:S(2)}) %collective-permute-start) | collective-permute-done | bytes 1048608 | tf_op jit(solution)/shard_map/ppermute | solution.py:602
  49.5 7.8 %collective-permute-done.2.refs_3_ = bf16[256,2048]{1,0:T(8,128)(2,1)} collective-permute-done((bf16[256,2048]{1,0:T(8,128)(2,1)}, bf16[256,2048]{1,0:T(8,128)(2,1)}, u32[]{:S(2)}, u32[]{:S(2)}) %collective-permute-start.2) | collective-permute-done | bytes 1048608 | tf_op jit(solution)/shard_map/ppermute | solution.py:602
  61.1 21.5 %collective-permute-done.7.refs_1_ = bf16[256,2048]{1,0:T(8,128)(2,1)} collective-permute-done((bf16[256,2048]{1,0:T(8,128)(2,1)S(1)}, bf16[256,2048]{1,0:T(8,128)(2,1)}, u32[]{:S(2)}, u32[]{:S(2)}) %collective-permute-start.7) | collective-permute-done | bytes 1048608 | tf_op jit(solution)/shard_map/ppermute | solution.py:602
  87.0 13.2 %norm_pieces.1 = (bf16[2048,2048]{1,0:T(8,128)(2,1)}, bf16[2048,1024]{1,0:T(8,128)(2,1)}, bf16[2048,1024]{1,0:T(8,128)(2,1)}) custom-call(s32[9]{0:T(128)S(1)} %concatenate.30.places_ref, f32[1,2048]{1,0:T(1,128)S(1)} %bitcast.116, f32[1,2048]{1,0:T(1,128)S(1)} %bitcast.117, bf16[256,2048]{1,0:T(8,128)(2,1)S(1)} %bitcast.110, ...), custom_call_target="tpu_custom_call" | custom-call | tf_op jit(solution)/shard_map/norm_pieces/pallas_call | solution.py:233
  106.2 8.7 %order_both.1 = bf16[2048,2048]{1,0:T(8,128)(2,1)} custom-call(s32[8]{0:T(128)S(1)} %concatenate.33.places_ref, bf16[256,2048]{1,0:T(8,128)(2,1)S(1)} %bitcast.114, bf16[256,2048]{1,0:T(8,128)(2,1)} %collective-permute-done.7.refs_1_, bf16[256,2048]{1,0:T(8,128)(2,1)} %collective-permute-done.8.refs_2_, bf16[256,2048]{1,0:T(8,128)(2,1)} %collective-permute-done.9.refs_3_, ...), custom_call_target="tpu_custom_call" | custom-call | tf_op jit(solution)/shard_map/order_both/pallas_call | solution.py:269
  115.0 55.5 %all-gather.3.cloned.1.call-done = bf16[4096,2048]{1,0:T(8,128)(2,1)} async-done(((bf16[512,2048]{1,0:T(8,128)(2,1)}), bf16[4096,2048]{1,0:T(8,128)(2,1)}) %all-gather.3.cloned.1.call-update) | async-done | bytes 16777232 | tf_op jit(solution)/shard_map/all_gather | solution.py:683
  170.5 6.6 %fusion.34 = (bf16[4,2,256,2048]{3,2,1,0:T(8,128)(2,1)S(1)}, bf16[4,2,256,2048]{3,2,1,0:T(8,128)(2,1)S(1)}) fusion(bf16[4,2,512,2048]{3,2,1,0:T(8,128)(2,1)} %bitcast.124), kind=kLoop, calls=%fused_computation.113 | loop fusion | bytes 33554432 | tf_op jit(solution)/shard_map/slice | solution.py:777
  179.8 16.4 %multiply_convert_fusion.1 = (bf16[2048,1024]{1,0:T(8,128)(2,1)S(1)}, f32[2048,1024]{1,0:T(8,128)}) fusion(f32[1024]{0:T(1024)S(1)} %bitcast.154, bf16[2048,2048]{1,0:T(8,128)(2,1)} %get-tuple-element.80, bf16[2048,1024]{1,0:T(8,128)(2,1)} %constant_dynamic-slice_fusion.2.first_right_ref), kind=kOutput, calls=%fused_computation.5 | convolution fusion | flops 8610906112 | bytes 25169920 | tf_op jit(solution)/shard_map/dot_general | solution.py:50
  196.2 11.0 %convolution_convert_fusion = bf16[1024,2048]{1,0:T(8,128)(2,1)} fusion(bf16[2048,1024]{1,0:T(8,128)(2,1)S(1)} %get-tuple-element.86, bf16[2048,2048]{1,0:T(8,128)(2,1)S(1)} %bitcast.119), kind=kOutput, calls=%fused_computation.9 | convolution fusion | flops 8592031744 | bytes 16777216 | tf_op jit(solution)/shard_map/dot_general | solution.py:716
  209.5 17.3 %multiply_convert_fusion.first_ref = bf16[2048,1024]{1,0:T(8,128)(2,1)S(1)} fusion(f32[2048,1024]{1,0:T(8,128)} %get-tuple-element.157, bf16[2048,2048]{1,0:T(8,128)(2,1)S(1)} %bitcast.119, bf16[1024,2048]{1,0:T(8,128)(2,1)} %bitcast.129, f32[1024]{0:T(1024)S(1)} %bitcast.155), kind=kOutput, calls=%fused_computation.4 | convolution fusion | flops 8629780480 | bytes 25169920 | tf_op jit(solution)/shard_map/dot_general | solution.py:46
  226.8 13.1 %convolution_convert_fusion.1 = bf16[2048,1024]{1,0:T(8,128)(2,1)S(1)} fusion(bf16[2048,2048]{1,0:T(8,128)(2,1)} %get-tuple-element.80, bf16[2048,1024]{1,0:T(8,128)(2,1)S(1)} %multiply_convert_fusion.first_ref), kind=kOutput, calls=%fused_computation.10 | convolution fusion | flops 8592031744 | bytes 16777216 | tf_op jit(solution)/shard_map/dot_general | solution.py:716
  246.9 7.1 %pad_maximum_fusion = bf16[4,512,2048]{2,1,0:T(8,128)(2,1)} fusion(bf16[4,256,2048]{2,1,0:T(8,128)(2,1)} %bitcast.135, bf16[4,256,1024]{2,1,0:T(8,128)(2,1)} %collective-permute-done.14, bf16[4,256,1024]{2,1,0:T(8,128)(2,1)} %get-tuple-element.140), kind=kLoop, calls=%fused_computation | loop fusion | flops 25165824 | bytes 16777216 | tf_op jit(solution)/shard_map/concatenate | solution.py:789
  262.9 9.2 %broadcast_add_fusion.mixed_ref = f32[2048,768]{1,0:T(8,128)S(1)} fusion(f32[768]{0:T(1024)S(1)} %fusion.27, bf16[2048,2048]{1,0:T(8,128)(2,1)} %get-tuple-element.80, bf16[2048,768]{1,0:T(8,128)(2,1)S(1)} %constant_dynamic-slice_fusion.second_right_ref), kind=kOutput, calls=%fused_computation.11 | convolution fusion | flops 6444023808 | bytes 17828864 | tf_op jit(solution)/shard_map/dot_general | solution.py:50
  272.1 15.3 %attend.1 = (bf16[2048,768]{1,0:T(8,128)(2,1)S(1)}, bf16[2048,256]{1,0:T(8,128)(2,1)S(1)}, f32[2,2,2,1024]{3,2,1,0:T(2,128)S(1)}) custom-call(f32[2048,768]{1,0:T(8,128)S(1)} %broadcast_add_fusion.mixed_ref, f32[1024,128]{1,0:T(8,128)S(1)} %copy-done.13, f32[1024,128]{1,0:T(8,128)S(1)} %copy-done.11, f32[1024,128]{1,0:T(8,128)S(1)} %copy-done.9), custom_call_target="tpu_custom_call" | custom-call | flops 2147483648 | bytes 12582912 | tf_op jit(solution)/shard_map/attend/pallas_call | solution.py:150
  296.4 7.8 %add_convert_fusion = bf16[1024,2048]{1,0:T(8,128)(2,1)} fusion(bf16[1024,2048]{1,0:T(8,128)(2,1)S(1)} %fusion.23, bf16[1024,2048]{1,0:T(8,128)(2,1)S(1)} %bitcast.130, bf16[2048,1024]{1,0:T(8,128)(2,1)} %copy-done.42), kind=kOutput, calls=%fused_computation.2 | convolution fusion | flops 4301258752 | bytes 14680064 | tf_op jit(solution)/shard_map/dot_general | solution.py:50
  321.6 20.4 %attend_back.1.second_ref = bf16[2048,768]{1,0:T(8,128)(2,1)S(1)} custom-call(bf16[2048,768]{1,0:T(8,128)(2,1)S(1)} %copy-done.17, bf16[2048,256]{1,0:T(8,128)(2,1)S(1)} %copy-done.18, f32[2,2,2,1024]{3,2,1,0:T(2,128)S(1)} %get-tuple-element.93.logsum_ref, f32[1024,128]{1,0:T(8,128)S(1)} %copy-done.14, f32[1024,128]{1,0:T(8,128)S(1)} %copy-done.12, ...), custom_call_target="tpu_custom_call" | custom-call | flops 5368709120 | bytes 9437184 | tf_op jit(solution)/shard_map/attend_back/pallas_call | solution.py:180
  351.8 22.1 %two_products.1 = (bf16[1024,2048]{1,0:T(8,128)(2,1)}, bf16[1024,2048]{1,0:T(8,128)(2,1)}) custom-call(bf16[2048,1024]{1,0:T(8,128)(2,1)} %copy-done.23, bf16[2048,1024]{1,0:T(8,128)(2,1)} %constant_dynamic-slice_fusion.2.first_right_ref, bf16[2048,768]{1,0:T(8,128)(2,1)S(1)} %attend_back.1.second_ref, bf16[2048,768]{1,0:T(8,128)(2,1)} %copy-done.26), custom_call_target="tpu_custom_call" | custom-call | flops 15032385536 | bytes 23068672 | tf_op jit(solution)/shard_map/two_products/pallas_call | solution.py:518
  381.6 7.2 %add_convert_fusion.3 = (bf16[256,2048]{1,0:T(8,128)(2,1)}, bf16[256,2048]{1,0:T(8,128)(2,1)S(1)}, bf16[256,2048]{1,0:T(8,128)(2,1)}, f32[256,2048]{1,0:T(8,128)}) fusion(bf16[1024,2048]{1,0:T(8,128)(2,1)} %collective-permute-done.19, s32[]{:T(128)S(6)} %select_n.188, bf16[1024,2048]{1,0:T(8,128)(2,1)} %get-tuple-element.99, s32[]{:T(128)S(6)} %select_n.187, ...), kind=kLoop, calls=%fused_computation.37 | loop fusion | flops 7864320 | bytes 13631504 | tf_op jit(solution)/shard_map/convert_element_type | solution.py:740
  403.9 11.2 %collective-permute-done.21 = bf16[256,2048]{1,0:T(8,128)(2,1)} collective-permute-done((bf16[256,2048]{1,0:T(8,128)(2,1)}, bf16[256,2048]{1,0:T(8,128)(2,1)}, u32[]{:S(2)}, u32[]{:S(2)}) %collective-permute-start.21) | collective-permute-done | bytes 1048608 | tf_op jit(solution)/shard_map/ppermute | solution.py:602
  420.0 22.9 %collective-permute-done.23 = bf16[256,2048]{1,0:T(8,128)(2,1)S(1)} collective-permute-done((bf16[256,2048]{1,0:T(8,128)(2,1)S(1)}, bf16[256,2048]{1,0:T(8,128)(2,1)S(1)}, u32[]{:S(2)}, u32[]{:S(2)}) %collective-permute-start.23) | collective-permute-done | bytes 1048608 | tf_op jit(solution)/shard_map/ppermute | solution.py:602
  447.4 19.4 %collective-permute-done.24.refs_1_ = bf16[512,2048]{1,0:T(8,128)(2,1)} collective-permute-done((bf16[512,2048]{1,0:T(8,128)(2,1)}, bf16[512,2048]{1,0:T(8,128)(2,1)}, u32[]{:S(2)}, u32[]{:S(2)}) %collective-permute-start.24) | collective-permute-done | bytes 2097184 | tf_op jit(solution)/shard_map/ppermute | solution.py:602
  466.8 9.5 %collective-permute-done.25.refs_2_ = bf16[512,2048]{1,0:T(8,128)(2,1)} collective-permute-done((bf16[512,2048]{1,0:T(8,128)(2,1)}, bf16[512,2048]{1,0:T(8,128)(2,1)}, u32[]{:S(2)}, u32[]{:S(2)}) %collective-permute-start.25) | collective-permute-done | bytes 2097184 | tf_op jit(solution)/shard_map/ppermute | solution.py:602
  477.2 12.6 %reduce-scatter.5.cloned.1.call-done.refs_0_ = bf16[256,2048]{1,0:T(8,128)(2,1)} async-done(((bf16[1024,2048]{1,0:T(8,128)(2,1)}), bf16[256,2048]{1,0:T(8,128)(2,1)}) %reduce-scatter.5.cloned.1.call-update) | async-done | bytes 1048592 | tf_op jit(solution)/shard_map/reduce_scatter | solution.py:768
  493.7 18.8 %collective-permute-done.28.refs_3_ = bf16[512,2048]{1,0:T(8,128)(2,1)S(1)} collective-permute-done((bf16[512,2048]{1,0:T(8,128)(2,1)}, bf16[512,2048]{1,0:T(8,128)(2,1)S(1)}, u32[]{:S(2)}, u32[]{:S(2)}) %collective-permute-start.28) | collective-permute-done | bytes 2097184 | tf_op jit(solution)/shard_map/ppermute | solution.py:602
  (274 shorter events, 183.2 us)
Async XLA Ops:
  7.2 163.3 %all-gather.3.cloned.1.call-start = ((), (), s32[]{:S(2)}) async-start(), calls=%async_computation.4 | async-start | bytes 18874368 | tf_op jit(solution)/shard_map/all_gather | solution.py:683
  15.6 26.5 %collective-permute-start = (bf16[256,2048]{1,0:T(8,128)(2,1)S(1)}, bf16[256,2048]{1,0:T(8,128)(2,1)}, u32[]{:S(2)}, u32[]{:S(2)}) collective-permute-start(bf16[256,2048]{1,0:T(8,128)(2,1)S(1)} %bitcast.107), channel_id=1, source_target_pairs={{0,8},{1,17},{2,10},{3,19},{4,12},{5,21},{6,14},{7,23},{8,0},{9,25... | collective-permute-start | bytes 3145736 | tf_op jit(solution)/shard_map/ppermute | solution.py:602
  18.6 23.5 %collective-permute-start.1 = (bf16[256,2048]{1,0:T(8,128)(2,1)S(1)}, bf16[256,2048]{1,0:T(8,128)(2,1)}, u32[]{:S(2)}, u32[]{:S(2)}) collective-permute-start(bf16[256,2048]{1,0:T(8,128)(2,1)S(1)} %bitcast.108), channel_id=1, source_target_pairs={{0,16},{1,9},{2,18},{3,11},{4,20},{5,13},{6,22},{7,15},{8,24},{9,1... | collective-permute-start | bytes 3145736 | tf_op jit(solution)/shard_map/ppermute | solution.py:602
  23.5 24.4 %all-to-all-start = ((bf16[8,2,1408]{2,1,0:T(2,128)(2,1)}), bf16[8,2,1408]{2,1,0:T(2,128)(2,1)S(1)}, u32[]{:S(2)}, u32[]{:S(2)}) async-start(bf16[8,2,1408]{2,1,0:T(2,128)(2,1)} %reshape.261), calls=%async_computation | async-start | bytes 90112 | tf_op jit(solution)/shard_map/all_to_all | solution.py:649
  28.4 225.9 %all-gather.5.cloned.1.call-start = ((), (), s32[]{:S(2)}) async-start(), calls=%async_computation.5 | async-start | bytes 9437184 | tf_op jit(solution)/shard_map/all_gather | solution.py:705
  57.3 25.3 %collective-permute-start.7 = (bf16[256,2048]{1,0:T(8,128)(2,1)S(1)}, bf16[256,2048]{1,0:T(8,128)(2,1)}, u32[]{:S(2)}, u32[]{:S(2)}) collective-permute-start(bf16[256,2048]{1,0:T(8,128)(2,1)S(1)} %bitcast.111), channel_id=1, source_target_pairs={{0,8},{1,17},{2,10},{3,19},{4,12},{5,21},{6,14},{7,23},{8,0},{9,25... | collective-permute-start | bytes 3145736 | tf_op jit(solution)/shard_map/ppermute | solution.py:602
  59.8 22.8 %collective-permute-start.8 = (bf16[256,2048]{1,0:T(8,128)(2,1)S(1)}, bf16[256,2048]{1,0:T(8,128)(2,1)}, u32[]{:S(2)}, u32[]{:S(2)}) collective-permute-start(bf16[256,2048]{1,0:T(8,128)(2,1)S(1)} %bitcast.112), channel_id=1, source_target_pairs={{0,16},{1,9},{2,18},{3,11},{4,20},{5,13},{6,22},{7,15},{8,24},{9,1... | collective-permute-start | bytes 3145736 | tf_op jit(solution)/shard_map/ppermute | solution.py:602
  60.5 24.0 %collective-permute-start.3 = (bf16[256,2048]{1,0:T(8,128)(2,1)S(1)}, bf16[256,2048]{1,0:T(8,128)(2,1)S(1)}, u32[]{:S(2)}, u32[]{:S(2)}) collective-permute-start(bf16[256,2048]{1,0:T(8,128)(2,1)S(1)} %bitcast.109), channel_id=1, source_target_pairs={{0,1},{1,0},{2,3},{3,2},{4,5},{5,4},{6,7},{7,6},{8,9},{9,8},{10,11... | collective-permute-start | bytes 3145736 | tf_op jit(solution)/shard_map/ppermute | solution.py:590
  60.5 25.2 %collective-permute-start.4 = (bf16[256,2048]{1,0:T(8,128)(2,1)}, bf16[256,2048]{1,0:T(8,128)(2,1)}, u32[]{:S(2)}, u32[]{:S(2)}) collective-permute-start(bf16[256,2048]{1,0:T(8,128)(2,1)} %collective-permute-done.refs_1_), channel_id=1, source_target_pairs={{0,1},{1,0},{2,3},{3,2},{4,5},{5,4},{6,7},{7,6},{8,9},{9,8},{10,11... | collective-permute-start | bytes 3145736 | tf_op jit(solution)/shard_map/ppermute | solution.py:590
  61.1 24.7 %collective-permute-start.5 = (bf16[256,2048]{1,0:T(8,128)(2,1)}, bf16[256,2048]{1,0:T(8,128)(2,1)}, u32[]{:S(2)}, u32[]{:S(2)}) collective-permute-start(bf16[256,2048]{1,0:T(8,128)(2,1)} %collective-permute-done.1.refs_2_), channel_id=1, source_target_pairs={{0,1},{1,0},{2,3},{3,2},{4,5},{5,4},{6,7},{7,6},{8,9},{9,8},{10,11... | collective-permute-start | bytes 3145736 | tf_op jit(solution)/shard_map/ppermute | solution.py:590
  82.6 18.2 %collective-permute-start.9 = (bf16[256,2048]{1,0:T(8,128)(2,1)}, bf16[256,2048]{1,0:T(8,128)(2,1)}, u32[]{:S(2)}, u32[]{:S(2)}) collective-permute-start(bf16[256,2048]{1,0:T(8,128)(2,1)} %collective-permute-done.7.refs_1_), channel_id=1, source_target_pairs={{0,16},{1,9},{2,18},{3,11},{4,20},{5,13},{6,22},{7,15},{8,24},{9,1... | collective-permute-start | bytes 3145736 | tf_op jit(solution)/shard_map/ppermute | solution.py:602
  85.5 18.4 %collective-permute-start.10 = (bf16[256,2048]{1,0:T(8,128)(2,1)S(1)}, bf16[256,2048]{1,0:T(8,128)(2,1)}, u32[]{:S(2)}, u32[]{:S(2)}) collective-permute-start(bf16[256,2048]{1,0:T(8,128)(2,1)S(1)} %bitcast.113), channel_id=1, source_target_pairs={{0,1},{1,0},{2,3},{3,2},{4,5},{5,4},{6,7},{7,6},{8,9},{9,8},{10,11... | collective-permute-start | bytes 3145736 | tf_op jit(solution)/shard_map/ppermute | solution.py:590
  103.5 311.6 %reduce-scatter.3.cloned.1.call-start = ((), (), s32[]{:S(2)}) async-start(), calls=%async_computation.6 | async-start | bytes 10485760 | tf_op jit(solution)/shard_map/reduce_scatter | solution.py:768
  254.0 235.8 %reduce-scatter.5.cloned.1.call-start = ((), (), s32[]{:S(2)}) async-start(), calls=%async_computation.7 | async-start | bytes 5242880 | tf_op jit(solution)/shard_map/reduce_scatter | solution.py:768
  319.5 30.9 %collective-permute-start.17 = (bf16[256,2048]{1,0:T(8,128)(2,1)S(1)}, bf16[256,2048]{1,0:T(8,128)(2,1)S(1)}, u32[]{:S(2)}, u32[]{:S(2)}) collective-permute-start(bf16[256,2048]{1,0:T(8,128)(2,1)S(1)} %get-tuple-element.137), channel_id=1, source_target_pairs={{0,8},{1,17},{2,10},{3,19},{4,12},{5,21},{6,14},{7,23},{8,0},{9,25... | collective-permute-start | bytes 3145736 | tf_op jit(solution)/shard_map/ppermute | solution.py:602
  320.8 29.6 %collective-permute-start.16 = (bf16[256,2048]{1,0:T(8,128)(2,1)S(1)}, bf16[256,2048]{1,0:T(8,128)(2,1)S(1)}, u32[]{:S(2)}, u32[]{:S(2)}) collective-permute-start(bf16[256,2048]{1,0:T(8,128)(2,1)S(1)} %get-tuple-element.138), channel_id=1, source_target_pairs={{0,8},{1,17},{2,10},{3,19},{4,12},{5,21},{6,14},{7,23},{8,0},{9,25... | collective-permute-start | bytes 3145736 | tf_op jit(solution)/shard_map/ppermute | solution.py:602
  389.8 25.3 %collective-permute-start.21 = (bf16[256,2048]{1,0:T(8,128)(2,1)}, bf16[256,2048]{1,0:T(8,128)(2,1)}, u32[]{:S(2)}, u32[]{:S(2)}) collective-permute-start(bf16[256,2048]{1,0:T(8,128)(2,1)} %get-tuple-element.134), channel_id=1, source_target_pairs={{0,8},{1,17},{2,10},{3,19},{4,12},{5,21},{6,14},{7,23},{8,0},{9,25... | collective-permute-start | bytes 3145736 | tf_op jit(solution)/shard_map/ppermute | solution.py:602
  416.9 26.0 %collective-permute-start.23 = (bf16[256,2048]{1,0:T(8,128)(2,1)S(1)}, bf16[256,2048]{1,0:T(8,128)(2,1)S(1)}, u32[]{:S(2)}, u32[]{:S(2)}) collective-permute-start(bf16[256,2048]{1,0:T(8,128)(2,1)S(1)} %add_convert_fusion.2), channel_id=1, source_target_pairs={{0,16},{1,9},{2,18},{3,11},{4,20},{5,13},{6,22},{7,15},{8,24},{9,1... | collective-permute-start | bytes 3145736 | tf_op jit(solution)/shard_map/ppermute | solution.py:602
  418.0 48.9 %collective-permute-start.24 = (bf16[512,2048]{1,0:T(8,128)(2,1)}, bf16[512,2048]{1,0:T(8,128)(2,1)}, u32[]{:S(2)}, u32[]{:S(2)}) collective-permute-start(bf16[512,2048]{1,0:T(8,128)(2,1)} %reduce-scatter.3.cloned.1.call-done.refs_0_), channel_id=1, source_target_pairs={{0,8},{1,17},{2,10},{3,19},{4,12},{5,21},{6,14},{7,23},{8,0},{9,25... | collective-permute-start | bytes 6291464 | tf_op jit(solution)/shard_map/ppermute | solution.py:602
  419.1 57.2 %collective-permute-start.25 = (bf16[512,2048]{1,0:T(8,128)(2,1)}, bf16[512,2048]{1,0:T(8,128)(2,1)}, u32[]{:S(2)}, u32[]{:S(2)}) collective-permute-start(bf16[512,2048]{1,0:T(8,128)(2,1)} %reduce-scatter.3.cloned.1.call-done.refs_0_), channel_id=1, source_target_pairs={{0,16},{1,9},{2,18},{3,11},{4,20},{5,13},{6,22},{7,15},{8,24},{9,1... | collective-permute-start | bytes 6291464 | tf_op jit(solution)/shard_map/ppermute | solution.py:602
  476.3 36.2 %collective-permute-start.28 = (bf16[512,2048]{1,0:T(8,128)(2,1)}, bf16[512,2048]{1,0:T(8,128)(2,1)S(1)}, u32[]{:S(2)}, u32[]{:S(2)}) collective-permute-start(bf16[512,2048]{1,0:T(8,128)(2,1)} %collective-permute-done.24.refs_1_), channel_id=1, source_target_pairs={{0,16},{1,9},{2,18},{3,11},{4,20},{5,13},{6,22},{7,15},{8,24},{9,1... | collective-permute-start | bytes 6291464 | tf_op jit(solution)/shard_map/ppermute | solution.py:602
  489.8 30.6 %collective-permute-start.26 = (bf16[256,2048]{1,0:T(8,128)(2,1)}, bf16[256,2048]{1,0:T(8,128)(2,1)}, u32[]{:S(2)}, u32[]{:S(2)}) collective-permute-start(bf16[256,2048]{1,0:T(8,128)(2,1)} %reduce-scatter.5.cloned.1.call-done.refs_0_), channel_id=1, source_target_pairs={{0,8},{1,17},{2,10},{3,19},{4,12},{5,21},{6,14},{7,23},{8,0},{9,25... | collective-permute-start | bytes 3145736 | tf_op jit(solution)/shard_map/ppermute | solution.py:602
  491.3 33.8 %collective-permute-start.27 = (bf16[256,2048]{1,0:T(8,128)(2,1)}, bf16[256,2048]{1,0:T(8,128)(2,1)}, u32[]{:S(2)}, u32[]{:S(2)}) collective-permute-start(bf16[256,2048]{1,0:T(8,128)(2,1)} %reduce-scatter.5.cloned.1.call-done.refs_0_), channel_id=1, source_target_pairs={{0,16},{1,9},{2,18},{3,11},{4,20},{5,13},{6,22},{7,15},{8,24},{9,1... | collective-permute-start | bytes 3145736 | tf_op jit(solution)/shard_map/ppermute | solution.py:602
  525.1 20.5 %collective-permute-start.29 = (bf16[256,2048]{1,0:T(8,128)(2,1)}, bf16[256,2048]{1,0:T(8,128)(2,1)}, u32[]{:S(2)}, u32[]{:S(2)}) collective-permute-start(bf16[256,2048]{1,0:T(8,128)(2,1)} %collective-permute-done.26.refs_1_), channel_id=1, source_target_pairs={{0,16},{1,9},{2,18},{3,11},{4,20},{5,13},{6,22},{7,15},{8,24},{9,1... | collective-permute-start | bytes 3145736 | tf_op jit(solution)/shard_map/ppermute | solution.py:602
  (59 other events, 752.0 us)
Sparse Core Ops, SparseCore 0:
  15.7 154.7 all-gather.2
  172.7 79.3 all-gather.4
  255.0 142.9 reduce-scatter.2
  415.2 74.5 reduce-scatter.4

commit v5 on v4

--- a/solution.py
+++ b/solution.py
@@ -879,9 +879,12 @@
 
     def everyone_sum(sums):
         flat = jnp.concatenate([v.reshape(nf, -1) for v in sums], axis=1)
-        flat = jnp.broadcast_to(flat[None], (ns,) + flat.shape).reshape(ns * nf, -1)
-        flat = lax.all_to_all(after(flat, *passed), everyone, split_axis=0, concat_axis=0, tiled=True)
-        flat = jnp.sum(flat, axis=0)
+        flat = after(flat, attn_pieces.pieces[0])
+        flat = lax.all_to_all(flat, "fsdp", split_axis=0, concat_axis=0, tiled=True)
+        part = after(jnp.sum(flat, axis=0), *passed)
+        flat = part
+        for step in range(1, ns):
+            flat = flat + plane_send(part, step)
         shards, at = [], 0
         for v in sums:
             size = v.shape[0] // nf

time: 567 us -> 569 us (level)
  blocking collectives: 0 us -> 8.5 us
  waiting for transfers between devices: 214 us -> 208 us
    all_to_all x0 -> x1, blocking collectives: none -> 8.5 us  [everyone_sum(): flat = lax.all_to_all(flat, 'fsdp', split_axis=0, concat_axis=0, tiled=True)]
    all_to_all x1 -> x0, waiting for transfers between devices: 6.37 us -> none  [everyone_sum(): lax.all_to_all(after(flat, *passed), everyone, split_axis=0, concat_axis=...]
  transfers between devices with their start and end apart: 36 -> 38, of which waited for: 17 -> 16; matrix products, arithmetic and copies ran while one was open for 30% -> 30% of each run, Pallas kernels for 18% -> 18%
where the time goes in v5:
time: 569 us; the launch traced here: 565 us
  waiting for transfers between devices  208 us (37%)
  Pallas kernels  116 us (20%)
  matrix products  100 us (18%)
  other arithmetic  44.9 us (8%)
  local copies, waits for them, and re-layouts  37.5 us (7%)
  starting transfers between devices  36.2 us (6%)
  between operations  14.8 us (3%)
  blocking collectives  8.5 us (1%)
    ppermute x18, waiting for transfers between devices, plane_hop(): return lax.ppermute(x, everyone, hops)  132 us
    all_gather x1, waiting for transfers between devices, on_device(): lax.all_gather(jnp.concatenate([up_part, down_part]), 'fsdp', axis=0, til...  55.5 us
    dot_general x6, matrix products, plain_dot(): return jnp.dot(left, right, preferred_element_type=f32)  43.7 us
    dot_general x5, matrix products, first_first(): lax.dot_general(left, right, (((0,), (0,)), ((), ())), preferred_element_...  35.7 us
    ppermute x18, starting transfers between devices, plane_hop(): return lax.ppermute(x, everyone, hops)  24.3 us
    pallas_call x1, Pallas kernels, two_products(): pl.pallas_call(two_products_kernel, grid=(2 * half,), in_specs=[left(firs...  22.1 us
    dot_general x2, matrix products, last_last(): lax.dot_general(left, right, (((1,), (1,)), ((), ())), preferred_element_...  20.6 us
    pallas_call x1, Pallas kernels, attend_back(): pl.pallas_call(attend_back_kernel, grid=(count, pairs), in_specs=[wide, p...  20.4 us
  transfers between devices with their start and end apart: 38, of which 16 were waited for; matrix products, arithmetic and copies ran while one was open for 30% of the time, Pallas kernels for 18%

profile of v5, /device:TPU:0, one launch (start us, length us, event | category | flops | bytes accessed | tf_op | source)
XLA Modules:
  0.0 565.3 jit_solution(1624821797150780148)
XLA Ops:
  31.9 10.3 %collective-permute-done.refs_1_ = bf16[256,2048]{1,0:T(8,128)(2,1)} collective-permute-done((bf16[256,2048]{1,0:T(8,128)(2,1)S(1)}, bf16[256,2048]{1,0:T(8,128)(2,1)}, u32[]{:S(2)}, u32[]{:S(2)}) %collective-permute-start) | collective-permute-done | bytes 1048608 | tf_op jit(solution)/shard_map/ppermute | solution.py:602
  49.5 7.8 %collective-permute-done.2.refs_3_ = bf16[256,2048]{1,0:T(8,128)(2,1)} collective-permute-done((bf16[256,2048]{1,0:T(8,128)(2,1)}, bf16[256,2048]{1,0:T(8,128)(2,1)}, u32[]{:S(2)}, u32[]{:S(2)}) %collective-permute-start.2) | collective-permute-done | bytes 1048608 | tf_op jit(solution)/shard_map/ppermute | solution.py:602
  61.1 21.5 %collective-permute-done.7.refs_1_ = bf16[256,2048]{1,0:T(8,128)(2,1)} collective-permute-done((bf16[256,2048]{1,0:T(8,128)(2,1)S(1)}, bf16[256,2048]{1,0:T(8,128)(2,1)}, u32[]{:S(2)}, u32[]{:S(2)}) %collective-permute-start.7) | collective-permute-done | bytes 1048608 | tf_op jit(solution)/shard_map/ppermute | solution.py:602
  87.0 13.3 %norm_pieces.1 = (bf16[2048,2048]{1,0:T(8,128)(2,1)}, bf16[2048,1024]{1,0:T(8,128)(2,1)}, bf16[2048,1024]{1,0:T(8,128)(2,1)}) custom-call(s32[9]{0:T(128)S(1)} %concatenate.30.places_ref, f32[1,2048]{1,0:T(1,128)S(1)} %bitcast.114, f32[1,2048]{1,0:T(1,128)S(1)} %bitcast.115, bf16[256,2048]{1,0:T(8,128)(2,1)S(1)} %bitcast.108, ...), custom_call_target="tpu_custom_call" | custom-call | tf_op jit(solution)/shard_map/norm_pieces/pallas_call | solution.py:233
  106.3 8.8 %order_both.1 = bf16[2048,2048]{1,0:T(8,128)(2,1)} custom-call(s32[8]{0:T(128)S(1)} %concatenate.33.places_ref, bf16[256,2048]{1,0:T(8,128)(2,1)S(1)} %bitcast.112, bf16[256,2048]{1,0:T(8,128)(2,1)} %collective-permute-done.7.refs_1_, bf16[256,2048]{1,0:T(8,128)(2,1)} %collective-permute-done.8.refs_2_, bf16[256,2048]{1,0:T(8,128)(2,1)} %collective-permute-done.9.refs_3_, ...), custom_call_target="tpu_custom_call" | custom-call | tf_op jit(solution)/shard_map/order_both/pallas_call | solution.py:269
  115.1 55.5 %all-gather.3.cloned.1.call-done = bf16[4096,2048]{1,0:T(8,128)(2,1)} async-done(((bf16[512,2048]{1,0:T(8,128)(2,1)}), bf16[4096,2048]{1,0:T(8,128)(2,1)}) %all-gather.3.cloned.1.call-update) | async-done | bytes 16777232 | tf_op jit(solution)/shard_map/all_gather | solution.py:683
  179.8 16.4 %multiply_convert_fusion.1 = (bf16[2048,1024]{1,0:T(8,128)(2,1)S(1)}, f32[2048,1024]{1,0:T(8,128)}) fusion(f32[1024]{0:T(1024)S(1)} %bitcast.152, bf16[2048,2048]{1,0:T(8,128)(2,1)} %get-tuple-element.81, bf16[2048,1024]{1,0:T(8,128)(2,1)} %constant_dynamic-slice_fusion.2.first_right_ref), kind=kOutput, calls=%fused_computation.5 | convolution fusion | flops 8610906112 | bytes 25169920 | tf_op jit(solution)/shard_map/dot_general | solution.py:50
  196.2 11.0 %convolution_convert_fusion = bf16[1024,2048]{1,0:T(8,128)(2,1)} fusion(bf16[2048,1024]{1,0:T(8,128)(2,1)S(1)} %get-tuple-element.87, bf16[2048,2048]{1,0:T(8,128)(2,1)S(1)} %bitcast.117), kind=kOutput, calls=%fused_computation.9 | convolution fusion | flops 8592031744 | bytes 16777216 | tf_op jit(solution)/shard_map/dot_general | solution.py:716
  209.5 17.3 %multiply_convert_fusion.first_ref = bf16[2048,1024]{1,0:T(8,128)(2,1)S(1)} fusion(f32[2048,1024]{1,0:T(8,128)} %get-tuple-element.159, bf16[2048,2048]{1,0:T(8,128)(2,1)S(1)} %bitcast.117, bf16[1024,2048]{1,0:T(8,128)(2,1)} %bitcast.127, f32[1024]{0:T(1024)S(1)} %bitcast.153), kind=kOutput, calls=%fused_computation.4 | convolution fusion | flops 8629780480 | bytes 25169920 | tf_op jit(solution)/shard_map/dot_general | solution.py:46
  226.8 13.1 %convolution_convert_fusion.1 = bf16[2048,1024]{1,0:T(8,128)(2,1)S(1)} fusion(bf16[2048,2048]{1,0:T(8,128)(2,1)} %get-tuple-element.81, bf16[2048,1024]{1,0:T(8,128)(2,1)S(1)} %multiply_convert_fusion.first_ref), kind=kOutput, calls=%fused_computation.10 | convolution fusion | flops 8592031744 | bytes 16777216 | tf_op jit(solution)/shard_map/dot_general | solution.py:716
  246.9 7.1 %pad_maximum_fusion = bf16[4,512,2048]{2,1,0:T(8,128)(2,1)} fusion(bf16[4,256,2048]{2,1,0:T(8,128)(2,1)} %bitcast.133, bf16[4,256,1024]{2,1,0:T(8,128)(2,1)} %collective-permute-done.14, bf16[4,256,1024]{2,1,0:T(8,128)(2,1)} %get-tuple-element.142), kind=kLoop, calls=%fused_computation | loop fusion | flops 25165824 | bytes 16777216 | tf_op jit(solution)/shard_map/concatenate | solution.py:789
  262.9 9.2 %broadcast_add_fusion.mixed_ref = f32[2048,768]{1,0:T(8,128)S(1)} fusion(f32[768]{0:T(1024)S(1)} %fusion.27, bf16[2048,2048]{1,0:T(8,128)(2,1)} %get-tuple-element.81, bf16[2048,768]{1,0:T(8,128)(2,1)S(1)} %constant_dynamic-slice_fusion.second_right_ref), kind=kOutput, calls=%fused_computation.11 | convolution fusion | flops 6444023808 | bytes 17828864 | tf_op jit(solution)/shard_map/dot_general | solution.py:50
  272.1 15.3 %attend.1 = (bf16[2048,768]{1,0:T(8,128)(2,1)S(1)}, bf16[2048,256]{1,0:T(8,128)(2,1)S(1)}, f32[2,2,2,1024]{3,2,1,0:T(2,128)S(1)}) custom-call(f32[2048,768]{1,0:T(8,128)S(1)} %broadcast_add_fusion.mixed_ref, f32[1024,128]{1,0:T(8,128)S(1)} %copy-done.13, f32[1024,128]{1,0:T(8,128)S(1)} %copy-done.11, f32[1024,128]{1,0:T(8,128)S(1)} %copy-done.9), custom_call_target="tpu_custom_call" | custom-call | flops 2147483648 | bytes 12582912 | tf_op jit(solution)/shard_map/attend/pallas_call | solution.py:150
  296.3 7.8 %add_convert_fusion = bf16[1024,2048]{1,0:T(8,128)(2,1)} fusion(bf16[1024,2048]{1,0:T(8,128)(2,1)S(1)} %fusion.23, bf16[1024,2048]{1,0:T(8,128)(2,1)S(1)} %bitcast.128, bf16[2048,1024]{1,0:T(8,128)(2,1)} %copy-done.42), kind=kOutput, calls=%fused_computation.2 | convolution fusion | flops 4301258752 | bytes 14680064 | tf_op jit(solution)/shard_map/dot_general | solution.py:50
  321.6 20.4 %attend_back.1.second_ref = bf16[2048,768]{1,0:T(8,128)(2,1)S(1)} custom-call(bf16[2048,768]{1,0:T(8,128)(2,1)S(1)} %copy-done.17, bf16[2048,256]{1,0:T(8,128)(2,1)S(1)} %copy-done.18, f32[2,2,2,1024]{3,2,1,0:T(2,128)S(1)} %get-tuple-element.94.logsum_ref, f32[1024,128]{1,0:T(8,128)S(1)} %copy-done.14, f32[1024,128]{1,0:T(8,128)S(1)} %copy-done.12, ...), custom_call_target="tpu_custom_call" | custom-call | flops 5368709120 | bytes 9437184 | tf_op jit(solution)/shard_map/attend_back/pallas_call | solution.py:180
  351.7 22.1 %two_products.1 = (bf16[1024,2048]{1,0:T(8,128)(2,1)}, bf16[1024,2048]{1,0:T(8,128)(2,1)}) custom-call(bf16[2048,1024]{1,0:T(8,128)(2,1)} %copy-done.23, bf16[2048,1024]{1,0:T(8,128)(2,1)} %constant_dynamic-slice_fusion.2.first_right_ref, bf16[2048,768]{1,0:T(8,128)(2,1)S(1)} %attend_back.1.second_ref, bf16[2048,768]{1,0:T(8,128)(2,1)} %copy-done.26), custom_call_target="tpu_custom_call" | custom-call | flops 15032385536 | bytes 23068672 | tf_op jit(solution)/shard_map/two_products/pallas_call | solution.py:518
  381.6 7.2 %add_convert_fusion.3 = (bf16[256,2048]{1,0:T(8,128)(2,1)}, bf16[256,2048]{1,0:T(8,128)(2,1)S(1)}, bf16[256,2048]{1,0:T(8,128)(2,1)}, f32[256,2048]{1,0:T(8,128)}) fusion(bf16[1024,2048]{1,0:T(8,128)(2,1)} %collective-permute-done.19, s32[]{:T(128)S(6)} %select_n.188, bf16[1024,2048]{1,0:T(8,128)(2,1)} %get-tuple-element.100, s32[]{:T(128)S(6)} %select_n.187, ...), kind=kLoop, calls=%fused_computation.37 | loop fusion | flops 7864320 | bytes 13631504 | tf_op jit(solution)/shard_map/convert_element_type | solution.py:740
  403.8 11.2 %collective-permute-done.21 = bf16[256,2048]{1,0:T(8,128)(2,1)} collective-permute-done((bf16[256,2048]{1,0:T(8,128)(2,1)}, bf16[256,2048]{1,0:T(8,128)(2,1)}, u32[]{:S(2)}, u32[]{:S(2)}) %collective-permute-start.21) | collective-permute-done | bytes 1048608 | tf_op jit(solution)/shard_map/ppermute | solution.py:602
  420.0 22.9 %collective-permute-done.23 = bf16[256,2048]{1,0:T(8,128)(2,1)S(1)} collective-permute-done((bf16[256,2048]{1,0:T(8,128)(2,1)S(1)}, bf16[256,2048]{1,0:T(8,128)(2,1)S(1)}, u32[]{:S(2)}, u32[]{:S(2)}) %collective-permute-start.23) | collective-permute-done | bytes 1048608 | tf_op jit(solution)/shard_map/ppermute | solution.py:602
  447.4 19.4 %collective-permute-done.24.refs_1_ = bf16[512,2048]{1,0:T(8,128)(2,1)} collective-permute-done((bf16[512,2048]{1,0:T(8,128)(2,1)}, bf16[512,2048]{1,0:T(8,128)(2,1)}, u32[]{:S(2)}, u32[]{:S(2)}) %collective-permute-start.24) | collective-permute-done | bytes 2097184 | tf_op jit(solution)/shard_map/ppermute | solution.py:602
  466.8 9.4 %collective-permute-done.25.refs_2_ = bf16[512,2048]{1,0:T(8,128)(2,1)} collective-permute-done((bf16[512,2048]{1,0:T(8,128)(2,1)}, bf16[512,2048]{1,0:T(8,128)(2,1)}, u32[]{:S(2)}, u32[]{:S(2)}) %collective-permute-start.25) | collective-permute-done | bytes 2097184 | tf_op jit(solution)/shard_map/ppermute | solution.py:602
  477.2 12.6 %reduce-scatter.5.cloned.1.call-done.refs_0_ = bf16[256,2048]{1,0:T(8,128)(2,1)} async-done(((bf16[1024,2048]{1,0:T(8,128)(2,1)}), bf16[256,2048]{1,0:T(8,128)(2,1)}) %reduce-scatter.5.cloned.1.call-update) | async-done | bytes 1048592 | tf_op jit(solution)/shard_map/reduce_scatter | solution.py:768
  493.6 18.9 %collective-permute-done.28.refs_3_ = bf16[512,2048]{1,0:T(8,128)(2,1)S(1)} collective-permute-done((bf16[512,2048]{1,0:T(8,128)(2,1)}, bf16[512,2048]{1,0:T(8,128)(2,1)S(1)}, u32[]{:S(2)}, u32[]{:S(2)}) %collective-permute-start.28) | collective-permute-done | bytes 2097184 | tf_op jit(solution)/shard_map/ppermute | solution.py:602
  526.1 8.5 %all_to_all.18 = f32[8,1,2560]{2,1,0:T(1,128)S(1)} all-to-all(f32[8,1,2560]{2,1,0:T(1,128)S(1)} %all_to_all.14), channel_id=1, replica_groups=mesh['seq'=4,'fsdp'=8] {'fsdp'}, dimensions={0} | all-to-all | bytes 163840 | tf_op jit(solution)/shard_map/all_to_all | solution.py:883
  (279 shorter events, 183.4 us)
Async XLA Ops:
  7.2 163.3 %all-gather.3.cloned.1.call-start = ((), (), s32[]{:S(2)}) async-start(), calls=%async_computation.4 | async-start | bytes 18874368 | tf_op jit(solution)/shard_map/all_gather | solution.py:683
  15.6 26.5 %collective-permute-start = (bf16[256,2048]{1,0:T(8,128)(2,1)S(1)}, bf16[256,2048]{1,0:T(8,128)(2,1)}, u32[]{:S(2)}, u32[]{:S(2)}) collective-permute-start(bf16[256,2048]{1,0:T(8,128)(2,1)S(1)} %bitcast.105), channel_id=1, source_target_pairs={{0,8},{1,17},{2,10},{3,19},{4,12},{5,21},{6,14},{7,23},{8,0},{9,25... | collective-permute-start | bytes 3145736 | tf_op jit(solution)/shard_map/ppermute | solution.py:602
  18.6 23.5 %collective-permute-start.1 = (bf16[256,2048]{1,0:T(8,128)(2,1)S(1)}, bf16[256,2048]{1,0:T(8,128)(2,1)}, u32[]{:S(2)}, u32[]{:S(2)}) collective-permute-start(bf16[256,2048]{1,0:T(8,128)(2,1)S(1)} %bitcast.106), channel_id=1, source_target_pairs={{0,16},{1,9},{2,18},{3,11},{4,20},{5,13},{6,22},{7,15},{8,24},{9,1... | collective-permute-start | bytes 3145736 | tf_op jit(solution)/shard_map/ppermute | solution.py:602
  23.5 24.4 %all-to-all-start = ((bf16[8,2,1408]{2,1,0:T(2,128)(2,1)}), bf16[8,2,1408]{2,1,0:T(2,128)(2,1)S(1)}, u32[]{:S(2)}, u32[]{:S(2)}) async-start(bf16[8,2,1408]{2,1,0:T(2,128)(2,1)} %reshape.256), calls=%async_computation | async-start | bytes 90112 | tf_op jit(solution)/shard_map/all_to_all | solution.py:649
  28.4 225.9 %all-gather.5.cloned.1.call-start = ((), (), s32[]{:S(2)}) async-start(), calls=%async_computation.5 | async-start | bytes 9437184 | tf_op jit(solution)/shard_map/all_gather | solution.py:705
  57.3 25.3 %collective-permute-start.7 = (bf16[256,2048]{1,0:T(8,128)(2,1)S(1)}, bf16[256,2048]{1,0:T(8,128)(2,1)}, u32[]{:S(2)}, u32[]{:S(2)}) collective-permute-start(bf16[256,2048]{1,0:T(8,128)(2,1)S(1)} %bitcast.109), channel_id=1, source_target_pairs={{0,8},{1,17},{2,10},{3,19},{4,12},{5,21},{6,14},{7,23},{8,0},{9,25... | collective-permute-start | bytes 3145736 | tf_op jit(solution)/shard_map/ppermute | solution.py:602
  59.8 22.8 %collective-permute-start.8 = (bf16[256,2048]{1,0:T(8,128)(2,1)S(1)}, bf16[256,2048]{1,0:T(8,128)(2,1)}, u32[]{:S(2)}, u32[]{:S(2)}) collective-permute-start(bf16[256,2048]{1,0:T(8,128)(2,1)S(1)} %bitcast.110), channel_id=1, source_target_pairs={{0,16},{1,9},{2,18},{3,11},{4,20},{5,13},{6,22},{7,15},{8,24},{9,1... | collective-permute-start | bytes 3145736 | tf_op jit(solution)/shard_map/ppermute | solution.py:602
  60.5 24.0 %collective-permute-start.3 = (bf16[256,2048]{1,0:T(8,128)(2,1)S(1)}, bf16[256,2048]{1,0:T(8,128)(2,1)S(1)}, u32[]{:S(2)}, u32[]{:S(2)}) collective-permute-start(bf16[256,2048]{1,0:T(8,128)(2,1)S(1)} %bitcast.107), channel_id=1, source_target_pairs={{0,1},{1,0},{2,3},{3,2},{4,5},{5,4},{6,7},{7,6},{8,9},{9,8},{10,11... | collective-permute-start | bytes 3145736 | tf_op jit(solution)/shard_map/ppermute | solution.py:590
  60.5 25.2 %collective-permute-start.4 = (bf16[256,2048]{1,0:T(8,128)(2,1)}, bf16[256,2048]{1,0:T(8,128)(2,1)}, u32[]{:S(2)}, u32[]{:S(2)}) collective-permute-start(bf16[256,2048]{1,0:T(8,128)(2,1)} %collective-permute-done.refs_1_), channel_id=1, source_target_pairs={{0,1},{1,0},{2,3},{3,2},{4,5},{5,4},{6,7},{7,6},{8,9},{9,8},{10,11... | collective-permute-start | bytes 3145736 | tf_op jit(solution)/shard_map/ppermute | solution.py:590
  61.1 24.7 %collective-permute-start.5 = (bf16[256,2048]{1,0:T(8,128)(2,1)}, bf16[256,2048]{1,0:T(8,128)(2,1)}, u32[]{:S(2)}, u32[]{:S(2)}) collective-permute-start(bf16[256,2048]{1,0:T(8,128)(2,1)} %collective-permute-done.1.refs_2_), channel_id=1, source_target_pairs={{0,1},{1,0},{2,3},{3,2},{4,5},{5,4},{6,7},{7,6},{8,9},{9,8},{10,11... | collective-permute-start | bytes 3145736 | tf_op jit(solution)/shard_map/ppermute | solution.py:590
  82.6 18.2 %collective-permute-start.9 = (bf16[256,2048]{1,0:T(8,128)(2,1)}, bf16[256,2048]{1,0:T(8,128)(2,1)}, u32[]{:S(2)}, u32[]{:S(2)}) collective-permute-start(bf16[256,2048]{1,0:T(8,128)(2,1)} %collective-permute-done.7.refs_1_), channel_id=1, source_target_pairs={{0,16},{1,9},{2,18},{3,11},{4,20},{5,13},{6,22},{7,15},{8,24},{9,1... | collective-permute-start | bytes 3145736 | tf_op jit(solution)/shard_map/ppermute | solution.py:602
  85.5 18.4 %collective-permute-start.10 = (bf16[256,2048]{1,0:T(8,128)(2,1)S(1)}, bf16[256,2048]{1,0:T(8,128)(2,1)}, u32[]{:S(2)}, u32[]{:S(2)}) collective-permute-start(bf16[256,2048]{1,0:T(8,128)(2,1)S(1)} %bitcast.111), channel_id=1, source_target_pairs={{0,1},{1,0},{2,3},{3,2},{4,5},{5,4},{6,7},{7,6},{8,9},{9,8},{10,11... | collective-permute-start | bytes 3145736 | tf_op jit(solution)/shard_map/ppermute | solution.py:590
  103.6 311.5 %reduce-scatter.3.cloned.1.call-start = ((), (), s32[]{:S(2)}) async-start(), calls=%async_computation.6 | async-start | bytes 10485760 | tf_op jit(solution)/shard_map/reduce_scatter | solution.py:768
  254.0 235.8 %reduce-scatter.5.cloned.1.call-start = ((), (), s32[]{:S(2)}) async-start(), calls=%async_computation.7 | async-start | bytes 5242880 | tf_op jit(solution)/shard_map/reduce_scatter | solution.py:768
  319.5 30.8 %collective-permute-start.17 = (bf16[256,2048]{1,0:T(8,128)(2,1)S(1)}, bf16[256,2048]{1,0:T(8,128)(2,1)S(1)}, u32[]{:S(2)}, u32[]{:S(2)}) collective-permute-start(bf16[256,2048]{1,0:T(8,128)(2,1)S(1)} %get-tuple-element.139), channel_id=1, source_target_pairs={{0,8},{1,17},{2,10},{3,19},{4,12},{5,21},{6,14},{7,23},{8,0},{9,25... | collective-permute-start | bytes 3145736 | tf_op jit(solution)/shard_map/ppermute | solution.py:602
  320.7 29.6 %collective-permute-start.16 = (bf16[256,2048]{1,0:T(8,128)(2,1)S(1)}, bf16[256,2048]{1,0:T(8,128)(2,1)S(1)}, u32[]{:S(2)}, u32[]{:S(2)}) collective-permute-start(bf16[256,2048]{1,0:T(8,128)(2,1)S(1)} %get-tuple-element.140), channel_id=1, source_target_pairs={{0,8},{1,17},{2,10},{3,19},{4,12},{5,21},{6,14},{7,23},{8,0},{9,25... | collective-permute-start | bytes 3145736 | tf_op jit(solution)/shard_map/ppermute | solution.py:602
  389.7 25.3 %collective-permute-start.21 = (bf16[256,2048]{1,0:T(8,128)(2,1)}, bf16[256,2048]{1,0:T(8,128)(2,1)}, u32[]{:S(2)}, u32[]{:S(2)}) collective-permute-start(bf16[256,2048]{1,0:T(8,128)(2,1)} %get-tuple-element.136), channel_id=1, source_target_pairs={{0,8},{1,17},{2,10},{3,19},{4,12},{5,21},{6,14},{7,23},{8,0},{9,25... | collective-permute-start | bytes 3145736 | tf_op jit(solution)/shard_map/ppermute | solution.py:602
  416.9 26.0 %collective-permute-start.23 = (bf16[256,2048]{1,0:T(8,128)(2,1)S(1)}, bf16[256,2048]{1,0:T(8,128)(2,1)S(1)}, u32[]{:S(2)}, u32[]{:S(2)}) collective-permute-start(bf16[256,2048]{1,0:T(8,128)(2,1)S(1)} %add_convert_fusion.2), channel_id=1, source_target_pairs={{0,16},{1,9},{2,18},{3,11},{4,20},{5,13},{6,22},{7,15},{8,24},{9,1... | collective-permute-start | bytes 3145736 | tf_op jit(solution)/shard_map/ppermute | solution.py:602
  417.9 48.9 %collective-permute-start.24 = (bf16[512,2048]{1,0:T(8,128)(2,1)}, bf16[512,2048]{1,0:T(8,128)(2,1)}, u32[]{:S(2)}, u32[]{:S(2)}) collective-permute-start(bf16[512,2048]{1,0:T(8,128)(2,1)} %reduce-scatter.3.cloned.1.call-done.refs_0_), channel_id=1, source_target_pairs={{0,8},{1,17},{2,10},{3,19},{4,12},{5,21},{6,14},{7,23},{8,0},{9,25... | collective-permute-start | bytes 6291464 | tf_op jit(solution)/shard_map/ppermute | solution.py:602
  419.0 57.2 %collective-permute-start.25 = (bf16[512,2048]{1,0:T(8,128)(2,1)}, bf16[512,2048]{1,0:T(8,128)(2,1)}, u32[]{:S(2)}, u32[]{:S(2)}) collective-permute-start(bf16[512,2048]{1,0:T(8,128)(2,1)} %reduce-scatter.3.cloned.1.call-done.refs_0_), channel_id=1, source_target_pairs={{0,16},{1,9},{2,18},{3,11},{4,20},{5,13},{6,22},{7,15},{8,24},{9,1... | collective-permute-start | bytes 6291464 | tf_op jit(solution)/shard_map/ppermute | solution.py:602
  476.3 36.2 %collective-permute-start.28 = (bf16[512,2048]{1,0:T(8,128)(2,1)}, bf16[512,2048]{1,0:T(8,128)(2,1)S(1)}, u32[]{:S(2)}, u32[]{:S(2)}) collective-permute-start(bf16[512,2048]{1,0:T(8,128)(2,1)} %collective-permute-done.24.refs_1_), channel_id=1, source_target_pairs={{0,16},{1,9},{2,18},{3,11},{4,20},{5,13},{6,22},{7,15},{8,24},{9,1... | collective-permute-start | bytes 6291464 | tf_op jit(solution)/shard_map/ppermute | solution.py:602
  489.8 30.6 %collective-permute-start.26 = (bf16[256,2048]{1,0:T(8,128)(2,1)}, bf16[256,2048]{1,0:T(8,128)(2,1)}, u32[]{:S(2)}, u32[]{:S(2)}) collective-permute-start(bf16[256,2048]{1,0:T(8,128)(2,1)} %reduce-scatter.5.cloned.1.call-done.refs_0_), channel_id=1, source_target_pairs={{0,8},{1,17},{2,10},{3,19},{4,12},{5,21},{6,14},{7,23},{8,0},{9,25... | collective-permute-start | bytes 3145736 | tf_op jit(solution)/shard_map/ppermute | solution.py:602
  491.3 33.8 %collective-permute-start.27 = (bf16[256,2048]{1,0:T(8,128)(2,1)}, bf16[256,2048]{1,0:T(8,128)(2,1)}, u32[]{:S(2)}, u32[]{:S(2)}) collective-permute-start(bf16[256,2048]{1,0:T(8,128)(2,1)} %reduce-scatter.5.cloned.1.call-done.refs_0_), channel_id=1, source_target_pairs={{0,16},{1,9},{2,18},{3,11},{4,20},{5,13},{6,22},{7,15},{8,24},{9,1... | collective-permute-start | bytes 3145736 | tf_op jit(solution)/shard_map/ppermute | solution.py:602
  525.1 22.6 %collective-permute-start.29 = (bf16[256,2048]{1,0:T(8,128)(2,1)}, bf16[256,2048]{1,0:T(8,128)(2,1)}, u32[]{:S(2)}, u32[]{:S(2)}) collective-permute-start(bf16[256,2048]{1,0:T(8,128)(2,1)} %collective-permute-done.26.refs_1_), channel_id=1, source_target_pairs={{0,16},{1,9},{2,18},{3,11},{4,20},{5,13},{6,22},{7,15},{8,24},{9,1... | collective-permute-start | bytes 3145736 | tf_op jit(solution)/shard_map/ppermute | solution.py:602
  (61 other events, 773.7 us)
Sparse Core Ops, SparseCore 0:
  15.7 154.7 all-gather.2
  172.7 79.3 all-gather.4
  255.0 142.9 reduce-scatter.2
  415.2 74.5 reduce-scatter.4
